TPU v7x, 256 devices: a whole 4x4x8 slice. The times are simulated.
256 devices in a mesh: tm: 16 (over y_lo, x, core), chan: 16 (over z, y_hi).
Axes of the slice: x: 4, y: 4 (y_hi: 2, y_lo: 2; y = y_hi * 2 + y_lo), z: 8, core: 2. Of those that a mesh axis runs over, the one named last changes fastest.
Arguments:
- visibility: float32 [2, 2048, 128, 512], P(None, None, 'tm', 'chan'), may hold values from -8 to 8
- groups: int32 [2048], replicated, may hold values from 0 to 63
- flags: int32 [2048, 512], P(None, 'chan'), may hold values 0 or 1
- fringe: bfloat16 [2, 64, 128, 128], P(None, 'tm'), may hold values from -0.375 to 0.375
- delay: bfloat16 [8, 512, 512], P(None, 'chan'), may hold values from -0.25 to 0.25
Outputs:
- filtered: float32 [2, 2048, 128, 512], P(None, ('tm', 'chan'))
All inputs are finite; a program needn't handle non-finite values. No bound on the sum of `flags` on one device may be relied on, other than what follows from the above.
Results may differ from a plain program's by a relative error of at most 0.0003.
Values may be sent and summed in bfloat16 or wider, within the bound.
No kernel may reach another device: no remote copies, remote signals or barrier semaphores. Data moves between devices by JAX's collectives and lax.ppermute only.
A program may use at most 128 MiB of HBM per device.

v0:
```python
import functools

import jax
import jax.numpy as jnp
from jax import lax
from jax.experimental import pallas as pl
from jax.experimental.pallas import tpu as pltpu
from jax.sharding import PartitionSpec as P

LANES = 128
SUB = 8
FULL = 32760.0
MIDDLE = 32768.0
VMEM = 40 * 1024 * 1024


def pack_kernel(vis_ref, flag_ref, out_ref, rows):
    for tile in range(vis_ref.shape[3] // LANES):
        lanes = pl.ds(tile * LANES, LANES)
        keep = flag_ref[:, lanes].astype(jnp.float32)
        masked = vis_ref[:, :, :, lanes] * keep[None, None]
        loudest = jnp.max(jnp.abs(masked), axis=(0, 1, 2), keepdims=True)
        level = jnp.ceil(jnp.log2(jnp.maximum(loudest, 1e-30)) * 4.0)
        factor = FULL / jnp.exp2(level * 0.25)
        coded = (masked * factor + (MIDDLE + 0.5)).astype(jnp.int32)
        words = coded[0] | (coded[1] << 16)
        level_row = level.reshape(1, LANES).astype(jnp.int32)
        times, chans = words.shape[0], words.shape[1]
        fold = LANES // chans
        for part in range(times // fold):
            turned = words[part * fold : (part + 1) * fold].reshape(LANES, LANES).T
            for owner in range(LANES // SUB):
                place = (tile * (LANES // SUB) + owner) * rows + part * SUB
                out_ref[place : place + SUB, :] = turned[owner * SUB : (owner + 1) * SUB]
        for owner in range(LANES // SUB):
            place = (tile * (LANES // SUB) + owner) * rows + rows - 1
            out_ref[place : place + 1, :] = level_row


def select_kernel(groups_ref, place_ref, table_ref, out_ref):
    owners, each = out_ref.shape[0], out_ref.shape[1]
    chan_count = groups_ref.shape[0] // (owners * each)

    def step(n, carry):
        owner = n // each
        slot = n % each
        group = groups_ref[(owner * chan_count + place_ref[1]) * each + slot]
        out_ref[owner, slot] = table_ref[group]
        return carry

    lax.fori_loop(0, owners * each, step, 0, unroll=8)


def filter_kernel(
    groups_ref, place_ref, words_ref, fringe_ref, delay_ref, out_ref, levels, samples, *, rows
):
    baseline = pl.program_id(0)
    blocks = words_ref.shape[0]
    chan_count = words_ref.shape[1] // rows
    quads = chan_count // 4
    times = rows - 1

    @pl.when(baseline == 0)
    def unpack():
        lane = lax.broadcasted_iota(jnp.int32, (SUB, LANES), 1)
        low_half = lane < 64
        even_group = (lane & 32) == 0
        group = lane // 32
        level_rows = [
            words_ref[block, source * rows + rows - 1 : source * rows + rows, :]
            for block in range(blocks)
            for source in range(chan_count)
        ]
        level_all = jnp.concatenate(level_rows, axis=0).astype(jnp.float32)
        scale_all = jnp.exp2(level_all * 0.25) * (1.0 / FULL)
        levels[...] = scale_all.T
        own = levels[pl.ds(pl.multiple_of(place_ref[1] * SUB, SUB), SUB), :]
        for block in range(blocks):
            for quad in range(quads):
                first = block * chan_count + quad * 4
                scale = jnp.broadcast_to(own[:, first : first + 1], (SUB, LANES))
                for member in range(1, 4):
                    other = jnp.broadcast_to(own[:, first + member : first + member + 1], (SUB, LANES))
                    scale = jnp.where(group == member, other, scale)
                offset = scale * -MIDDLE
                for half in range(times // SUB):
                    v = [
                        words_ref[block, pl.ds((quad * 4 + member) * rows + half * SUB, SUB), :]
                        for member in range(4)
                    ]
                    r = [pltpu.roll(x, 64, 1) for x in v]
                    a0 = jnp.where(low_half, v[0], r[2])
                    a2 = jnp.where(low_half, r[0], v[2])
                    a1 = jnp.where(low_half, v[1], r[3])
                    a3 = jnp.where(low_half, r[1], v[3])
                    turned = (
                        jnp.where(even_group, a0, pltpu.roll(a1, 32, 1)),
                        jnp.where(even_group, pltpu.roll(a0, 96, 1), a1),
                        jnp.where(even_group, a2, pltpu.roll(a3, 32, 1)),
                        jnp.where(even_group, pltpu.roll(a2, 96, 1), a3),
                    )
                    for step, word in enumerate(turned):
                        at = (block * 8 + half * 4 + step) * SUB
                        real = (word & 0xFFFF).astype(jnp.float32) * scale + offset
                        imag = lax.shift_right_logical(word, 16).astype(jnp.float32) * scale + offset
                        samples[0, quad, at : at + SUB, :] = real
                        samples[1, quad, at : at + SUB, :] = imag

    count = samples.shape[2] // SUB
    parts = []
    for part in range(2):
        parts.append(
            jnp.concatenate(
                [samples[part, quad, pl.ds(baseline, count, stride=SUB), :] for quad in range(quads)], axis=1
            )
        )
    data = jnp.concatenate(parts, axis=0)
    high = data.astype(jnp.bfloat16)
    low = (data - high.astype(jnp.float32)).astype(jnp.bfloat16)
    mats = fringe_ref[...].reshape(2 * count, count)
    real, imag = mats[:count], mats[count:]
    both = jnp.concatenate(
        [jnp.concatenate([real, -imag], axis=1), jnp.concatenate([imag, real], axis=1)], axis=0
    )
    rated = jnp.dot(both, high, preferred_element_type=jnp.float32) + jnp.dot(
        both, low, preferred_element_type=jnp.float32
    )
    high = rated.astype(jnp.bfloat16)
    low = (rated - high.astype(jnp.float32)).astype(jnp.bfloat16)
    total = None
    wide = delay_ref.shape[3]
    for piece in range(delay_ref.shape[1]):
        for values in (high, low):
            term = lax.dot_general(
                values[:, piece * wide : (piece + 1) * wide],
                delay_ref[0, piece],
                (((1,), (1,)), ((), ())),
                preferred_element_type=jnp.float32,
            )
            total = term if total is None else total + term
    out_ref[...] = total.reshape(out_ref.shape)


def shards(visibility, groups, flags, fringe, delay):
    time_count = lax.axis_size("tm")
    chan_count = lax.axis_size("chan")
    everyone = ("tm", "chan")
    devices = time_count * chan_count
    total = groups.shape[0]
    own = total // devices
    times, chans = visibility.shape[2], visibility.shape[3]
    all_times, all_chans = times * time_count, chans * chan_count
    time_place = lax.axis_index("tm")
    chan_place = lax.axis_index("chan")
    place = jnp.stack([time_place, chan_place]).astype(jnp.int32)
    params = functools.partial(pltpu.CompilerParams, vmem_limit_bytes=VMEM)

    delay_groups = delay.shape[0]
    pieces = time_count // delay_groups
    wide = all_chans // pieces
    share = lax.dynamic_slice(
        delay, (time_place // pieces, 0, (time_place % pieces) * wide), (1, chans, wide)
    )
    share = lax.all_to_all(
        jnp.broadcast_to(share, (chan_count, chans, wide)), "chan", split_axis=0, concat_axis=0, tiled=True
    )
    delay_all = lax.all_gather(share.reshape(all_chans, wide), "tm", axis=0, tiled=True)
    delay_all = delay_all.reshape(delay_groups, pieces, all_chans, wide)

    rows = times * chans * SUB // LANES // SUB * own + 1
    step_lanes = 2 * LANES
    packed = pl.pallas_call(
        functools.partial(pack_kernel, rows=rows),
        grid=(total // step_lanes,),
        in_specs=[
            pl.BlockSpec((2, times, chans, step_lanes), lambda n: (0, 0, 0, n)),
            pl.BlockSpec((chans, step_lanes), lambda n: (0, n)),
        ],
        out_specs=pl.BlockSpec((step_lanes // SUB * rows, LANES), lambda n: (n, 0)),
        out_shape=jax.ShapeDtypeStruct((devices * rows, LANES), jnp.int32),
        compiler_params=params(),
        name="pack",
    )(jnp.transpose(visibility, (0, 2, 3, 1)), flags.T)
    words = lax.all_to_all(
        packed.reshape(devices, 1, rows * LANES), everyone, split_axis=0, concat_axis=0, tiled=True
    )
    words = words.reshape(time_count, chan_count * rows, LANES)

    held = fringe.shape[1]
    slab = 2 * all_times // time_count
    slabs = fringe.reshape(2, held, all_times // slab, slab, all_times)
    slabs = jnp.transpose(slabs, (0, 2, 1, 3, 4)).reshape(time_count, held, slab, all_times)
    table = lax.all_to_all(slabs, "tm", split_axis=0, concat_axis=0, tiled=True)
    table = table.reshape(time_count * held, slab, all_times)
    chosen = pl.pallas_call(
        select_kernel,
        grid_spec=pltpu.PrefetchScalarGridSpec(
            num_scalar_prefetch=2,
            grid=(),
            in_specs=[pl.BlockSpec(memory_space=pltpu.VMEM)],
            out_specs=pl.BlockSpec(memory_space=pltpu.VMEM),
        ),
        out_shape=jax.ShapeDtypeStruct((time_count, own, slab, all_times), jnp.bfloat16),
        compiler_params=params(),
        name="select",
    )(groups, place, table)
    mats = lax.all_to_all(chosen, "tm", split_axis=0, concat_axis=0, tiled=True)

    spread = time_count * held // delay_groups

    def delay_index(n, groups_ref, place_ref):
        mine = (place_ref[0] * chan_count + place_ref[1]) * own + n
        return (groups_ref[mine] // spread, 0, 0, 0)

    return pl.pallas_call(
        functools.partial(filter_kernel, rows=rows),
        grid_spec=pltpu.PrefetchScalarGridSpec(
            num_scalar_prefetch=2,
            grid=(own,),
            in_specs=[
                pl.BlockSpec((time_count, chan_count * rows, LANES), lambda n, *_: (0, 0, 0)),
                pl.BlockSpec((time_count, 1, slab, all_times), lambda n, *_: (0, n, 0, 0)),
                pl.BlockSpec((1, pieces, all_chans, wide), delay_index),
            ],
            out_specs=pl.BlockSpec((2, 1, all_times, all_chans), lambda n, *_: (0, n, 0, 0)),
            scratch_shapes=[
                pltpu.VMEM((LANES, devices), jnp.float32),
                pltpu.VMEM((2, all_chans // LANES, all_times * SUB, LANES), jnp.float32),
            ],
        ),
        out_shape=jax.ShapeDtypeStruct((2, own, all_times, all_chans), jnp.float32),
        compiler_params=params(),
        name="filter",
    )(groups, place, words, mats, delay_all)


def solution(mesh):
    placed = (
        P(None, None, "tm", "chan"),
        P(),
        P(None, "chan"),
        P(None, "tm", None, None),
        P(None, "chan", None),
    )
    return jax.shard_map(
        shards,
        mesh=mesh,
        in_specs=placed,
        out_specs=P(None, ("tm", "chan"), None, None),
        check_vma=False,
    )
```

profile of v0, /device:TPU:33, one launch (start us, length us, event | category | flops | bytes accessed | tf_op | source)
XLA Modules:
  0.0 158.1 jit_solution(17203985687717220359)
XLA Ops:
  6.5 0.0 copy-start
  6.5 0.0 copy-start.4
  6.5 0.0 all-gather.2.cloned.1.call-start
  6.5 0.9 copy-done
  7.5 21.1 %all_to_all.20 = bf16[16,32,256]{2,1,0:T(8,128)(2,1)} all-to-all(bf16[16,32,256]{2,1,0:T(8,128)(2,1)S(1)} %broadcast_in_dim.8), channel_id=1, replica_groups=mesh['tm'=16,'chan'=16] {'chan'}, dimensions={0} | all-to-all | bytes 524288 | tf_op jit(solution)/shard_map/all_to_all | solution.py:164
  28.6 0.0 all-gather.2.cloned.1.call-update
  28.6 1.7 %copy.8 = bf16[2,8,4,16,128]{4,3,2,1,0:T(8,128)(2,1)} copy(bf16[2,8,4,16,128]{4,3,1,2,0:T(8,128)(2,1)} %bitcast.22) | data formatting | bytes 524288 | tf_op jit(solution)/shard_map/transpose | solution.py:192
  30.3 7.3 %all-to-all-start.1 = ((bf16[16,4,16,128]{3,2,1,0:T(8,128)(2,1)}), bf16[16,4,16,128]{3,2,1,0:T(8,128)(2,1)S(1)}, u32[]{:S(2)}, u32[]{:S(2)}) async-start(bf16[16,4,16,128]{3,2,1,0:T(8,128)(2,1)} %bitcast.8), calls=%async_computation.1 | async-start | bytes 524288 | tf_op jit(solution)/shard_map/all_to_all | solution.py:193
  37.6 0.1 pad_add_fusion.place_ref
  37.6 9.1 %all-to-all-done.1 = bf16[16,4,16,128]{3,2,1,0:T(8,128)(2,1)S(1)} async-done(((bf16[16,4,16,128]{3,2,1,0:T(8,128)(2,1)}), bf16[16,4,16,128]{3,2,1,0:T(8,128)(2,1)S(1)}, u32[]{:S(2)}, u32[]{:S(2)}) %all-to-all-start.1) | async-done | bytes 262176 | tf_op jit(solution)/shard_map/all_to_all | solution.py:193
  46.7 0.0 copy-start.5
  46.7 0.7 copy-done.5
  47.4 2.6 %select.7 = bf16[16,8,16,128]{3,2,1,0:T(8,128)(2,1)} custom-call(s32[2048]{0:T(1024)S(1)} %copy-done.5, s32[2]{0:T(128)S(1)} %pad_add_fusion.place_ref, bf16[64,16,128]{2,1,0:T(8,128)(2,1)S(1)} %bitcast.19), custom_call_target="tpu_custom_call" | custom-call | tf_op jit(solution)/shard_map/select/pallas_call | solution.py:195
  50.0 4.5 %all-to-all-start.2 = ((bf16[16,8,16,128]{3,2,1,0:T(8,128)(2,1)}), bf16[16,8,16,128]{3,2,1,0:T(8,128)(2,1)S(1)}, u32[]{:S(2)}, u32[]{:S(2)}) async-start(bf16[16,8,16,128]{3,2,1,0:T(8,128)(2,1)} %select.7), calls=%async_computation.2 | async-start | bytes 1048576 | tf_op jit(solution)/shard_map/all_to_all | solution.py:207
  54.5 0.0 copy-done.4
  54.5 0.0 copy-start.3
  54.5 2.3 %copy-done.3 = f32[2,2048,8,32]{1,3,2,0:T(8,128)S(1)} copy-done((f32[2,2048,8,32]{1,3,2,0:T(8,128)S(1)}, f32[2,2048,8,32]{1,3,2,0:T(8,128)}, u32[]{:S(2)}) %copy-start.3) | copy-done | bytes 4194328
  56.8 0.0 copy-start.6
  56.8 2.2 %pack.1 = s32[4352,128]{1,0:T(8,128)S(1)} custom-call(f32[2,8,32,2048]{3,2,1,0:T(8,128)S(1)} %bitcast.18, s32[32,2048]{1,0:T(8,128)S(1)} %bitcast.20), custom_call_target="tpu_custom_call" | custom-call | tf_op jit(solution)/shard_map/pack/pallas_call | solution.py:172
  59.0 0.0 copy-start.1
  59.0 1.4 copy-done.1
  60.3 8.1 %all-to-all-done.2.fringe_ref = bf16[16,8,16,128]{3,2,1,0:T(8,128)(2,1)S(1)} async-done(((bf16[16,8,16,128]{3,2,1,0:T(8,128)(2,1)}), bf16[16,8,16,128]{3,2,1,0:T(8,128)(2,1)S(1)}, u32[]{:S(2)}, u32[]{:S(2)}) %all-to-all-start.2) | async-done | bytes 524320 | tf_op jit(solution)/shard_map/all_to_all | solution.py:207
  68.4 63.2 %all_to_all.21 = s32[256,1,2176]{2,1,0:T(1,128)S(1)} all-to-all(s32[256,1,2176]{2,1,0:T(1,128)} %bitcast.16), channel_id=1, replica_groups=mesh['tm'=16,'chan'=16] {'tm','chan'}, dimensions={0} | all-to-all | bytes 4456448 | tf_op jit(solution)/shard_map/all_to_all | solution.py:184
  131.6 0.0 all-gather.2.cloned.1.call-done
  131.6 0.0 copy-done.6
  131.6 0.0 copy-start.2
  131.6 2.2 %copy-done.2 = bf16[8192,256]{1,0:T(8,128)(2,1)S(1)} copy-done((bf16[8192,256]{1,0:T(8,128)(2,1)S(1)}, bf16[8192,256]{1,0:T(8,128)(2,1)}, u32[]{:S(2)}) %copy-start.2) | copy-done | bytes 4194328
  133.8 17.5 %filter.1 = f32[2,8,128,512]{3,2,1,0:T(8,128)} custom-call(s32[2048]{0:T(1024)S(1)} %copy-done.6, s32[2]{0:T(128)S(1)} %pad_add_fusion.place_ref, s32[16,272,128]{2,1,0:T(8,128)S(1)} %bitcast.15, bf16[16,8,16,128]{3,2,1,0:T(8,128)(2,1)S(1)} %all-to-all-done.2.fringe_ref, bf16[8,2,512,256]{3,2,1,0:T(8,128)(2,1)S(1)} %bitcast.17), custom_call_target="tpu_custom_call" | custom-call | tf_op jit(solution)/shard_map/filter/pallas_call | solution.py:215
  (2 shorter events, 0.0 us)
Async XLA Ops:
  6.5 1.0 copy-start
  6.5 47.9 %copy-start.4 = (s32[2048,32]{0,1:T(8,128)S(1)}, s32[2048,32]{0,1:T(8,128)}, u32[]{:S(2)}) copy-start(s32[2048,32]{0,1:T(8,128)} %param.7) | copy-start | bytes 786436
  6.5 125.1 %all-gather.2.cloned.1.call-start = ((), (), s32[]{:S(2)}) async-start(), calls=%async_computation.4 | async-start | bytes 4456448 | tf_op jit(solution)/shard_map/all_gather | solution.py:167
  30.3 16.4 %all-to-all-start.1 = ((bf16[16,4,16,128]{3,2,1,0:T(8,128)(2,1)}), bf16[16,4,16,128]{3,2,1,0:T(8,128)(2,1)S(1)}, u32[]{:S(2)}, u32[]{:S(2)}) async-start(bf16[16,4,16,128]{3,2,1,0:T(8,128)(2,1)} %bitcast.8), calls=%async_computation.1 | async-start | bytes 524288 | tf_op jit(solution)/shard_map/all_to_all | solution.py:193
  46.7 0.7 copy-start.5
  50.0 18.4 %all-to-all-start.2 = ((bf16[16,8,16,128]{3,2,1,0:T(8,128)(2,1)}), bf16[16,8,16,128]{3,2,1,0:T(8,128)(2,1)S(1)}, u32[]{:S(2)}, u32[]{:S(2)}) async-start(bf16[16,8,16,128]{3,2,1,0:T(8,128)(2,1)} %select.7), calls=%async_computation.2 | async-start | bytes 1048576 | tf_op jit(solution)/shard_map/all_to_all | solution.py:207
  54.5 2.3 %copy-start.3 = (f32[2,2048,8,32]{1,3,2,0:T(8,128)S(1)}, f32[2,2048,8,32]{1,3,2,0:T(8,128)}, u32[]{:S(2)}) copy-start(f32[2,2048,8,32]{1,3,2,0:T(8,128)} %param.5) | copy-start | bytes 12582916
  56.8 74.8 %copy-start.6 = (s32[2048]{0:T(1024)S(1)}, s32[2048]{0:T(1024)}, u32[]{:S(2)}) copy-start(s32[2048]{0:T(1024)} %groups_ref.3) | copy-start | bytes 24580
  59.0 1.4 copy-start.1
  131.6 2.2 %copy-start.2 = (bf16[8192,256]{1,0:T(8,128)(2,1)S(1)}, bf16[8192,256]{1,0:T(8,128)(2,1)}, u32[]{:S(2)}) copy-start(bf16[8192,256]{1,0:T(8,128)(2,1)} %all-gather.2.cloned.1.call-done) | copy-start | bytes 12582916
Sparse Core Ops, SparseCore 0:
  28.7 45.1 all-gather.1
where the time goes:
time: 159 us; the launch traced here: 158 us
  blocking collectives  84.3 us (53%)
  Pallas kernels  22.2 us (14%)
  waiting for transfers between devices  17.2 us (11%)
  between operations  13.4 us (8%)
  starting transfers between devices  11.7 us (7%)
  local copies, waits for them, and re-layouts  9.2 us (6%)
    all_to_all x1, blocking collectives, shards(): lax.all_to_all(packed.reshape(devices, 1, rows * LANES), everyone, split_...  63.2 us
    all_to_all x1, blocking collectives, shards(): lax.all_to_all(jnp.broadcast_to(share, (chan_count, chans, wide)), 'chan'...  21.1 us
    pallas_call x1, Pallas kernels, shards(): pl.pallas_call(functools.partial(filter_kernel, rows=rows), grid_spec=plt...  17.5 us
    all_to_all x1, waiting for transfers between devices, shards(): table = lax.all_to_all(slabs, 'tm', split_axis=0, concat_axis=0, tiled=True)  9.07 us
    all_to_all x1, waiting for transfers between devices, shards(): mats = lax.all_to_all(chosen, 'tm', split_axis=0, concat_axis=0, tiled=True)  8.06 us
    unnamed x14, local copies, waits for them, and re-layouts  7.49 us
    all_to_all x1, starting transfers between devices, shards(): table = lax.all_to_all(slabs, 'tm', split_axis=0, concat_axis=0, tiled=True)  7.27 us
    all_to_all x1, starting transfers between devices, shards(): mats = lax.all_to_all(chosen, 'tm', split_axis=0, concat_axis=0, tiled=True)  4.48 us
  transfers between devices with their start and end apart: 3, of which 2 were waited for; matrix products, arithmetic and copies ran while one was open for 1% of the time, Pallas kernels for 3%

commit v1 on v0

--- a/solution.py
+++ b/solution.py
@@ -11,7 +11,8 @@
 SUB = 8
 FULL = 32760.0
 MIDDLE = 32768.0
-VMEM = 40 * 1024 * 1024
+VMEM = 56 * 1024 * 1024
+CORES = 2
 
 
 def pack_kernel(vis_ref, flag_ref, out_ref, rows):
@@ -37,55 +38,84 @@
             out_ref[place : place + 1, :] = level_row
 
 
-def select_kernel(groups_ref, place_ref, table_ref, out_ref):
-    owners, each = out_ref.shape[0], out_ref.shape[1]
-    chan_count = groups_ref.shape[0] // (owners * each)
-
-    def step(n, carry):
-        owner = n // each
-        slot = n % each
-        group = groups_ref[(owner * chan_count + place_ref[1]) * each + slot]
-        out_ref[owner, slot] = table_ref[group]
-        return carry
-
-    lax.fori_loop(0, owners * each, step, 0, unroll=8)
-
-
-def filter_kernel(
-    groups_ref, place_ref, words_ref, fringe_ref, delay_ref, out_ref, levels, samples, *, rows
-):
+def shares_kernel(place_ref, fringe_ref, *out_refs):
+    halves, pieces = fringe_ref.shape[0], fringe_ref.shape[2]
+    for core, out_ref in enumerate(out_refs):
+        for chip in range(out_ref.shape[0]):
+            slab = place_ref[0] ^ (chip * CORES + core)
+            out_ref[chip] = fringe_ref[slab // pieces, :, lax.rem(slab, pieces)]
+
+
+def regroup_kernel(*refs):
+    for core in range(CORES):
+        for chip, out_ref in enumerate(refs[CORES:]):
+            out_ref[core] = refs[core][chip]
+
+
+def select_kernel(groups_ref, place_ref, *refs):
+    in_refs, out_refs, table = refs[: -CORES - 1], refs[-CORES - 1 : -1], refs[-1]
+    count, held, each = table.shape[0], table.shape[1], out_refs[0].shape[1]
+    chan_count = groups_ref.shape[0] // (count * each)
+    for chip, in_ref in enumerate(in_refs):
+        for core in range(CORES):
+            table[place_ref[0] ^ (chip * CORES + core)] = in_ref[core]
+    for core, out_ref in enumerate(out_refs):
+        for chip in range(out_ref.shape[0]):
+            owner = place_ref[0] ^ (chip * CORES + core)
+            for slot in range(each):
+                group = groups_ref[(owner * chan_count + place_ref[1]) * each + slot]
+                out_ref[chip, slot] = table[group // held, lax.rem(group, held)]
+
+
+def filter_kernel(groups_ref, place_ref, words_ref, delay_ref, *refs, rows, spread):
+    fringe_refs = refs[:-10]
+    out_ref, words, levels, samples, slabs, mats, delay, word_sems, slab_sems, delay_sems = refs[-10:]
     baseline = pl.program_id(0)
+    baselines = pl.num_programs(0)
     blocks = words_ref.shape[0]
     chan_count = words_ref.shape[1] // rows
     quads = chan_count // 4
-    times = rows - 1
+    slot = lax.rem(baseline, 2)
+
+    def fetch_words(block):
+        return pltpu.make_async_copy(words_ref.at[block], words.at[block], word_sems.at[block])
+
+    def fetch_slabs(chip):
+        return pltpu.make_async_copy(fringe_refs[chip], slabs.at[chip], slab_sems.at[chip])
+
+    def fetch_delay(number, to):
+        mine = (place_ref[0] * chan_count + place_ref[1]) * baselines + number
+        group = groups_ref[mine] // spread
+        return pltpu.make_async_copy(delay_ref.at[group], delay.at[to], delay_sems.at[to])
 
     @pl.when(baseline == 0)
     def unpack():
+        for block in range(blocks):
+            fetch_words(block).start()
+        for chip in range(len(fringe_refs)):
+            fetch_slabs(chip).start()
+        fetch_delay(0, 0).start()
         lane = lax.broadcasted_iota(jnp.int32, (SUB, LANES), 1)
         low_half = lane < 64
         even_group = (lane & 32) == 0
         group = lane // 32
-        level_rows = [
-            words_ref[block, source * rows + rows - 1 : source * rows + rows, :]
-            for block in range(blocks)
-            for source in range(chan_count)
-        ]
-        level_all = jnp.concatenate(level_rows, axis=0).astype(jnp.float32)
-        scale_all = jnp.exp2(level_all * 0.25) * (1.0 / FULL)
-        levels[...] = scale_all.T
-        own = levels[pl.ds(pl.multiple_of(place_ref[1] * SUB, SUB), SUB), :]
         for block in range(blocks):
+            fetch_words(block).wait()
+            level = words[block, pl.ds(rows - 1, chan_count, stride=rows), :].astype(jnp.float32)
+            scales = jnp.exp2(level * 0.25) * (1.0 / FULL)
+            scales = jnp.concatenate([scales, jnp.zeros((LANES - chan_count, LANES), jnp.float32)], axis=0)
+            levels[...] = scales.T
+            own = levels[pl.ds(pl.multiple_of(place_ref[1] * SUB, SUB), SUB), :]
             for quad in range(quads):
-                first = block * chan_count + quad * 4
+                first = quad * 4
                 scale = jnp.broadcast_to(own[:, first : first + 1], (SUB, LANES))
                 for member in range(1, 4):
                     other = jnp.broadcast_to(own[:, first + member : first + member + 1], (SUB, LANES))
                     scale = jnp.where(group == member, other, scale)
                 offset = scale * -MIDDLE
-                for half in range(times // SUB):
+                for half in range((rows - 1) // SUB):
                     v = [
-                        words_ref[block, pl.ds((quad * 4 + member) * rows + half * SUB, SUB), :]
+                        words[block, pl.ds((quad * 4 + member) * rows + half * SUB, SUB), :]
                         for member in range(4)
                     ]
                     r = [pltpu.roll(x, 64, 1) for x in v]
@@ -105,6 +135,12 @@
                         imag = lax.shift_right_logical(word, 16).astype(jnp.float32) * scale + offset
                         samples[0, quad, at : at + SUB, :] = real
                         samples[1, quad, at : at + SUB, :] = imag
+        for chip in range(len(fringe_refs)):
+            fetch_slabs(chip).wait()
+
+    @pl.when(baseline + 1 < baselines)
+    def ahead():
+        fetch_delay(baseline + 1, 1 - slot).start()
 
     count = samples.shape[2] // SUB
     parts = []
@@ -117,8 +153,11 @@
     data = jnp.concatenate(parts, axis=0)
     high = data.astype(jnp.bfloat16)
     low = (data - high.astype(jnp.float32)).astype(jnp.bfloat16)
-    mats = fringe_ref[...].reshape(2 * count, count)
-    real, imag = mats[:count], mats[count:]
+    for chip in range(len(fringe_refs)):
+        for core in range(CORES):
+            mats[place_ref[0] ^ (chip * CORES + core)] = slabs[chip, core, baseline]
+    whole = mats[...].reshape(2 * count, count)
+    real, imag = whole[:count], whole[count:]
     both = jnp.concatenate(
         [jnp.concatenate([real, -imag], axis=1), jnp.concatenate([imag, real], axis=1)], axis=0
     )
@@ -127,18 +166,19 @@
     )
     high = rated.astype(jnp.bfloat16)
     low = (rated - high.astype(jnp.float32)).astype(jnp.bfloat16)
+    fetch_delay(baseline, slot).wait()
+    both = jnp.concatenate([high, low], axis=0)
+    wide = delay.shape[3]
     total = None
-    wide = delay_ref.shape[3]
-    for piece in range(delay_ref.shape[1]):
-        for values in (high, low):
-            term = lax.dot_general(
-                values[:, piece * wide : (piece + 1) * wide],
-                delay_ref[0, piece],
-                (((1,), (1,)), ((), ())),
-                preferred_element_type=jnp.float32,
-            )
-            total = term if total is None else total + term
-    out_ref[...] = total.reshape(out_ref.shape)
+    for piece in range(delay.shape[1]):
+        term = lax.dot_general(
+            both[:, piece * wide : (piece + 1) * wide],
+            delay[slot, piece],
+            (((1,), (1,)), ((), ())),
+            preferred_element_type=jnp.float32,
+        )
+        total = term if total is None else total + term
+    out_ref[...] = (total[: 2 * count] + total[2 * count :]).reshape(out_ref.shape)
 
 
 def shards(visibility, groups, flags, fringe, delay):
@@ -164,8 +204,6 @@
     share = lax.all_to_all(
         jnp.broadcast_to(share, (chan_count, chans, wide)), "chan", split_axis=0, concat_axis=0, tiled=True
     )
-    delay_all = lax.all_gather(share.reshape(all_chans, wide), "tm", axis=0, tiled=True)
-    delay_all = delay_all.reshape(delay_groups, pieces, all_chans, wide)
 
     rows = times * chans * SUB // LANES // SUB * own + 1
     step_lanes = 2 * LANES
@@ -181,57 +219,83 @@
         compiler_params=params(),
         name="pack",
     )(jnp.transpose(visibility, (0, 2, 3, 1)), flags.T)
+    share, fringe, packed = lax.optimization_barrier((share, fringe, packed))
+    delay_all = lax.all_gather(share.reshape(all_chans, wide), "tm", axis=0, tiled=True)
+    delay_all = delay_all.reshape(delay_groups, pieces, all_chans, wide)
     words = lax.all_to_all(
         packed.reshape(devices, 1, rows * LANES), everyone, split_axis=0, concat_axis=0, tiled=True
     )
     words = words.reshape(time_count, chan_count * rows, LANES)
 
+    def crossed(array, mask):
+        return lax.ppermute(array, "tm", [(k, k ^ mask) for k in range(time_count)]) if mask else array
+
+    chips = time_count // CORES
     held = fringe.shape[1]
     slab = 2 * all_times // time_count
-    slabs = fringe.reshape(2, held, all_times // slab, slab, all_times)
-    slabs = jnp.transpose(slabs, (0, 2, 1, 3, 4)).reshape(time_count, held, slab, all_times)
-    table = lax.all_to_all(slabs, "tm", split_axis=0, concat_axis=0, tiled=True)
-    table = table.reshape(time_count * held, slab, all_times)
+    inside = pl.BlockSpec(memory_space=pltpu.VMEM)
+
+    def exchanged(arrays):
+        _, *block = arrays[0].shape
+        turned = pl.pallas_call(
+            regroup_kernel,
+            in_specs=[inside] * CORES,
+            out_specs=[inside] * chips,
+            out_shape=[jax.ShapeDtypeStruct((CORES, *block), jnp.bfloat16)] * chips,
+            compiler_params=params(),
+            name="regroup",
+        )(*[crossed(array, core) for core, array in enumerate(arrays)])
+        return [crossed(array, chip * CORES) for chip, array in enumerate(turned)]
+
+    shares = pl.pallas_call(
+        shares_kernel,
+        grid_spec=pltpu.PrefetchScalarGridSpec(
+            num_scalar_prefetch=1, grid=(), in_specs=[inside], out_specs=[inside] * CORES
+        ),
+        out_shape=[jax.ShapeDtypeStruct((chips, held, slab, all_times), jnp.bfloat16)] * CORES,
+        compiler_params=params(),
+        name="shares",
+    )(place, fringe.reshape(2, held, all_times // slab, slab, all_times))
     chosen = pl.pallas_call(
         select_kernel,
         grid_spec=pltpu.PrefetchScalarGridSpec(
             num_scalar_prefetch=2,
             grid=(),
-            in_specs=[pl.BlockSpec(memory_space=pltpu.VMEM)],
-            out_specs=pl.BlockSpec(memory_space=pltpu.VMEM),
+            in_specs=[inside] * chips,
+            out_specs=[inside] * CORES,
+            scratch_shapes=[pltpu.VMEM((time_count, held, slab, all_times), jnp.bfloat16)],
         ),
-        out_shape=jax.ShapeDtypeStruct((time_count, own, slab, all_times), jnp.bfloat16),
+        out_shape=[jax.ShapeDtypeStruct((chips, own, slab, all_times), jnp.bfloat16)] * CORES,
         compiler_params=params(),
         name="select",
-    )(groups, place, table)
-    mats = lax.all_to_all(chosen, "tm", split_axis=0, concat_axis=0, tiled=True)
+    )(groups, place, *exchanged(shares))
+    mats = exchanged(chosen)
 
     spread = time_count * held // delay_groups
 
-    def delay_index(n, groups_ref, place_ref):
-        mine = (place_ref[0] * chan_count + place_ref[1]) * own + n
-        return (groups_ref[mine] // spread, 0, 0, 0)
-
     return pl.pallas_call(
-        functools.partial(filter_kernel, rows=rows),
+        functools.partial(filter_kernel, rows=rows, spread=spread),
         grid_spec=pltpu.PrefetchScalarGridSpec(
             num_scalar_prefetch=2,
             grid=(own,),
-            in_specs=[
-                pl.BlockSpec((time_count, chan_count * rows, LANES), lambda n, *_: (0, 0, 0)),
-                pl.BlockSpec((time_count, 1, slab, all_times), lambda n, *_: (0, n, 0, 0)),
-                pl.BlockSpec((1, pieces, all_chans, wide), delay_index),
-            ],
+            in_specs=[pl.BlockSpec(memory_space=pl.ANY)] * (2 + chips),
             out_specs=pl.BlockSpec((2, 1, all_times, all_chans), lambda n, *_: (0, n, 0, 0)),
             scratch_shapes=[
-                pltpu.VMEM((LANES, devices), jnp.float32),
+                pltpu.VMEM((time_count, chan_count * rows, LANES), jnp.int32),
+                pltpu.VMEM((LANES, LANES), jnp.float32),
                 pltpu.VMEM((2, all_chans // LANES, all_times * SUB, LANES), jnp.float32),
+                pltpu.VMEM((chips, CORES, own, slab, all_times), jnp.bfloat16),
+                pltpu.VMEM((time_count, slab, all_times), jnp.bfloat16),
+                pltpu.VMEM((2, pieces, all_chans, wide), jnp.bfloat16),
+                pltpu.SemaphoreType.DMA((time_count,)),
+                pltpu.SemaphoreType.DMA((chips,)),
+                pltpu.SemaphoreType.DMA((2,)),
             ],
         ),
         out_shape=jax.ShapeDtypeStruct((2, own, all_times, all_chans), jnp.float32),
         compiler_params=params(),
         name="filter",
-    )(groups, place, words, mats, delay_all)
+    )(groups, place, words, delay_all, *mats)
 
 
 def solution(mesh):

time: 159 us -> 120 us (0.75)
  blocking collectives: 84.3 us -> 0 us
  starting transfers between devices: 11.7 us -> 44.5 us
  Pallas kernels: 22.2 us -> 30.2 us
  waiting for transfers between devices: 17.2 us -> 24 us
  local copies, waits for them, and re-layouts: 9.2 us -> 5.69 us
    all_to_all x2 -> x0, blocking collectives: 84.3 us -> none  [the longest x1 63.2 us: shards(): lax.all_to_all(packed.reshape(devices, 1, rows * LANES), everyone, split_...]
    ppermute x0 -> x16, starting transfers between devices: none -> 23.8 us  [crossed(): lax.ppermute(array, 'tm', [(k, k ^ mask) for k in range(time_count)])]
    ppermute x0 -> x16, waiting for transfers between devices: none -> 18.9 us  [crossed(): lax.ppermute(array, 'tm', [(k, k ^ mask) for k in range(time_count)])]
    all_to_all x2, waiting for transfers between devices: 17.1 us -> 5.08 us  [the longest x1 3.63 us: shards(): lax.all_to_all(jnp.broadcast_to(share, (chan_count, chans, wide)), 'chan'...]
    all_to_all x2, starting transfers between devices: 11.7 us -> 20.7 us  [the longest x1 10.7 us: shards(): lax.all_to_all(jnp.broadcast_to(share, (chan_count, chans, wide)), 'chan'...]
    pallas_call x1, Pallas kernels: 2.17 us -> 6.84 us  [shards(): pl.pallas_call(functools.partial(pack_kernel, rows=rows), grid=(total //...]
    pallas_call x1 -> x4, Pallas kernels: 17.5 us -> 20.1 us  [the longest x1 14.2 us: shards(): pl.pallas_call(functools.partial(filter_kernel, rows=rows, spread=spread)...]
    unnamed x14 -> x38, local copies, waits for them, and re-layouts: 7.49 us -> 4.96 us
  transfers between devices with their start and end apart: 3 -> 19, of which waited for: 2 -> 10; matrix products, arithmetic and copies ran while one was open for 1% -> 1% of each run, Pallas kernels for 3% -> 14%
where the time goes in v1:
time: 120 us; the launch traced here: 119 us
  starting transfers between devices  44.5 us (37%)
  Pallas kernels  30.2 us (25%)
  waiting for transfers between devices  24 us (20%)
  between operations  13.6 us (11%)
  local copies, waits for them, and re-layouts  5.69 us (5%)
    ppermute x16, starting transfers between devices, crossed(): lax.ppermute(array, 'tm', [(k, k ^ mask) for k in range(time_count)])  23.8 us
    ppermute x16, waiting for transfers between devices, crossed(): lax.ppermute(array, 'tm', [(k, k ^ mask) for k in range(time_count)])  18.9 us
    pallas_call x1, Pallas kernels, shards(): pl.pallas_call(functools.partial(filter_kernel, rows=rows, spread=spread)...  14.2 us
    all_to_all x1, starting transfers between devices, shards(): lax.all_to_all(jnp.broadcast_to(share, (chan_count, chans, wide)), 'chan'...  10.7 us
    all_to_all x1, starting transfers between devices, shards(): lax.all_to_all(packed.reshape(devices, 1, rows * LANES), everyone, split_...  10 us
    pallas_call x1, Pallas kernels, shards(): pl.pallas_call(functools.partial(pack_kernel, rows=rows), grid=(total //...  6.84 us
    unnamed x38, local copies, waits for them, and re-layouts  4.96 us
    all_to_all x1, waiting for transfers between devices, shards(): lax.all_to_all(jnp.broadcast_to(share, (chan_count, chans, wide)), 'chan'...  3.63 us
  transfers between devices with their start and end apart: 19, of which 10 were waited for; matrix products, arithmetic and copies ran while one was open for 1% of the time, Pallas kernels for 14%

profile of v1, /device:TPU:33, one launch (start us, length us, event | category | flops | bytes accessed | tf_op | source)
XLA Modules:
  0.0 118.7 jit_solution(665675237689727546)
XLA Ops:
  6.5 0.0 copy-start
  6.5 0.9 copy-done
  7.5 0.7 broadcast_in_dim.8
  8.2 10.7 %all-to-all-start = ((bf16[16,32,256]{2,1,0:T(8,128)(2,1)}), bf16[16,32,256]{2,1,0:T(8,128)(2,1)S(1)}, u32[]{:S(2)}, u32[]{:S(2)}) async-start(bf16[16,32,256]{2,1,0:T(8,128)(2,1)} %broadcast_in_dim.8), calls=%async_computation | async-start | bytes 524288 | tf_op jit(solution)/shard_map/all_to_all | solution.py:204
  18.9 0.0 all-gather.2.cloned.1.call-start
  18.9 6.8 %pack.1 = s32[4352,128]{1,0:T(8,128)} custom-call(f32[2,8,32,2048]{3,2,1,0:T(8,128)} %bitcast.14, s32[32,2048]{1,0:T(8,128)} %bitcast.16), custom_call_target="tpu_custom_call" | custom-call | tf_op jit(solution)/shard_map/pack/pallas_call | solution.py:210
  25.8 3.6 %all-to-all-done = bf16[16,32,256]{2,1,0:T(8,128)(2,1)S(1)} async-done(((bf16[16,32,256]{2,1,0:T(8,128)(2,1)}), bf16[16,32,256]{2,1,0:T(8,128)(2,1)S(1)}, u32[]{:S(2)}, u32[]{:S(2)}) %all-to-all-start) | async-done | bytes 262176 | tf_op jit(solution)/shard_map/all_to_all | solution.py:204
  29.4 0.7 copy-done.2
  30.1 0.0 all-gather.2.cloned.1.call-update
  30.1 10.0 %all-to-all-start.1 = ((s32[256,1,2176]{2,1,0:T(1,128)}), s32[256,1,2176]{2,1,0:T(1,128)S(1)}, u32[]{:S(2)}, u32[]{:S(2)}) async-start(s32[256,1,2176]{2,1,0:T(1,128)} %bitcast.12), calls=%async_computation.1 | async-start | bytes 4456448 | tf_op jit(solution)/shard_map/all_to_all | solution.py:225
  40.2 0.7 pad_add_fusion.place_ref
  40.9 2.4 %shares.1 = (bf16[8,4,16,128]{3,2,1,0:T(8,128)(2,1)}, bf16[8,4,16,128]{3,2,1,0:T(8,128)(2,1)}) custom-call(s32[2]{0:T(128)} %pad_add_fusion.place_ref, bf16[2,4,8,16,128]{4,3,2,1,0:T(8,128)(2,1)} %bitcast.17), custom_call_target="tpu_custom_call" | custom-call | tf_op jit(solution)/shard_map/shares/pallas_call | solution.py:250
  43.2 0.4 collective-permute-start
  43.6 1.2 %collective-permute-done.refs_1_ = bf16[8,4,16,128]{3,2,1,0:T(8,128)(2,1)S(1)} collective-permute-done((bf16[8,4,16,128]{3,2,1,0:T(8,128)(2,1)}, bf16[8,4,16,128]{3,2,1,0:T(8,128)(2,1)S(1)}, u32[]{:S(2)}, u32[]{:S(2)}) %collective-permute-start) | collective-permute-done | bytes 131104 | tf_op jit(solution)/shard_map/ppermute | solution.py:231
  44.8 0.6 copy-done.4
  45.4 1.7 %regroup.2 = (bf16[2,4,16,128]{3,2,1,0:T(8,128)(2,1)}, bf16[2,4,16,128]{3,2,1,0:T(8,128)(2,1)}, bf16[2,4,16,128]{3,2,1,0:T(8,128)(2,1)}, bf16[2,4,16,128]{3,2,1,...) custom-call(bf16[8,4,16,128]{3,2,1,0:T(8,128)(2,1)} %get-tuple-eleme, ...), custom_call_target="tpu_custom_call" | custom-call | tf_op jit(solution)/shard_map/regroup/pallas_call | solution.py:240
  47.1 1.2 %collective-permute-start.1 = (bf16[2,4,16,128]{3,2,1,0:T(8,128)(2,1)}, bf16[2,4,16,128]{3,2,1,0:T(8,128)(2,1)S(1)}, u32[]{:S(2)}, u32[]{:S(2)}) collective-permute-start(bf16[2,4,16,128]{3,2,1,0:T(8,128)(2,1)} %get-tuple-element.34), channel_id=1, source_target_pairs={{0,32},{16,48},{32,0},{48,16},{64,96},{80,112},{96,64},{112,80},{1... | collective-permute-start | bytes 98312 | tf_op jit(solution)/shard_map/ppermute | solution.py:231
  48.3 2.4 %collective-permute-start.2 = (bf16[2,4,16,128]{3,2,1,0:T(8,128)(2,1)}, bf16[2,4,16,128]{3,2,1,0:T(8,128)(2,1)S(1)}, u32[]{:S(2)}, u32[]{:S(2)}) collective-permute-start(bf16[2,4,16,128]{3,2,1,0:T(8,128)(2,1)} %get-tuple-element.35), channel_id=1, source_target_pairs={{0,64},{16,80},{32,96},{48,112},{64,0},{80,16},{96,32},{112,48},{1... | collective-permute-start | bytes 98312 | tf_op jit(solution)/shard_map/ppermute | solution.py:231
  50.8 0.2 collective-permute-start.3
  51.0 1.3 %collective-permute-start.4 = (bf16[2,4,16,128]{3,2,1,0:T(8,128)(2,1)}, bf16[2,4,16,128]{3,2,1,0:T(8,128)(2,1)S(1)}, u32[]{:S(2)}, u32[]{:S(2)}) collective-permute-start(bf16[2,4,16,128]{3,2,1,0:T(8,128)(2,1)} %get-tuple-element.37), channel_id=1, source_target_pairs={{0,128},{16,144},{32,160},{48,176},{64,192},{80,208},{96,224},{112... | collective-permute-start | bytes 98312 | tf_op jit(solution)/shard_map/ppermute | solution.py:231
  52.2 0.0 collective-permute-start.5
  52.3 0.7 collective-permute-done.1.refs_1_
  53.0 3.8 %collective-permute-start.6 = (bf16[2,4,16,128]{3,2,1,0:T(8,128)(2,1)}, bf16[2,4,16,128]{3,2,1,0:T(8,128)(2,1)S(1)}, u32[]{:S(2)}, u32[]{:S(2)}) collective-permute-start(bf16[2,4,16,128]{3,2,1,0:T(8,128)(2,1)} %get-tuple-element.39), channel_id=1, source_target_pairs={{0,192},{16,208},{32,224},{48,240},{64,128},{80,144},{96,160},{112... | collective-permute-start | bytes 98312 | tf_op jit(solution)/shard_map/ppermute | solution.py:231
  56.8 0.0 collective-permute-done.2.refs_2_
  56.8 1.7 %collective-permute-start.7 = (bf16[2,4,16,128]{3,2,1,0:T(8,128)(2,1)}, bf16[2,4,16,128]{3,2,1,0:T(8,128)(2,1)S(1)}, u32[]{:S(2)}, u32[]{:S(2)}) collective-permute-start(bf16[2,4,16,128]{3,2,1,0:T(8,128)(2,1)} %get-tuple-element.40), channel_id=1, source_target_pairs={{0,224},{16,240},{32,192},{48,208},{64,160},{80,176},{96,128},{112... | collective-permute-start | bytes 98312 | tf_op jit(solution)/shard_map/ppermute | solution.py:231
  58.5 0.0 collective-permute-done.3.refs_3_
  58.5 0.0 collective-permute-done.4.refs_4_
  58.5 0.0 copy-start.15
  58.6 0.0 collective-permute-done.5.refs_5_
  58.6 0.0 copy-start.16
  58.6 4.0 %collective-permute-done.6.refs_6_ = bf16[2,4,16,128]{3,2,1,0:T(8,128)(2,1)S(1)} collective-permute-done((bf16[2,4,16,128]{3,2,1,0:T(8,128)(2,1)}, bf16[2,4,16,128]{3,2,1,0:T(8,128)(2,1)S(1)}, u32[]{:S(2)}, u32[]{:S(2)}) %collective-permute-start.6) | collective-permute-done | bytes 32800 | tf_op jit(solution)/shard_map/ppermute | solution.py:231
  62.5 0.0 collective-permute-done.7.refs_7_
  62.6 0.0 copy-done.12
  62.6 0.0 copy-done.13
  62.6 0.0 copy-done.14
  62.6 0.0 copy-done.15
  62.6 0.0 copy-done.16
  62.6 0.5 copy-done.17
  63.1 0.0 copy-done.18
  63.2 3.3 %select.7 = (bf16[8,8,16,128]{3,2,1,0:T(8,128)(2,1)}, bf16[8,8,16,128]{3,2,1,0:T(8,128)(2,1)}) custom-call(s32[2048]{0:T(1024)} %groups_ref.3, s32[2]{0:T(128)} %pad_add_fusion.place_ref, bf16[2,4,16,128]{3,2,1,0:T(8,128)(2,1)} %get-tuple-element.33.refs_0_, bf16[2,4,16,128]{3,2,1,0:T(8,128)(2,1)} %copy-done.12, bf16[2,4,16,128]{3,2,1,0:T(8,128)(2,1)} %copy-done.13, ...), custom_call_target="tpu_custom_call" | custom-call | tf_op jit(solution)/shard_map/select/pallas_call | solution.py:259
  66.4 3.6 %collective-permute-start.8 = (bf16[8,8,16,128]{3,2,1,0:T(8,128)(2,1)}, bf16[8,8,16,128]{3,2,1,0:T(8,128)(2,1)S(1)}, u32[]{:S(2)}, u32[]{:S(2)}) collective-permute-start(bf16[8,8,16,128]{3,2,1,0:T(8,128)(2,1)} %get-tuple-element.42), channel_id=1, source_target_pairs={{0,16},{16,0},{32,48},{48,32},{64,80},{80,64},{96,112},{112,96},{1... | collective-permute-start | bytes 786440 | tf_op jit(solution)/shard_map/ppermute | solution.py:231
  70.0 1.4 %collective-permute-done.8.refs_1_ = bf16[8,8,16,128]{3,2,1,0:T(8,128)(2,1)S(1)} collective-permute-done((bf16[8,8,16,128]{3,2,1,0:T(8,128)(2,1)}, bf16[8,8,16,128]{3,2,1,0:T(8,128)(2,1)S(1)}, u32[]{:S(2)}, u32[]{:S(2)}) %collective-permute-start.8) | collective-permute-done | bytes 262176 | tf_op jit(solution)/shard_map/ppermute | solution.py:231
  71.4 0.7 copy-done.3
  72.1 1.9 %regroup.3 = (bf16[2,8,16,128]{3,2,1,0:T(8,128)(2,1)}, bf16[2,8,16,128]{3,2,1,0:T(8,128)(2,1)}, bf16[2,8,16,128]{3,2,1,0:T(8,128)(2,1)}, bf16[2,8,16,128]{3,2,1,...) custom-call(bf16[8,8,16,128]{3,2,1,0:T(8,128)(2,1)} %get-tuple-eleme, ...), custom_call_target="tpu_custom_call" | custom-call | tf_op jit(solution)/shard_map/regroup/pallas_call | solution.py:240
  73.9 0.0 collective-permute-start.9
  73.9 1.0 collective-permute-start.10
  74.9 2.9 %collective-permute-start.11 = (bf16[2,8,16,128]{3,2,1,0:T(8,128)(2,1)}, bf16[2,8,16,128]{3,2,1,0:T(8,128)(2,1)S(1)}, u32[]{:S(2)}, u32[]{:S(2)}) collective-permute-start(bf16[2,8,16,128]{3,2,1,0:T(8,128)(2,1)} %get-tuple-element.46), channel_id=1, source_target_pairs={{0,96},{16,112},{32,64},{48,80},{64,32},{80,48},{96,0},{112,16},{1... | collective-permute-start | bytes 196616 | tf_op jit(solution)/shard_map/ppermute | solution.py:231
  77.8 0.2 collective-permute-start.12
  78.0 0.0 collective-permute-start.13
  78.0 2.3 %collective-permute-done.9.refs_1_ = bf16[2,8,16,128]{3,2,1,0:T(8,128)(2,1)S(1)} collective-permute-done((bf16[2,8,16,128]{3,2,1,0:T(8,128)(2,1)}, bf16[2,8,16,128]{3,2,1,0:T(8,128)(2,1)S(1)}, u32[]{:S(2)}, u32[]{:S(2)}) %collective-permute-start.9) | collective-permute-done | bytes 65568 | tf_op jit(solution)/shard_map/ppermute | solution.py:231
  80.3 2.9 %collective-permute-start.14 = (bf16[2,8,16,128]{3,2,1,0:T(8,128)(2,1)}, bf16[2,8,16,128]{3,2,1,0:T(8,128)(2,1)S(1)}, u32[]{:S(2)}, u32[]{:S(2)}) collective-permute-start(bf16[2,8,16,128]{3,2,1,0:T(8,128)(2,1)} %get-tuple-element.49), channel_id=1, source_target_pairs={{0,192},{16,208},{32,224},{48,240},{64,128},{80,144},{96,160},{112... | collective-permute-start | bytes 196616 | tf_op jit(solution)/shard_map/ppermute | solution.py:231
  83.2 3.2 %collective-permute-done.10.refs_2_ = bf16[2,8,16,128]{3,2,1,0:T(8,128)(2,1)S(1)} collective-permute-done((bf16[2,8,16,128]{3,2,1,0:T(8,128)(2,1)}, bf16[2,8,16,128]{3,2,1,0:T(8,128)(2,1)S(1)}, u32[]{:S(2)}, u32[]{:S(2)}) %collective-permute-start.10) | collective-permute-done | bytes 65568 | tf_op jit(solution)/shard_map/ppermute | solution.py:231
  86.4 2.2 %collective-permute-start.15 = (bf16[2,8,16,128]{3,2,1,0:T(8,128)(2,1)}, bf16[2,8,16,128]{3,2,1,0:T(8,128)(2,1)S(1)}, u32[]{:S(2)}, u32[]{:S(2)}) collective-permute-start(bf16[2,8,16,128]{3,2,1,0:T(8,128)(2,1)} %get-tuple-element.50), channel_id=1, source_target_pairs={{0,224},{16,240},{32,192},{48,208},{64,160},{80,176},{96,128},{112... | collective-permute-start | bytes 196616 | tf_op jit(solution)/shard_map/ppermute | solution.py:231
  88.6 0.0 collective-permute-done.11.refs_3_
  88.6 0.0 collective-permute-done.12.refs_4_
  88.6 0.0 copy-start.8
  88.7 2.3 %collective-permute-done.13.refs_5_ = bf16[2,8,16,128]{3,2,1,0:T(8,128)(2,1)S(1)} collective-permute-done((bf16[2,8,16,128]{3,2,1,0:T(8,128)(2,1)}, bf16[2,8,16,128]{3,2,1,0:T(8,128)(2,1)S(1)}, u32[]{:S(2)}, u32[]{:S(2)}) %collective-permute-start.13) | collective-permute-done | bytes 65568 | tf_op jit(solution)/shard_map/ppermute | solution.py:231
  91.0 3.8 %collective-permute-done.14.refs_6_ = bf16[2,8,16,128]{3,2,1,0:T(8,128)(2,1)S(1)} collective-permute-done((bf16[2,8,16,128]{3,2,1,0:T(8,128)(2,1)}, bf16[2,8,16,128]{3,2,1,0:T(8,128)(2,1)S(1)}, u32[]{:S(2)}, u32[]{:S(2)}) %collective-permute-start.14) | collective-permute-done | bytes 65568 | tf_op jit(solution)/shard_map/ppermute | solution.py:231
  94.8 0.0 collective-permute-done.15.refs_7_
  94.8 1.4 %all-to-all-done.1 = s32[256,1,2176]{2,1,0:T(1,128)S(1)} async-done(((s32[256,1,2176]{2,1,0:T(1,128)}), s32[256,1,2176]{2,1,0:T(1,128)S(1)}, u32[]{:S(2)}, u32[]{:S(2)}) %all-to-all-start.1) | async-done | bytes 2228256 | tf_op jit(solution)/shard_map/all_to_all | solution.py:225
  96.2 0.0 copy-done.5
  96.2 0.0 copy-done.6
  96.3 1.3 %copy-done.1 = s32[256,1,2176]{2,1,0:T(1,128)} copy-done((s32[256,1,2176]{2,1,0:T(1,128)}, s32[256,1,2176]{2,1,0:T(1,128)S(1)}, u32[]{:S(2)}) %copy-start.1) | copy-done | bytes 2228248
  97.6 14.2 %filter.1 = f32[2,8,128,512]{3,2,1,0:T(8,128)} custom-call(s32[2048]{0:T(1024)} %groups_ref.3, s32[2]{0:T(128)} %pad_add_fusion.place_ref, s32[16,272,128]{2,1,0:T(8,128)} %bitcast.11, bf16[8,2,512,256]{3,2,1,0:T(8,128)(2,1)} %bitcast.13, bf16[2,8,16,128]{3,2,1,0:T(8,128)(2,1)} %get-tuple-element.43.refs_0_, bf16[2,8,16,128]{3,2,1,0:T(8,128)(2,1)} %copy-done.5, ...), custom_call_target="tpu_custom_call" | custom-call | tf_op jit(solution)/shard_map/filter/pallas_call | solution.py:276
  (22 shorter events, 0.0 us)
Async XLA Ops:
  6.5 1.0 copy-start
  8.2 21.2 %all-to-all-start = ((bf16[16,32,256]{2,1,0:T(8,128)(2,1)}), bf16[16,32,256]{2,1,0:T(8,128)(2,1)S(1)}, u32[]{:S(2)}, u32[]{:S(2)}) async-start(bf16[16,32,256]{2,1,0:T(8,128)(2,1)} %broadcast_in_dim.8), calls=%async_computation | async-start | bytes 524288 | tf_op jit(solution)/shard_map/all_to_all | solution.py:204
  18.9 77.3 %all-gather.2.cloned.1.call-start = ((), (), s32[]{:S(2)}) async-start(), calls=%async_computation.2 | async-start | bytes 4456448 | tf_op jit(solution)/shard_map/all_gather | solution.py:223
  29.4 0.7 copy-start.2
  30.1 66.1 %all-to-all-start.1 = ((s32[256,1,2176]{2,1,0:T(1,128)}), s32[256,1,2176]{2,1,0:T(1,128)S(1)}, u32[]{:S(2)}, u32[]{:S(2)}) async-start(s32[256,1,2176]{2,1,0:T(1,128)} %bitcast.12), calls=%async_computation.1 | async-start | bytes 4456448 | tf_op jit(solution)/shard_map/all_to_all | solution.py:225
  43.2 1.6 %collective-permute-start = (bf16[8,4,16,128]{3,2,1,0:T(8,128)(2,1)}, bf16[8,4,16,128]{3,2,1,0:T(8,128)(2,1)S(1)}, u32[]{:S(2)}, u32[]{:S(2)}) collective-permute-start(bf16[8,4,16,128]{3,2,1,0:T(8,128)(2,1)} %get-tuple-element.32), channel_id=1, source_target_pairs={{0,16},{16,0},{32,48},{48,32},{64,80},{80,64},{96,112},{112,96},{1... | collective-permute-start | bytes 393224 | tf_op jit(solution)/shard_map/ppermute | solution.py:231
  44.8 0.6 copy-start.4
  47.1 5.8 %collective-permute-start.1 = (bf16[2,4,16,128]{3,2,1,0:T(8,128)(2,1)}, bf16[2,4,16,128]{3,2,1,0:T(8,128)(2,1)S(1)}, u32[]{:S(2)}, u32[]{:S(2)}) collective-permute-start(bf16[2,4,16,128]{3,2,1,0:T(8,128)(2,1)} %get-tuple-element.34), channel_id=1, source_target_pairs={{0,32},{16,48},{32,0},{48,16},{64,96},{80,112},{96,64},{112,80},{1... | collective-permute-start | bytes 98312 | tf_op jit(solution)/shard_map/ppermute | solution.py:231
  48.3 8.5 %collective-permute-start.2 = (bf16[2,4,16,128]{3,2,1,0:T(8,128)(2,1)}, bf16[2,4,16,128]{3,2,1,0:T(8,128)(2,1)S(1)}, u32[]{:S(2)}, u32[]{:S(2)}) collective-permute-start(bf16[2,4,16,128]{3,2,1,0:T(8,128)(2,1)} %get-tuple-element.35), channel_id=1, source_target_pairs={{0,64},{16,80},{32,96},{48,112},{64,0},{80,16},{96,32},{112,48},{1... | collective-permute-start | bytes 98312 | tf_op jit(solution)/shard_map/ppermute | solution.py:231
  50.8 7.8 %collective-permute-start.3 = (bf16[2,4,16,128]{3,2,1,0:T(8,128)(2,1)}, bf16[2,4,16,128]{3,2,1,0:T(8,128)(2,1)S(1)}, u32[]{:S(2)}, u32[]{:S(2)}) collective-permute-start(bf16[2,4,16,128]{3,2,1,0:T(8,128)(2,1)} %get-tuple-element.36), channel_id=1, source_target_pairs={{0,96},{16,112},{32,64},{48,80},{64,32},{80,48},{96,0},{112,16},{1... | collective-permute-start | bytes 98312 | tf_op jit(solution)/shard_map/ppermute | solution.py:231
  51.0 7.6 %collective-permute-start.4 = (bf16[2,4,16,128]{3,2,1,0:T(8,128)(2,1)}, bf16[2,4,16,128]{3,2,1,0:T(8,128)(2,1)S(1)}, u32[]{:S(2)}, u32[]{:S(2)}) collective-permute-start(bf16[2,4,16,128]{3,2,1,0:T(8,128)(2,1)} %get-tuple-element.37), channel_id=1, source_target_pairs={{0,128},{16,144},{32,160},{48,176},{64,192},{80,208},{96,224},{112... | collective-permute-start | bytes 98312 | tf_op jit(solution)/shard_map/ppermute | solution.py:231
  52.2 6.3 %collective-permute-start.5 = (bf16[2,4,16,128]{3,2,1,0:T(8,128)(2,1)}, bf16[2,4,16,128]{3,2,1,0:T(8,128)(2,1)S(1)}, u32[]{:S(2)}, u32[]{:S(2)}) collective-permute-start(bf16[2,4,16,128]{3,2,1,0:T(8,128)(2,1)} %get-tuple-element.38), channel_id=1, source_target_pairs={{0,160},{16,176},{32,128},{48,144},{64,224},{80,240},{96,192},{112... | collective-permute-start | bytes 98312 | tf_op jit(solution)/shard_map/ppermute | solution.py:231
  53.0 9.6 %copy-start.12 = (bf16[2,4,16,128]{3,2,1,0:T(8,128)(2,1)}, bf16[2,4,16,128]{3,2,1,0:T(8,128)(2,1)S(1)}, u32[]{:S(2)}) copy-start(bf16[2,4,16,128]{3,2,1,0:T(8,128)(2,1)S(1)} %collective-permute-done.1.refs_1_) | copy-start | bytes 98308
  53.0 9.6 %collective-permute-start.6 = (bf16[2,4,16,128]{3,2,1,0:T(8,128)(2,1)}, bf16[2,4,16,128]{3,2,1,0:T(8,128)(2,1)S(1)}, u32[]{:S(2)}, u32[]{:S(2)}) collective-permute-start(bf16[2,4,16,128]{3,2,1,0:T(8,128)(2,1)} %get-tuple-element.39), channel_id=1, source_target_pairs={{0,192},{16,208},{32,224},{48,240},{64,128},{80,144},{96,160},{112... | collective-permute-start | bytes 98312 | tf_op jit(solution)/shard_map/ppermute | solution.py:231
  56.8 5.8 %copy-start.13 = (bf16[2,4,16,128]{3,2,1,0:T(8,128)(2,1)}, bf16[2,4,16,128]{3,2,1,0:T(8,128)(2,1)S(1)}, u32[]{:S(2)}) copy-start(bf16[2,4,16,128]{3,2,1,0:T(8,128)(2,1)S(1)} %collective-permute-done.2.refs_2_) | copy-start | bytes 98308
  56.8 5.7 %collective-permute-start.7 = (bf16[2,4,16,128]{3,2,1,0:T(8,128)(2,1)}, bf16[2,4,16,128]{3,2,1,0:T(8,128)(2,1)S(1)}, u32[]{:S(2)}, u32[]{:S(2)}) collective-permute-start(bf16[2,4,16,128]{3,2,1,0:T(8,128)(2,1)} %get-tuple-element.40), channel_id=1, source_target_pairs={{0,224},{16,240},{32,192},{48,208},{64,160},{80,176},{96,128},{112... | collective-permute-start | bytes 98312 | tf_op jit(solution)/shard_map/ppermute | solution.py:231
  58.5 4.0 %copy-start.14 = (bf16[2,4,16,128]{3,2,1,0:T(8,128)(2,1)}, bf16[2,4,16,128]{3,2,1,0:T(8,128)(2,1)S(1)}, u32[]{:S(2)}) copy-start(bf16[2,4,16,128]{3,2,1,0:T(8,128)(2,1)S(1)} %collective-permute-done.3.refs_3_) | copy-start | bytes 98308
  58.5 4.0 %copy-start.15 = (bf16[2,4,16,128]{3,2,1,0:T(8,128)(2,1)}, bf16[2,4,16,128]{3,2,1,0:T(8,128)(2,1)S(1)}, u32[]{:S(2)}) copy-start(bf16[2,4,16,128]{3,2,1,0:T(8,128)(2,1)S(1)} %collective-permute-done.4.refs_4_) | copy-start | bytes 98308
  58.6 4.0 %copy-start.16 = (bf16[2,4,16,128]{3,2,1,0:T(8,128)(2,1)}, bf16[2,4,16,128]{3,2,1,0:T(8,128)(2,1)S(1)}, u32[]{:S(2)}) copy-start(bf16[2,4,16,128]{3,2,1,0:T(8,128)(2,1)S(1)} %collective-permute-done.5.refs_5_) | copy-start | bytes 98308
  62.5 0.6 copy-start.17
  62.6 0.6 copy-start.18
  66.4 4.9 %collective-permute-start.8 = (bf16[8,8,16,128]{3,2,1,0:T(8,128)(2,1)}, bf16[8,8,16,128]{3,2,1,0:T(8,128)(2,1)S(1)}, u32[]{:S(2)}, u32[]{:S(2)}) collective-permute-start(bf16[8,8,16,128]{3,2,1,0:T(8,128)(2,1)} %get-tuple-element.42), channel_id=1, source_target_pairs={{0,16},{16,0},{32,48},{48,32},{64,80},{80,64},{96,112},{112,96},{1... | collective-permute-start | bytes 786440 | tf_op jit(solution)/shard_map/ppermute | solution.py:231
  71.4 0.7 copy-start.3
  73.9 6.4 %collective-permute-start.9 = (bf16[2,8,16,128]{3,2,1,0:T(8,128)(2,1)}, bf16[2,8,16,128]{3,2,1,0:T(8,128)(2,1)S(1)}, u32[]{:S(2)}, u32[]{:S(2)}) collective-permute-start(bf16[2,8,16,128]{3,2,1,0:T(8,128)(2,1)} %get-tuple-element.44), channel_id=1, source_target_pairs={{0,32},{16,48},{32,0},{48,16},{64,96},{80,112},{96,64},{112,80},{1... | collective-permute-start | bytes 196616 | tf_op jit(solution)/shard_map/ppermute | solution.py:231
  73.9 12.5 %collective-permute-start.10 = (bf16[2,8,16,128]{3,2,1,0:T(8,128)(2,1)}, bf16[2,8,16,128]{3,2,1,0:T(8,128)(2,1)S(1)}, u32[]{:S(2)}, u32[]{:S(2)}) collective-permute-start(bf16[2,8,16,128]{3,2,1,0:T(8,128)(2,1)} %get-tuple-element.45), channel_id=1, source_target_pairs={{0,64},{16,80},{32,96},{48,112},{64,0},{80,16},{96,32},{112,48},{1... | collective-permute-start | bytes 196616 | tf_op jit(solution)/shard_map/ppermute | solution.py:231
  74.9 13.7 %collective-permute-start.11 = (bf16[2,8,16,128]{3,2,1,0:T(8,128)(2,1)}, bf16[2,8,16,128]{3,2,1,0:T(8,128)(2,1)S(1)}, u32[]{:S(2)}, u32[]{:S(2)}) collective-permute-start(bf16[2,8,16,128]{3,2,1,0:T(8,128)(2,1)} %get-tuple-element.46), channel_id=1, source_target_pairs={{0,96},{16,112},{32,64},{48,80},{64,32},{80,48},{96,0},{112,16},{1... | collective-permute-start | bytes 196616 | tf_op jit(solution)/shard_map/ppermute | solution.py:231
  77.8 10.9 %collective-permute-start.12 = (bf16[2,8,16,128]{3,2,1,0:T(8,128)(2,1)}, bf16[2,8,16,128]{3,2,1,0:T(8,128)(2,1)S(1)}, u32[]{:S(2)}, u32[]{:S(2)}) collective-permute-start(bf16[2,8,16,128]{3,2,1,0:T(8,128)(2,1)} %get-tuple-element.47), channel_id=1, source_target_pairs={{0,128},{16,144},{32,160},{48,176},{64,192},{80,208},{96,224},{112... | collective-permute-start | bytes 196616 | tf_op jit(solution)/shard_map/ppermute | solution.py:231
  78.0 12.9 %collective-permute-start.13 = (bf16[2,8,16,128]{3,2,1,0:T(8,128)(2,1)}, bf16[2,8,16,128]{3,2,1,0:T(8,128)(2,1)S(1)}, u32[]{:S(2)}, u32[]{:S(2)}) collective-permute-start(bf16[2,8,16,128]{3,2,1,0:T(8,128)(2,1)} %get-tuple-element.48), channel_id=1, source_target_pairs={{0,160},{16,176},{32,128},{48,144},{64,224},{80,240},{96,192},{112... | collective-permute-start | bytes 196616 | tf_op jit(solution)/shard_map/ppermute | solution.py:231
  80.3 15.9 %copy-start.5 = (bf16[2,8,16,128]{3,2,1,0:T(8,128)(2,1)}, bf16[2,8,16,128]{3,2,1,0:T(8,128)(2,1)S(1)}, u32[]{:S(2)}) copy-start(bf16[2,8,16,128]{3,2,1,0:T(8,128)(2,1)S(1)} %collective-permute-done.9.refs_1_) | copy-start | bytes 196612
  80.3 14.5 %collective-permute-start.14 = (bf16[2,8,16,128]{3,2,1,0:T(8,128)(2,1)}, bf16[2,8,16,128]{3,2,1,0:T(8,128)(2,1)S(1)}, u32[]{:S(2)}, u32[]{:S(2)}) collective-permute-start(bf16[2,8,16,128]{3,2,1,0:T(8,128)(2,1)} %get-tuple-element.49), channel_id=1, source_target_pairs={{0,192},{16,208},{32,224},{48,240},{64,128},{80,144},{96,160},{112... | collective-permute-start | bytes 196616 | tf_op jit(solution)/shard_map/ppermute | solution.py:231
  86.4 9.8 %copy-start.6 = (bf16[2,8,16,128]{3,2,1,0:T(8,128)(2,1)}, bf16[2,8,16,128]{3,2,1,0:T(8,128)(2,1)S(1)}, u32[]{:S(2)}) copy-start(bf16[2,8,16,128]{3,2,1,0:T(8,128)(2,1)S(1)} %collective-permute-done.10.refs_2_) | copy-start | bytes 196612
  86.4 8.4 %collective-permute-start.15 = (bf16[2,8,16,128]{3,2,1,0:T(8,128)(2,1)}, bf16[2,8,16,128]{3,2,1,0:T(8,128)(2,1)S(1)}, u32[]{:S(2)}, u32[]{:S(2)}) collective-permute-start(bf16[2,8,16,128]{3,2,1,0:T(8,128)(2,1)} %get-tuple-element.50), channel_id=1, source_target_pairs={{0,224},{16,240},{32,192},{48,208},{64,160},{80,176},{96,128},{112... | collective-permute-start | bytes 196616 | tf_op jit(solution)/shard_map/ppermute | solution.py:231
  88.6 7.6 %copy-start.7 = (bf16[2,8,16,128]{3,2,1,0:T(8,128)(2,1)}, bf16[2,8,16,128]{3,2,1,0:T(8,128)(2,1)S(1)}, u32[]{:S(2)}) copy-start(bf16[2,8,16,128]{3,2,1,0:T(8,128)(2,1)S(1)} %collective-permute-done.11.refs_3_) | copy-start | bytes 196612
  88.6 7.6 %copy-start.8 = (bf16[2,8,16,128]{3,2,1,0:T(8,128)(2,1)}, bf16[2,8,16,128]{3,2,1,0:T(8,128)(2,1)S(1)}, u32[]{:S(2)}) copy-start(bf16[2,8,16,128]{3,2,1,0:T(8,128)(2,1)S(1)} %collective-permute-done.12.refs_4_) | copy-start | bytes 196612
  91.0 5.3 %copy-start.9 = (bf16[2,8,16,128]{3,2,1,0:T(8,128)(2,1)}, bf16[2,8,16,128]{3,2,1,0:T(8,128)(2,1)S(1)}, u32[]{:S(2)}) copy-start(bf16[2,8,16,128]{3,2,1,0:T(8,128)(2,1)S(1)} %collective-permute-done.13.refs_5_) | copy-start | bytes 196612
  94.8 1.5 %copy-start.10 = (bf16[2,8,16,128]{3,2,1,0:T(8,128)(2,1)}, bf16[2,8,16,128]{3,2,1,0:T(8,128)(2,1)S(1)}, u32[]{:S(2)}) copy-start(bf16[2,8,16,128]{3,2,1,0:T(8,128)(2,1)S(1)} %collective-permute-done.14.refs_6_) | copy-start | bytes 196612
  94.8 1.5 %copy-start.11 = (bf16[2,8,16,128]{3,2,1,0:T(8,128)(2,1)}, bf16[2,8,16,128]{3,2,1,0:T(8,128)(2,1)S(1)}, u32[]{:S(2)}) copy-start(bf16[2,8,16,128]{3,2,1,0:T(8,128)(2,1)S(1)} %collective-permute-done.15.refs_7_) | copy-start | bytes 196612
  96.2 1.4 %copy-start.1 = (s32[256,1,2176]{2,1,0:T(1,128)}, s32[256,1,2176]{2,1,0:T(1,128)S(1)}, u32[]{:S(2)}) copy-start(s32[256,1,2176]{2,1,0:T(1,128)S(1)} %all-to-all-done.1) | copy-start | bytes 6684676
Sparse Core Ops, SparseCore 0:
  30.2 63.2 all-gather.1

commit v2 on v1

--- a/solution.py
+++ b/solution.py
@@ -11,7 +11,8 @@
 SUB = 8
 FULL = 32760.0
 MIDDLE = 32768.0
-VMEM = 56 * 1024 * 1024
+VMEM = 32 * 1024 * 1024
+FILTER_VMEM = 60 * 1024 * 1024
 CORES = 2
 
 
@@ -68,14 +69,13 @@
 
 
 def filter_kernel(groups_ref, place_ref, words_ref, delay_ref, *refs, rows, spread):
-    fringe_refs = refs[:-10]
-    out_ref, words, levels, samples, slabs, mats, delay, word_sems, slab_sems, delay_sems = refs[-10:]
-    baseline = pl.program_id(0)
-    baselines = pl.num_programs(0)
+    fringe_refs = refs[:-12]
+    out_ref, words, levels, samples, slabs, mats, delay, results, *sems = refs[-12:]
+    word_sems, slab_sems, delay_sems, out_sems = sems
+    baselines = delay.shape[0]
     blocks = words_ref.shape[0]
     chan_count = words_ref.shape[1] // rows
     quads = chan_count // 4
-    slot = lax.rem(baseline, 2)
 
     def fetch_words(block):
         return pltpu.make_async_copy(words_ref.at[block], words.at[block], word_sems.at[block])
@@ -83,24 +83,30 @@
     def fetch_slabs(chip):
         return pltpu.make_async_copy(fringe_refs[chip], slabs.at[chip], slab_sems.at[chip])
 
-    def fetch_delay(number, to):
-        mine = (place_ref[0] * chan_count + place_ref[1]) * baselines + number
+    def fetch_delay(baseline, piece):
+        mine = (place_ref[0] * chan_count + place_ref[1]) * baselines + baseline
         group = groups_ref[mine] // spread
-        return pltpu.make_async_copy(delay_ref.at[group], delay.at[to], delay_sems.at[to])
-
-    @pl.when(baseline == 0)
+        return pltpu.make_async_copy(
+            delay_ref.at[group, piece], delay.at[baseline, piece], delay_sems.at[baseline, piece]
+        )
+
+    def send_out(baseline, slot, part):
+        return pltpu.make_async_copy(
+            results.at[slot, part], out_ref.at[part, baseline], out_sems.at[slot, part]
+        )
+
     def unpack():
         for block in range(blocks):
             fetch_words(block).start()
         for chip in range(len(fringe_refs)):
             fetch_slabs(chip).start()
-        fetch_delay(0, 0).start()
         lane = lax.broadcasted_iota(jnp.int32, (SUB, LANES), 1)
         low_half = lane < 64
         even_group = (lane & 32) == 0
         group = lane // 32
-        for block in range(blocks):
+        def unpack_block(block, carry):
             fetch_words(block).wait()
+            fetch_delay(block // delay.shape[1], lax.rem(block, delay.shape[1])).start()
             level = words[block, pl.ds(rows - 1, chan_count, stride=rows), :].astype(jnp.float32)
             scales = jnp.exp2(level * 0.25) * (1.0 / FULL)
             scales = jnp.concatenate([scales, jnp.zeros((LANES - chan_count, LANES), jnp.float32)], axis=0)
@@ -130,55 +136,78 @@
                         jnp.where(even_group, pltpu.roll(a2, 96, 1), a3),
                     )
                     for step, word in enumerate(turned):
-                        at = (block * 8 + half * 4 + step) * SUB
+                        at = pl.ds(pl.multiple_of((block * 8 + half * 4 + step) * SUB, SUB), SUB)
                         real = (word & 0xFFFF).astype(jnp.float32) * scale + offset
                         imag = lax.shift_right_logical(word, 16).astype(jnp.float32) * scale + offset
-                        samples[0, quad, at : at + SUB, :] = real
-                        samples[1, quad, at : at + SUB, :] = imag
+                        samples[0, quad, at, :] = real
+                        samples[1, quad, at, :] = imag
+            return carry
+
+        lax.fori_loop(0, blocks, unpack_block, 0)
         for chip in range(len(fringe_refs)):
             fetch_slabs(chip).wait()
 
-    @pl.when(baseline + 1 < baselines)
-    def ahead():
-        fetch_delay(baseline + 1, 1 - slot).start()
-
+    unpack()
     count = samples.shape[2] // SUB
-    parts = []
-    for part in range(2):
-        parts.append(
-            jnp.concatenate(
-                [samples[part, quad, pl.ds(baseline, count, stride=SUB), :] for quad in range(quads)], axis=1
+
+    def over_time(baseline):
+        parts = []
+        for part in range(2):
+            parts.append(
+                jnp.concatenate(
+                    [samples[part, quad, pl.ds(baseline, count, stride=SUB), :] for quad in range(quads)], axis=1
+                )
             )
+        data = jnp.concatenate(parts, axis=0)
+        high = data.astype(jnp.bfloat16)
+        low = (data - high.astype(jnp.float32)).astype(jnp.bfloat16)
+        for chip in range(len(fringe_refs)):
+            for core in range(CORES):
+                mats[place_ref[0] ^ (chip * CORES + core)] = slabs[chip, core, baseline]
+        whole = mats[...].reshape(2 * count, count)
+        real, imag = whole[:count], whole[count:]
+        both = jnp.concatenate(
+            [jnp.concatenate([real, -imag], axis=1), jnp.concatenate([imag, real], axis=1)], axis=0
         )
-    data = jnp.concatenate(parts, axis=0)
-    high = data.astype(jnp.bfloat16)
-    low = (data - high.astype(jnp.float32)).astype(jnp.bfloat16)
-    for chip in range(len(fringe_refs)):
-        for core in range(CORES):
-            mats[place_ref[0] ^ (chip * CORES + core)] = slabs[chip, core, baseline]
-    whole = mats[...].reshape(2 * count, count)
-    real, imag = whole[:count], whole[count:]
-    both = jnp.concatenate(
-        [jnp.concatenate([real, -imag], axis=1), jnp.concatenate([imag, real], axis=1)], axis=0
-    )
-    rated = jnp.dot(both, high, preferred_element_type=jnp.float32) + jnp.dot(
-        both, low, preferred_element_type=jnp.float32
-    )
-    high = rated.astype(jnp.bfloat16)
-    low = (rated - high.astype(jnp.float32)).astype(jnp.bfloat16)
-    fetch_delay(baseline, slot).wait()
-    both = jnp.concatenate([high, low], axis=0)
-    wide = delay.shape[3]
-    total = None
-    for piece in range(delay.shape[1]):
-        term = lax.dot_general(
-            both[:, piece * wide : (piece + 1) * wide],
-            delay[slot, piece],
-            (((1,), (1,)), ((), ())),
-            preferred_element_type=jnp.float32,
+        rated = jnp.dot(both, high, preferred_element_type=jnp.float32) + jnp.dot(
+            both, low, preferred_element_type=jnp.float32
         )
-        total = term if total is None else total + term
-    out_ref[...] = (total[: 2 * count] + total[2 * count :]).reshape(out_ref.shape)
+        high = rated.astype(jnp.bfloat16)
+        low = (rated - high.astype(jnp.float32)).astype(jnp.bfloat16)
+        return jnp.concatenate([high, low], axis=0)
+
+    def over_channels(baseline, both):
+        slot = baseline % results.shape[0]
+        wide = delay.shape[3]
+        for piece in range(delay.shape[1]):
+            fetch_delay(baseline, piece).wait()
+        if baseline >= results.shape[0]:
+            for part in range(2):
+                send_out(baseline, slot, part).wait()
+        for part in range(2):
+            rowsel = jnp.concatenate(
+                [both[part * count : (part + 1) * count], both[(2 + part) * count : (3 + part) * count]], axis=0
+            )
+            total = None
+            for piece in range(delay.shape[1]):
+                term = lax.dot_general(
+                    rowsel[:, piece * wide : (piece + 1) * wide],
+                    delay[baseline, piece],
+                    (((1,), (1,)), ((), ())),
+                    preferred_element_type=jnp.float32,
+                )
+                total = term if total is None else total + term
+            results[slot, part] = total[:count] + total[count:]
+            send_out(baseline, slot, part).start()
+
+    ready = over_time(0)
+    for baseline in range(baselines):
+        following = over_time(baseline + 1) if baseline + 1 < baselines else None
+        over_channels(baseline, ready)
+        ready = following
+    for baseline in range(baselines - results.shape[0], baselines):
+        for part in range(2):
+            send_out(baseline, baseline % results.shape[0], part).wait()
 
 
 def shards(visibility, groups, flags, fringe, delay):
@@ -277,23 +306,25 @@
         functools.partial(filter_kernel, rows=rows, spread=spread),
         grid_spec=pltpu.PrefetchScalarGridSpec(
             num_scalar_prefetch=2,
-            grid=(own,),
-            in_specs=[pl.BlockSpec(memory_space=pl.ANY)] * (2 + chips),
-            out_specs=pl.BlockSpec((2, 1, all_times, all_chans), lambda n, *_: (0, n, 0, 0)),
+            grid=(),
+            in_specs=[pl.BlockSpec(memory_space=pltpu.HBM)] * 2 + [pl.BlockSpec(memory_space=pl.ANY)] * chips,
+            out_specs=pl.BlockSpec(memory_space=pl.ANY),
             scratch_shapes=[
                 pltpu.VMEM((time_count, chan_count * rows, LANES), jnp.int32),
                 pltpu.VMEM((LANES, LANES), jnp.float32),
                 pltpu.VMEM((2, all_chans // LANES, all_times * SUB, LANES), jnp.float32),
                 pltpu.VMEM((chips, CORES, own, slab, all_times), jnp.bfloat16),
                 pltpu.VMEM((time_count, slab, all_times), jnp.bfloat16),
-                pltpu.VMEM((2, pieces, all_chans, wide), jnp.bfloat16),
+                pltpu.VMEM((own, pieces, all_chans, wide), jnp.bfloat16),
+                pltpu.VMEM((4, 2, all_times, all_chans), jnp.float32),
                 pltpu.SemaphoreType.DMA((time_count,)),
                 pltpu.SemaphoreType.DMA((chips,)),
-                pltpu.SemaphoreType.DMA((2,)),
+                pltpu.SemaphoreType.DMA((own, pieces)),
+                pltpu.SemaphoreType.DMA((4, 2)),
             ],
         ),
         out_shape=jax.ShapeDtypeStruct((2, own, all_times, all_chans), jnp.float32),
-        compiler_params=params(),
+        compiler_params=pltpu.CompilerParams(vmem_limit_bytes=FILTER_VMEM),
         name="filter",
     )(groups, place, words, delay_all, *mats)
 

time: 120 us -> 118 us (0.983); the launches traced: 119 us -> 118 us
  Pallas kernels: 30.2 us -> 19.3 us
  waiting for transfers between devices: 24 us -> 30.5 us
  starting transfers between devices: 44.5 us -> 46.9 us
  local copies, waits for them, and re-layouts: 5.69 us -> 7.5 us
    all_to_all x1, waiting for transfers between devices: 1.44 us -> 7.21 us  [shards(): lax.all_to_all(packed.reshape(devices, 1, rows * LANES), everyone, split_...]
    pallas_call x2, Pallas kernels: 3.54 us -> 0.05 us  [exchanged(): pl.pallas_call(regroup_kernel, in_specs=[inside] * CORES, out_specs=[insi...]
    pallas_call x1, Pallas kernels: 6.84 us -> 4.17 us  [shards(): pl.pallas_call(functools.partial(pack_kernel, rows=rows), grid=(total //...]
    ppermute x16, starting transfers between devices: 23.8 us -> 25.7 us  [crossed(): lax.ppermute(array, 'tm', [(k, k ^ mask) for k in range(time_count)])]
    unnamed x38 -> x32, local copies, waits for them, and re-layouts: 4.96 us -> 6.78 us
    pallas_call x1, Pallas kernels: 3.27 us -> 1.48 us  [shards(): pl.pallas_call(select_kernel, grid_spec=pltpu.PrefetchScalarGridSpec(num_...]
    pallas_call x1, Pallas kernels: 2.38 us -> 0.64 us  [shards(): pl.pallas_call(shares_kernel, grid_spec=pltpu.PrefetchScalarGridSpec(num_...]
    pallas_call x1, Pallas kernels: 14.2 us -> 12.9 us  [shards(): pl.pallas_call(functools.partial(filter_kernel, rows=rows, spread=spread)...]
  transfers between devices with their start and end apart: 19 -> 19, of which waited for: 10 -> 12; matrix products, arithmetic and copies ran while one was open for 1% -> 0% of each run, Pallas kernels for 14% -> 5%
where the time goes in v2:
time: 118 us
  starting transfers between devices  46.9 us (40%)
  waiting for transfers between devices  30.5 us (26%)
  Pallas kernels  19.3 us (16%)
  between operations  13.6 us (12%)
  local copies, waits for them, and re-layouts  7.5 us (6%)
    ppermute x16, starting transfers between devices, crossed(): lax.ppermute(array, 'tm', [(k, k ^ mask) for k in range(time_count)])  25.7 us
    ppermute x16, waiting for transfers between devices, crossed(): lax.ppermute(array, 'tm', [(k, k ^ mask) for k in range(time_count)])  20.2 us
    pallas_call x1, Pallas kernels, shards(): pl.pallas_call(functools.partial(filter_kernel, rows=rows, spread=spread)...  12.9 us
    all_to_all x1, starting transfers between devices, shards(): lax.all_to_all(jnp.broadcast_to(share, (chan_count, chans, wide)), 'chan'...  10.7 us
    all_to_all x1, starting transfers between devices, shards(): lax.all_to_all(packed.reshape(devices, 1, rows * LANES), everyone, split_...  10.5 us
    all_to_all x1, waiting for transfers between devices, shards(): lax.all_to_all(packed.reshape(devices, 1, rows * LANES), everyone, split_...  7.21 us
    unnamed x32, local copies, waits for them, and re-layouts  6.78 us
    pallas_call x1, Pallas kernels, shards(): pl.pallas_call(functools.partial(pack_kernel, rows=rows), grid=(total //...  4.17 us
  transfers between devices with their start and end apart: 19, of which 12 were waited for; matrix products, arithmetic and copies ran while one was open for 0% of the time, Pallas kernels for 5%

profile of v2, /device:TPU:33, one launch (start us, length us, event | category | flops | bytes accessed | tf_op | source)
XLA Modules:
  0.0 117.9 jit_solution(14550490625115017146)
XLA Ops:
  6.5 0.0 copy-start
  6.5 0.9 copy-done
  7.5 0.7 broadcast_in_dim.8
  8.2 10.7 %all-to-all-start = ((bf16[16,32,256]{2,1,0:T(8,128)(2,1)}), bf16[16,32,256]{2,1,0:T(8,128)(2,1)S(1)}, u32[]{:S(2)}, u32[]{:S(2)}) async-start(bf16[16,32,256]{2,1,0:T(8,128)(2,1)} %broadcast_in_dim.8), calls=%async_computation | async-start | bytes 524288 | tf_op jit(solution)/shard_map/all_to_all | solution.py:233
  18.9 0.0 all-gather.2.cloned.1.call-start
  18.9 0.0 copy-start.1
  18.9 2.2 %copy-done.1 = f32[2,2048,8,32]{1,3,2,0:T(8,128)S(1)} copy-done((f32[2,2048,8,32]{1,3,2,0:T(8,128)S(1)}, f32[2,2048,8,32]{1,3,2,0:T(8,128)}, u32[]{:S(2)}) %copy-start.1) | copy-done | bytes 4194328
  21.1 0.9 copy-done.2
  22.1 4.2 %pack.1 = s32[4352,128]{1,0:T(8,128)} custom-call(f32[2,8,32,2048]{3,2,1,0:T(8,128)S(1)} %bitcast.11, s32[32,2048]{1,0:T(8,128)S(1)} %bitcast.12), custom_call_target="tpu_custom_call" | custom-call | tf_op jit(solution)/shard_map/pack/pallas_call | solution.py:239
  26.2 3.1 %all-to-all-done = bf16[16,32,256]{2,1,0:T(8,128)(2,1)S(1)} async-done(((bf16[16,32,256]{2,1,0:T(8,128)(2,1)}), bf16[16,32,256]{2,1,0:T(8,128)(2,1)S(1)}, u32[]{:S(2)}, u32[]{:S(2)}) %all-to-all-start) | async-done | bytes 262176 | tf_op jit(solution)/shard_map/all_to_all | solution.py:233
  29.4 0.7 copy-done.8
  30.1 0.0 all-gather.2.cloned.1.call-update
  30.1 10.5 %all-to-all-start.1 = ((s32[256,1,2176]{2,1,0:T(1,128)}), s32[256,1,2176]{2,1,0:T(1,128)S(1)}, u32[]{:S(2)}, u32[]{:S(2)}) async-start(s32[256,1,2176]{2,1,0:T(1,128)} %bitcast.5), calls=%async_computation.1 | async-start | bytes 4456448 | tf_op jit(solution)/shard_map/all_to_all | solution.py:254
  40.7 0.1 pad_add_fusion.place_ref
  40.7 0.0 copy-done.3
  40.7 0.6 shares.1
  41.4 0.4 collective-permute-start
  41.8 1.0 collective-permute-done.refs_1_
  42.9 1.3 %collective-permute-start.1 = (bf16[2,4,16,128]{3,2,1,0:T(8,128)(2,1)S(1)}, bf16[2,4,16,128]{3,2,1,0:T(8,128)(2,1)S(1)}, u32[]{:S(2)}, u32[]{:S(2)}) collective-permute-start(bf16[2,4,16,128]{3,2,1,0:T(8,128)(2,1)S(1)} %get-tuple-element.34), channel_id=1, source_target_pairs={{0,32},{16,48},{32,0},{48,16},{64,96},{80,112},{96,64},{112,80},{1... | collective-permute-start | bytes 98312 | tf_op jit(solution)/shard_map/ppermute | solution.py:260
  44.1 2.4 %collective-permute-start.2 = (bf16[2,4,16,128]{3,2,1,0:T(8,128)(2,1)S(1)}, bf16[2,4,16,128]{3,2,1,0:T(8,128)(2,1)S(1)}, u32[]{:S(2)}, u32[]{:S(2)}) collective-permute-start(bf16[2,4,16,128]{3,2,1,0:T(8,128)(2,1)S(1)} %get-tuple-element.35), channel_id=1, source_target_pairs={{0,64},{16,80},{32,96},{48,112},{64,0},{80,16},{96,32},{112,48},{1... | collective-permute-start | bytes 98312 | tf_op jit(solution)/shard_map/ppermute | solution.py:260
  46.6 0.2 collective-permute-start.3
  46.8 1.2 %collective-permute-start.4 = (bf16[2,4,16,128]{3,2,1,0:T(8,128)(2,1)S(1)}, bf16[2,4,16,128]{3,2,1,0:T(8,128)(2,1)S(1)}, u32[]{:S(2)}, u32[]{:S(2)}) collective-permute-start(bf16[2,4,16,128]{3,2,1,0:T(8,128)(2,1)S(1)} %get-tuple-element.37), channel_id=1, source_target_pairs={{0,128},{16,144},{32,160},{48,176},{64,192},{80,208},{96,224},{112... | collective-permute-start | bytes 98312 | tf_op jit(solution)/shard_map/ppermute | solution.py:260
  48.1 0.0 collective-permute-start.5
  48.1 1.5 %collective-permute-done.1.refs_1_ = bf16[2,4,16,128]{3,2,1,0:T(8,128)(2,1)S(1)} collective-permute-done((bf16[2,4,16,128]{3,2,1,0:T(8,128)(2,1)S(1)}, bf16[2,4,16,128]{3,2,1,0:T(8,128)(2,1)S(1)}, u32[]{:S(2)}, u32[]{:S(2)}) %collective-permute-start.1) | collective-permute-done | bytes 32800 | tf_op jit(solution)/shard_map/ppermute | solution.py:260
  49.5 3.5 %collective-permute-start.6 = (bf16[2,4,16,128]{3,2,1,0:T(8,128)(2,1)S(1)}, bf16[2,4,16,128]{3,2,1,0:T(8,128)(2,1)S(1)}, u32[]{:S(2)}, u32[]{:S(2)}) collective-permute-start(bf16[2,4,16,128]{3,2,1,0:T(8,128)(2,1)S(1)} %get-tuple-element.39), channel_id=1, source_target_pairs={{0,192},{16,208},{32,224},{48,240},{64,128},{80,144},{96,160},{112... | collective-permute-start | bytes 98312 | tf_op jit(solution)/shard_map/ppermute | solution.py:260
  53.0 2.1 %collective-permute-done.2.refs_2_ = bf16[2,4,16,128]{3,2,1,0:T(8,128)(2,1)S(1)} collective-permute-done((bf16[2,4,16,128]{3,2,1,0:T(8,128)(2,1)S(1)}, bf16[2,4,16,128]{3,2,1,0:T(8,128)(2,1)S(1)}, u32[]{:S(2)}, u32[]{:S(2)}) %collective-permute-start.2) | collective-permute-done | bytes 32800 | tf_op jit(solution)/shard_map/ppermute | solution.py:260
  55.1 1.1 collective-permute-start.7
  56.2 0.0 collective-permute-done.3.refs_3_
  56.2 0.0 collective-permute-done.4.refs_4_
  56.2 0.0 collective-permute-done.5.refs_5_
  56.2 4.1 %collective-permute-done.6.refs_6_ = bf16[2,4,16,128]{3,2,1,0:T(8,128)(2,1)S(1)} collective-permute-done((bf16[2,4,16,128]{3,2,1,0:T(8,128)(2,1)S(1)}, bf16[2,4,16,128]{3,2,1,0:T(8,128)(2,1)S(1)}, u32[]{:S(2)}, u32[]{:S(2)}) %collective-permute-start.6) | collective-permute-done | bytes 32800 | tf_op jit(solution)/shard_map/ppermute | solution.py:260
  60.3 0.3 collective-permute-done.7.refs_7_
  60.6 0.0 copy-done.5
  60.6 1.5 %select.7 = (bf16[8,8,16,128]{3,2,1,0:T(8,128)(2,1)S(1)}, bf16[8,8,16,128]{3,2,1,0:T(8,128)(2,1)S(1)}) custom-call(s32[2048]{0:T(1024)S(1)} %copy-done.5, s32[2]{0:T(128)S(1)} %pad_add_fusion.place_ref, bf16[2,4,16,128]{3,2,1,0:T(8,128)(2,1)S(1)} %get-tuple-element.33.refs_0_, bf16[2,4,16,128]{3,2,1,0:T(8,128)(2,1)S(1)} %collective-permute-done.1.refs_1_, ...), custom_call_target="tpu_custom_call" | custom-call | tf_op jit(solution)/shard_map/select/pallas_call | solution.py:288
  62.1 3.0 %collective-permute-start.8 = (bf16[8,8,16,128]{3,2,1,0:T(8,128)(2,1)S(1)}, bf16[8,8,16,128]{3,2,1,0:T(8,128)(2,1)S(1)}, u32[]{:S(2)}, u32[]{:S(2)}) collective-permute-start(bf16[8,8,16,128]{3,2,1,0:T(8,128)(2,1)S(1)} %get-tuple-element.42), channel_id=1, source_target_pairs={{0,16},{16,0},{32,48},{48,32},{64,80},{80,64},{96,112},{112,96},{1... | collective-permute-start | bytes 786440 | tf_op jit(solution)/shard_map/ppermute | solution.py:260
  65.1 1.2 collective-permute-done.8.refs_1_
  66.3 0.0 copy-start.4
  66.3 0.6 copy-done.4
  66.9 1.2 %collective-permute-start.9 = (bf16[2,8,16,128]{3,2,1,0:T(8,128)(2,1)S(1)}, bf16[2,8,16,128]{3,2,1,0:T(8,128)(2,1)S(1)}, u32[]{:S(2)}, u32[]{:S(2)}) collective-permute-start(bf16[2,8,16,128]{3,2,1,0:T(8,128)(2,1)S(1)} %get-tuple-element.44), channel_id=1, source_target_pairs={{0,32},{16,48},{32,0},{48,16},{64,96},{80,112},{96,64},{112,80},{1... | collective-permute-start | bytes 196616 | tf_op jit(solution)/shard_map/ppermute | solution.py:260
  68.2 1.0 collective-permute-start.10
  69.2 1.6 %collective-permute-start.11 = (bf16[2,8,16,128]{3,2,1,0:T(8,128)(2,1)S(1)}, bf16[2,8,16,128]{3,2,1,0:T(8,128)(2,1)S(1)}, u32[]{:S(2)}, u32[]{:S(2)}) collective-permute-start(bf16[2,8,16,128]{3,2,1,0:T(8,128)(2,1)S(1)} %get-tuple-element.46), channel_id=1, source_target_pairs={{0,96},{16,112},{32,64},{48,80},{64,32},{80,48},{96,0},{112,16},{1... | collective-permute-start | bytes 196616 | tf_op jit(solution)/shard_map/ppermute | solution.py:260
  70.8 1.6 %collective-permute-start.12 = (bf16[2,8,16,128]{3,2,1,0:T(8,128)(2,1)S(1)}, bf16[2,8,16,128]{3,2,1,0:T(8,128)(2,1)S(1)}, u32[]{:S(2)}, u32[]{:S(2)}) collective-permute-start(bf16[2,8,16,128]{3,2,1,0:T(8,128)(2,1)S(1)} %get-tuple-element.47), channel_id=1, source_target_pairs={{0,128},{16,144},{32,160},{48,176},{64,192},{80,208},{96,224},{112... | collective-permute-start | bytes 196616 | tf_op jit(solution)/shard_map/ppermute | solution.py:260
  72.4 0.0 collective-permute-start.13
  72.4 2.5 %collective-permute-done.9.refs_1_ = bf16[2,8,16,128]{3,2,1,0:T(8,128)(2,1)S(1)} collective-permute-done((bf16[2,8,16,128]{3,2,1,0:T(8,128)(2,1)S(1)}, bf16[2,8,16,128]{3,2,1,0:T(8,128)(2,1)S(1)}, u32[]{:S(2)}, u32[]{:S(2)}) %collective-permute-start.9) | collective-permute-done | bytes 65568 | tf_op jit(solution)/shard_map/ppermute | solution.py:260
  74.9 2.3 %collective-permute-start.14 = (bf16[2,8,16,128]{3,2,1,0:T(8,128)(2,1)S(1)}, bf16[2,8,16,128]{3,2,1,0:T(8,128)(2,1)S(1)}, u32[]{:S(2)}, u32[]{:S(2)}) collective-permute-start(bf16[2,8,16,128]{3,2,1,0:T(8,128)(2,1)S(1)} %get-tuple-element.49), channel_id=1, source_target_pairs={{0,192},{16,208},{32,224},{48,240},{64,128},{80,144},{96,160},{112... | collective-permute-start | bytes 196616 | tf_op jit(solution)/shard_map/ppermute | solution.py:260
  77.2 1.3 %collective-permute-done.10.refs_2_ = bf16[2,8,16,128]{3,2,1,0:T(8,128)(2,1)S(1)} collective-permute-done((bf16[2,8,16,128]{3,2,1,0:T(8,128)(2,1)S(1)}, bf16[2,8,16,128]{3,2,1,0:T(8,128)(2,1)S(1)}, u32[]{:S(2)}, u32[]{:S(2)}) %collective-permute-start.10) | collective-permute-done | bytes 65568 | tf_op jit(solution)/shard_map/ppermute | solution.py:260
  78.5 4.7 %collective-permute-start.15 = (bf16[2,8,16,128]{3,2,1,0:T(8,128)(2,1)S(1)}, bf16[2,8,16,128]{3,2,1,0:T(8,128)(2,1)S(1)}, u32[]{:S(2)}, u32[]{:S(2)}) collective-permute-start(bf16[2,8,16,128]{3,2,1,0:T(8,128)(2,1)S(1)} %get-tuple-element.50), channel_id=1, source_target_pairs={{0,224},{16,240},{32,192},{48,208},{64,160},{80,176},{96,128},{112... | collective-permute-start | bytes 196616 | tf_op jit(solution)/shard_map/ppermute | solution.py:260
  83.2 0.0 collective-permute-done.11.refs_3_
  83.2 0.0 collective-permute-done.12.refs_4_
  83.2 0.0 copy-start.12
  83.2 2.8 %collective-permute-done.13.refs_5_ = bf16[2,8,16,128]{3,2,1,0:T(8,128)(2,1)S(1)} collective-permute-done((bf16[2,8,16,128]{3,2,1,0:T(8,128)(2,1)S(1)}, bf16[2,8,16,128]{3,2,1,0:T(8,128)(2,1)S(1)}, u32[]{:S(2)}, u32[]{:S(2)}) %collective-permute-start.13) | collective-permute-done | bytes 65568 | tf_op jit(solution)/shard_map/ppermute | solution.py:260
  86.0 3.5 %collective-permute-done.14.refs_6_ = bf16[2,8,16,128]{3,2,1,0:T(8,128)(2,1)S(1)} collective-permute-done((bf16[2,8,16,128]{3,2,1,0:T(8,128)(2,1)S(1)}, bf16[2,8,16,128]{3,2,1,0:T(8,128)(2,1)S(1)}, u32[]{:S(2)}, u32[]{:S(2)}) %collective-permute-start.14) | collective-permute-done | bytes 65568 | tf_op jit(solution)/shard_map/ppermute | solution.py:260
  89.5 0.0 collective-permute-done.15.refs_7_
  89.5 7.2 %all-to-all-done.1 = s32[256,1,2176]{2,1,0:T(1,128)S(1)} async-done(((s32[256,1,2176]{2,1,0:T(1,128)}), s32[256,1,2176]{2,1,0:T(1,128)S(1)}, u32[]{:S(2)}, u32[]{:S(2)}) %all-to-all-start.1) | async-done | bytes 2228256 | tf_op jit(solution)/shard_map/all_to_all | solution.py:254
  96.7 0.0 copy-done.6
  96.7 0.0 copy-done.9
  96.7 0.0 copy-done.10
  96.7 0.0 copy-done.11
  96.7 0.0 copy-done.12
  96.8 0.0 copy-done.13
  96.8 0.0 copy-done.14
  96.8 0.0 copy-done.15
  96.8 1.3 %copy-done.7 = s32[256,1,2176]{2,1,0:T(1,128)} copy-done((s32[256,1,2176]{2,1,0:T(1,128)}, s32[256,1,2176]{2,1,0:T(1,128)S(1)}, u32[]{:S(2)}) %copy-start.7) | copy-done | bytes 2228248
  98.1 12.9 %filter.1 = f32[2,8,128,512]{3,2,1,0:T(8,128)} custom-call(s32[2048]{0:T(1024)} %groups_ref.3, s32[2]{0:T(128)} %copy-done.6, s32[16,272,128]{2,1,0:T(8,128)} %bitcast.14, bf16[8,2,512,256]{3,2,1,0:T(8,128)(2,1)} %bitcast.15, bf16[2,8,16,128]{3,2,1,0:T(8,128)(2,1)} %copy-done.4, bf16[2,8,16,128]{3,2,1,0:T(8,128)(2,1)} %copy-done.9, ...), custom_call_target="tpu_custom_call" | custom-call | tf_op jit(solution)/shard_map/filter/pallas_call | solution.py:305
  (16 shorter events, 0.1 us)
Async XLA Ops:
  6.5 1.0 copy-start
  8.2 21.2 %all-to-all-start = ((bf16[16,32,256]{2,1,0:T(8,128)(2,1)}), bf16[16,32,256]{2,1,0:T(8,128)(2,1)S(1)}, u32[]{:S(2)}, u32[]{:S(2)}) async-start(bf16[16,32,256]{2,1,0:T(8,128)(2,1)} %broadcast_in_dim.8), calls=%async_computation | async-start | bytes 524288 | tf_op jit(solution)/shard_map/all_to_all | solution.py:233
  18.9 77.8 %all-gather.2.cloned.1.call-start = ((), (), s32[]{:S(2)}) async-start(), calls=%async_computation.2 | async-start | bytes 4456448 | tf_op jit(solution)/shard_map/all_gather | solution.py:252
  18.9 2.2 %copy-start.1 = (f32[2,2048,8,32]{1,3,2,0:T(8,128)S(1)}, f32[2,2048,8,32]{1,3,2,0:T(8,128)}, u32[]{:S(2)}) copy-start(f32[2,2048,8,32]{1,3,2,0:T(8,128)} %param.5) | copy-start | bytes 12582916
  21.1 0.9 copy-start.2
  22.1 18.7 %copy-start.3 = (bf16[2,4,128,128]{3,2,1,0:T(8,128)(2,1)S(1)}, bf16[2,4,128,128]{3,2,1,0:T(8,128)(2,1)}, u32[]{:S(2)}) copy-start(bf16[2,4,128,128]{3,2,1,0:T(8,128)(2,1)} %param.8) | copy-start | bytes 786436
  26.2 34.4 %copy-start.5 = (s32[2048]{0:T(1024)S(1)}, s32[2048]{0:T(1024)}, u32[]{:S(2)}) copy-start(s32[2048]{0:T(1024)} %groups_ref.3) | copy-start | bytes 24580
  29.4 0.7 copy-start.8
  30.1 66.6 %all-to-all-start.1 = ((s32[256,1,2176]{2,1,0:T(1,128)}), s32[256,1,2176]{2,1,0:T(1,128)S(1)}, u32[]{:S(2)}, u32[]{:S(2)}) async-start(s32[256,1,2176]{2,1,0:T(1,128)} %bitcast.5), calls=%async_computation.1 | async-start | bytes 4456448 | tf_op jit(solution)/shard_map/all_to_all | solution.py:254
  40.7 56.0 %copy-start.6 = (s32[2]{0:T(128)}, s32[2]{0:T(128)S(1)}, u32[]{:S(2)}) copy-start(s32[2]{0:T(128)S(1)} %pad_add_fusion.place_ref) | copy-start | bytes 28
  41.4 1.4 %collective-permute-start = (bf16[8,4,16,128]{3,2,1,0:T(8,128)(2,1)S(1)}, bf16[8,4,16,128]{3,2,1,0:T(8,128)(2,1)S(1)}, u32[]{:S(2)}, u32[]{:S(2)}) collective-permute-start(bf16[8,4,16,128]{3,2,1,0:T(8,128)(2,1)S(1)} %get-tuple-element.32), channel_id=1, source_target_pairs={{0,16},{16,0},{32,48},{48,32},{64,80},{80,64},{96,112},{112,96},{1... | collective-permute-start | bytes 393224 | tf_op jit(solution)/shard_map/ppermute | solution.py:260
  42.9 6.7 %collective-permute-start.1 = (bf16[2,4,16,128]{3,2,1,0:T(8,128)(2,1)S(1)}, bf16[2,4,16,128]{3,2,1,0:T(8,128)(2,1)S(1)}, u32[]{:S(2)}, u32[]{:S(2)}) collective-permute-start(bf16[2,4,16,128]{3,2,1,0:T(8,128)(2,1)S(1)} %get-tuple-element.34), channel_id=1, source_target_pairs={{0,32},{16,48},{32,0},{48,16},{64,96},{80,112},{96,64},{112,80},{1... | collective-permute-start | bytes 98312 | tf_op jit(solution)/shard_map/ppermute | solution.py:260
  44.1 11.0 %collective-permute-start.2 = (bf16[2,4,16,128]{3,2,1,0:T(8,128)(2,1)S(1)}, bf16[2,4,16,128]{3,2,1,0:T(8,128)(2,1)S(1)}, u32[]{:S(2)}, u32[]{:S(2)}) collective-permute-start(bf16[2,4,16,128]{3,2,1,0:T(8,128)(2,1)S(1)} %get-tuple-element.35), channel_id=1, source_target_pairs={{0,64},{16,80},{32,96},{48,112},{64,0},{80,16},{96,32},{112,48},{1... | collective-permute-start | bytes 98312 | tf_op jit(solution)/shard_map/ppermute | solution.py:260
  46.6 9.6 %collective-permute-start.3 = (bf16[2,4,16,128]{3,2,1,0:T(8,128)(2,1)S(1)}, bf16[2,4,16,128]{3,2,1,0:T(8,128)(2,1)S(1)}, u32[]{:S(2)}, u32[]{:S(2)}) collective-permute-start(bf16[2,4,16,128]{3,2,1,0:T(8,128)(2,1)S(1)} %get-tuple-element.36), channel_id=1, source_target_pairs={{0,96},{16,112},{32,64},{48,80},{64,32},{80,48},{96,0},{112,16},{1... | collective-permute-start | bytes 98312 | tf_op jit(solution)/shard_map/ppermute | solution.py:260
  46.8 9.4 %collective-permute-start.4 = (bf16[2,4,16,128]{3,2,1,0:T(8,128)(2,1)S(1)}, bf16[2,4,16,128]{3,2,1,0:T(8,128)(2,1)S(1)}, u32[]{:S(2)}, u32[]{:S(2)}) collective-permute-start(bf16[2,4,16,128]{3,2,1,0:T(8,128)(2,1)S(1)} %get-tuple-element.37), channel_id=1, source_target_pairs={{0,128},{16,144},{32,160},{48,176},{64,192},{80,208},{96,224},{112... | collective-permute-start | bytes 98312 | tf_op jit(solution)/shard_map/ppermute | solution.py:260
  48.1 8.1 %collective-permute-start.5 = (bf16[2,4,16,128]{3,2,1,0:T(8,128)(2,1)S(1)}, bf16[2,4,16,128]{3,2,1,0:T(8,128)(2,1)S(1)}, u32[]{:S(2)}, u32[]{:S(2)}) collective-permute-start(bf16[2,4,16,128]{3,2,1,0:T(8,128)(2,1)S(1)} %get-tuple-element.38), channel_id=1, source_target_pairs={{0,160},{16,176},{32,128},{48,144},{64,224},{80,240},{96,192},{112... | collective-permute-start | bytes 98312 | tf_op jit(solution)/shard_map/ppermute | solution.py:260
  49.5 10.8 %collective-permute-start.6 = (bf16[2,4,16,128]{3,2,1,0:T(8,128)(2,1)S(1)}, bf16[2,4,16,128]{3,2,1,0:T(8,128)(2,1)S(1)}, u32[]{:S(2)}, u32[]{:S(2)}) collective-permute-start(bf16[2,4,16,128]{3,2,1,0:T(8,128)(2,1)S(1)} %get-tuple-element.39), channel_id=1, source_target_pairs={{0,192},{16,208},{32,224},{48,240},{64,128},{80,144},{96,160},{112... | collective-permute-start | bytes 98312 | tf_op jit(solution)/shard_map/ppermute | solution.py:260
  55.1 5.5 %collective-permute-start.7 = (bf16[2,4,16,128]{3,2,1,0:T(8,128)(2,1)S(1)}, bf16[2,4,16,128]{3,2,1,0:T(8,128)(2,1)S(1)}, u32[]{:S(2)}, u32[]{:S(2)}) collective-permute-start(bf16[2,4,16,128]{3,2,1,0:T(8,128)(2,1)S(1)} %get-tuple-element.40), channel_id=1, source_target_pairs={{0,224},{16,240},{32,192},{48,208},{64,160},{80,176},{96,128},{112... | collective-permute-start | bytes 98312 | tf_op jit(solution)/shard_map/ppermute | solution.py:260
  62.1 4.2 %collective-permute-start.8 = (bf16[8,8,16,128]{3,2,1,0:T(8,128)(2,1)S(1)}, bf16[8,8,16,128]{3,2,1,0:T(8,128)(2,1)S(1)}, u32[]{:S(2)}, u32[]{:S(2)}) collective-permute-start(bf16[8,8,16,128]{3,2,1,0:T(8,128)(2,1)S(1)} %get-tuple-element.42), channel_id=1, source_target_pairs={{0,16},{16,0},{32,48},{48,32},{64,80},{80,64},{96,112},{112,96},{1... | collective-permute-start | bytes 786440 | tf_op jit(solution)/shard_map/ppermute | solution.py:260
  66.3 0.6 copy-start.4
  66.9 8.0 %collective-permute-start.9 = (bf16[2,8,16,128]{3,2,1,0:T(8,128)(2,1)S(1)}, bf16[2,8,16,128]{3,2,1,0:T(8,128)(2,1)S(1)}, u32[]{:S(2)}, u32[]{:S(2)}) collective-permute-start(bf16[2,8,16,128]{3,2,1,0:T(8,128)(2,1)S(1)} %get-tuple-element.44), channel_id=1, source_target_pairs={{0,32},{16,48},{32,0},{48,16},{64,96},{80,112},{96,64},{112,80},{1... | collective-permute-start | bytes 196616 | tf_op jit(solution)/shard_map/ppermute | solution.py:260
  68.2 10.3 %collective-permute-start.10 = (bf16[2,8,16,128]{3,2,1,0:T(8,128)(2,1)S(1)}, bf16[2,8,16,128]{3,2,1,0:T(8,128)(2,1)S(1)}, u32[]{:S(2)}, u32[]{:S(2)}) collective-permute-start(bf16[2,8,16,128]{3,2,1,0:T(8,128)(2,1)S(1)} %get-tuple-element.45), channel_id=1, source_target_pairs={{0,64},{16,80},{32,96},{48,112},{64,0},{80,16},{96,32},{112,48},{1... | collective-permute-start | bytes 196616 | tf_op jit(solution)/shard_map/ppermute | solution.py:260
  69.2 14.0 %collective-permute-start.11 = (bf16[2,8,16,128]{3,2,1,0:T(8,128)(2,1)S(1)}, bf16[2,8,16,128]{3,2,1,0:T(8,128)(2,1)S(1)}, u32[]{:S(2)}, u32[]{:S(2)}) collective-permute-start(bf16[2,8,16,128]{3,2,1,0:T(8,128)(2,1)S(1)} %get-tuple-element.46), channel_id=1, source_target_pairs={{0,96},{16,112},{32,64},{48,80},{64,32},{80,48},{96,0},{112,16},{1... | collective-permute-start | bytes 196616 | tf_op jit(solution)/shard_map/ppermute | solution.py:260
  70.8 12.4 %collective-permute-start.12 = (bf16[2,8,16,128]{3,2,1,0:T(8,128)(2,1)S(1)}, bf16[2,8,16,128]{3,2,1,0:T(8,128)(2,1)S(1)}, u32[]{:S(2)}, u32[]{:S(2)}) collective-permute-start(bf16[2,8,16,128]{3,2,1,0:T(8,128)(2,1)S(1)} %get-tuple-element.47), channel_id=1, source_target_pairs={{0,128},{16,144},{32,160},{48,176},{64,192},{80,208},{96,224},{112... | collective-permute-start | bytes 196616 | tf_op jit(solution)/shard_map/ppermute | solution.py:260
  72.4 13.6 %collective-permute-start.13 = (bf16[2,8,16,128]{3,2,1,0:T(8,128)(2,1)S(1)}, bf16[2,8,16,128]{3,2,1,0:T(8,128)(2,1)S(1)}, u32[]{:S(2)}, u32[]{:S(2)}) collective-permute-start(bf16[2,8,16,128]{3,2,1,0:T(8,128)(2,1)S(1)} %get-tuple-element.48), channel_id=1, source_target_pairs={{0,160},{16,176},{32,128},{48,144},{64,224},{80,240},{96,192},{112... | collective-permute-start | bytes 196616 | tf_op jit(solution)/shard_map/ppermute | solution.py:260
  74.9 21.8 %copy-start.9 = (bf16[2,8,16,128]{3,2,1,0:T(8,128)(2,1)}, bf16[2,8,16,128]{3,2,1,0:T(8,128)(2,1)S(1)}, u32[]{:S(2)}) copy-start(bf16[2,8,16,128]{3,2,1,0:T(8,128)(2,1)S(1)} %collective-permute-done.9.refs_1_) | copy-start | bytes 196612
  74.9 14.6 %collective-permute-start.14 = (bf16[2,8,16,128]{3,2,1,0:T(8,128)(2,1)S(1)}, bf16[2,8,16,128]{3,2,1,0:T(8,128)(2,1)S(1)}, u32[]{:S(2)}, u32[]{:S(2)}) collective-permute-start(bf16[2,8,16,128]{3,2,1,0:T(8,128)(2,1)S(1)} %get-tuple-element.49), channel_id=1, source_target_pairs={{0,192},{16,208},{32,224},{48,240},{64,128},{80,144},{96,160},{112... | collective-permute-start | bytes 196616 | tf_op jit(solution)/shard_map/ppermute | solution.py:260
  78.5 18.3 %copy-start.10 = (bf16[2,8,16,128]{3,2,1,0:T(8,128)(2,1)}, bf16[2,8,16,128]{3,2,1,0:T(8,128)(2,1)S(1)}, u32[]{:S(2)}) copy-start(bf16[2,8,16,128]{3,2,1,0:T(8,128)(2,1)S(1)} %collective-permute-done.10.refs_2_) | copy-start | bytes 196612
  78.5 11.0 %collective-permute-start.15 = (bf16[2,8,16,128]{3,2,1,0:T(8,128)(2,1)S(1)}, bf16[2,8,16,128]{3,2,1,0:T(8,128)(2,1)S(1)}, u32[]{:S(2)}, u32[]{:S(2)}) collective-permute-start(bf16[2,8,16,128]{3,2,1,0:T(8,128)(2,1)S(1)} %get-tuple-element.50), channel_id=1, source_target_pairs={{0,224},{16,240},{32,192},{48,208},{64,160},{80,176},{96,128},{112... | collective-permute-start | bytes 196616 | tf_op jit(solution)/shard_map/ppermute | solution.py:260
  83.2 13.6 %copy-start.11 = (bf16[2,8,16,128]{3,2,1,0:T(8,128)(2,1)}, bf16[2,8,16,128]{3,2,1,0:T(8,128)(2,1)S(1)}, u32[]{:S(2)}) copy-start(bf16[2,8,16,128]{3,2,1,0:T(8,128)(2,1)S(1)} %collective-permute-done.11.refs_3_) | copy-start | bytes 196612
  83.2 13.6 %copy-start.12 = (bf16[2,8,16,128]{3,2,1,0:T(8,128)(2,1)}, bf16[2,8,16,128]{3,2,1,0:T(8,128)(2,1)S(1)}, u32[]{:S(2)}) copy-start(bf16[2,8,16,128]{3,2,1,0:T(8,128)(2,1)S(1)} %collective-permute-done.12.refs_4_) | copy-start | bytes 196612
  86.0 10.7 %copy-start.13 = (bf16[2,8,16,128]{3,2,1,0:T(8,128)(2,1)}, bf16[2,8,16,128]{3,2,1,0:T(8,128)(2,1)S(1)}, u32[]{:S(2)}) copy-start(bf16[2,8,16,128]{3,2,1,0:T(8,128)(2,1)S(1)} %collective-permute-done.13.refs_5_) | copy-start | bytes 196612
  89.5 7.3 %copy-start.14 = (bf16[2,8,16,128]{3,2,1,0:T(8,128)(2,1)}, bf16[2,8,16,128]{3,2,1,0:T(8,128)(2,1)S(1)}, u32[]{:S(2)}) copy-start(bf16[2,8,16,128]{3,2,1,0:T(8,128)(2,1)S(1)} %collective-permute-done.14.refs_6_) | copy-start | bytes 196612
  89.5 7.3 %copy-start.15 = (bf16[2,8,16,128]{3,2,1,0:T(8,128)(2,1)}, bf16[2,8,16,128]{3,2,1,0:T(8,128)(2,1)S(1)}, u32[]{:S(2)}) copy-start(bf16[2,8,16,128]{3,2,1,0:T(8,128)(2,1)S(1)} %collective-permute-done.15.refs_7_) | copy-start | bytes 196612
  96.7 1.4 %copy-start.7 = (s32[256,1,2176]{2,1,0:T(1,128)}, s32[256,1,2176]{2,1,0:T(1,128)S(1)}, u32[]{:S(2)}) copy-start(s32[256,1,2176]{2,1,0:T(1,128)S(1)} %all-to-all-done.1) | copy-start | bytes 6684676
Sparse Core Ops, SparseCore 0:
  30.2 65.9 all-gather.1

commit v3 on v2

--- a/solution.py
+++ b/solution.py
@@ -12,31 +12,58 @@
 FULL = 32760.0
 MIDDLE = 32768.0
 VMEM = 32 * 1024 * 1024
-FILTER_VMEM = 60 * 1024 * 1024
+LARGE_VMEM = 60 * 1024 * 1024
 CORES = 2
 
 
-def pack_kernel(vis_ref, flag_ref, out_ref, rows):
-    for tile in range(vis_ref.shape[3] // LANES):
-        lanes = pl.ds(tile * LANES, LANES)
-        keep = flag_ref[:, lanes].astype(jnp.float32)
-        masked = vis_ref[:, :, :, lanes] * keep[None, None]
-        loudest = jnp.max(jnp.abs(masked), axis=(0, 1, 2), keepdims=True)
-        level = jnp.ceil(jnp.log2(jnp.maximum(loudest, 1e-30)) * 4.0)
-        factor = FULL / jnp.exp2(level * 0.25)
-        coded = (masked * factor + (MIDDLE + 0.5)).astype(jnp.int32)
-        words = coded[0] | (coded[1] << 16)
-        level_row = level.reshape(1, LANES).astype(jnp.int32)
-        times, chans = words.shape[0], words.shape[1]
-        fold = LANES // chans
-        for part in range(times // fold):
-            turned = words[part * fold : (part + 1) * fold].reshape(LANES, LANES).T
-            for owner in range(LANES // SUB):
-                place = (tile * (LANES // SUB) + owner) * rows + part * SUB
-                out_ref[place : place + SUB, :] = turned[owner * SUB : (owner + 1) * SUB]
-        for owner in range(LANES // SUB):
-            place = (tile * (LANES // SUB) + owner) * rows + rows - 1
-            out_ref[place : place + 1, :] = level_row
+def pack_kernel(vis_ref, flag_ref, out_ref, vis, flag, packed, vis_sems, flag_sem, out_sems, *, rows):
+    steps, lanes = vis.shape[0], vis.shape[4]
+    owners = LANES // SUB
+
+    def fetch_vis(step):
+        there = pl.ds(pl.multiple_of(step * lanes, lanes), lanes)
+        return pltpu.make_async_copy(vis_ref.at[:, :, :, there], vis.at[step], vis_sems.at[step])
+
+    def fetch_flag():
+        return pltpu.make_async_copy(flag_ref, flag, flag_sem)
+
+    def send_out(step):
+        there = pl.ds(pl.multiple_of(step * packed.shape[1], SUB), packed.shape[1])
+        return pltpu.make_async_copy(packed.at[step], out_ref.at[there], out_sems.at[step])
+
+    fetch_flag().start()
+    for step in range(steps):
+        fetch_vis(step).start()
+    fetch_flag().wait()
+
+    def one(step, carry):
+        fetch_vis(step).wait()
+        for tile in range(lanes // LANES):
+            here = pl.ds(tile * LANES, LANES)
+            keep = flag[:, pl.ds(pl.multiple_of(step * lanes + tile * LANES, LANES), LANES)].astype(jnp.float32)
+            masked = vis[step, :, :, :, here] * keep[None, None]
+            loudest = jnp.max(jnp.abs(masked), axis=(0, 1, 2), keepdims=True)
+            level = jnp.ceil(jnp.log2(jnp.maximum(loudest, 1e-30)) * 4.0)
+            factor = FULL / jnp.exp2(level * 0.25)
+            coded = (masked * factor + (MIDDLE + 0.5)).astype(jnp.int32)
+            words = coded[0] | (coded[1] << 16)
+            level_row = level.reshape(1, LANES).astype(jnp.int32)
+            times, chans = words.shape[0], words.shape[1]
+            fold = LANES // chans
+            for part in range(times // fold):
+                turned = words[part * fold : (part + 1) * fold].reshape(LANES, LANES).T
+                for owner in range(owners):
+                    place = (tile * owners + owner) * rows + part * SUB
+                    packed[step, place : place + SUB, :] = turned[owner * SUB : (owner + 1) * SUB]
+            for owner in range(owners):
+                place = (tile * owners + owner) * rows + rows - 1
+                packed[step, place : place + 1, :] = level_row
+        send_out(step).start()
+        return carry
+
+    lax.fori_loop(0, steps, one, 0)
+    for step in range(steps):
+        send_out(step).wait()
 
 
 def shares_kernel(place_ref, fringe_ref, *out_refs):
@@ -236,16 +263,22 @@
 
     rows = times * chans * SUB // LANES // SUB * own + 1
     step_lanes = 2 * LANES
+    steps = total // step_lanes
+    far = pl.BlockSpec(memory_space=pltpu.HBM)
     packed = pl.pallas_call(
         functools.partial(pack_kernel, rows=rows),
-        grid=(total // step_lanes,),
-        in_specs=[
-            pl.BlockSpec((2, times, chans, step_lanes), lambda n: (0, 0, 0, n)),
-            pl.BlockSpec((chans, step_lanes), lambda n: (0, n)),
+        in_specs=[far, far],
+        out_specs=far,
+        scratch_shapes=[
+            pltpu.VMEM((steps, 2, times, chans, step_lanes), jnp.float32),
+            pltpu.VMEM((chans, total), jnp.int32),
+            pltpu.VMEM((steps, step_lanes // SUB * rows, LANES), jnp.int32),
+            pltpu.SemaphoreType.DMA((steps,)),
+            pltpu.SemaphoreType.DMA,
+            pltpu.SemaphoreType.DMA((steps,)),
         ],
-        out_specs=pl.BlockSpec((step_lanes // SUB * rows, LANES), lambda n: (n, 0)),
         out_shape=jax.ShapeDtypeStruct((devices * rows, LANES), jnp.int32),
-        compiler_params=params(),
+        compiler_params=pltpu.CompilerParams(vmem_limit_bytes=LARGE_VMEM),
         name="pack",
     )(jnp.transpose(visibility, (0, 2, 3, 1)), flags.T)
     share, fringe, packed = lax.optimization_barrier((share, fringe, packed))
@@ -324,7 +357,7 @@
             ],
         ),
         out_shape=jax.ShapeDtypeStruct((2, own, all_times, all_chans), jnp.float32),
-        compiler_params=pltpu.CompilerParams(vmem_limit_bytes=FILTER_VMEM),
+        compiler_params=pltpu.CompilerParams(vmem_limit_bytes=LARGE_VMEM),
         name="filter",
     )(groups, place, words, delay_all, *mats)
 

time: 118 us -> 118 us (level)
  local copies, waits for them, and re-layouts: 7.5 us -> 4.39 us
  waiting for transfers between devices: 30.5 us -> 33 us
    unnamed x32 -> x28, local copies, waits for them, and re-layouts: 6.78 us -> 3.66 us
    all_to_all x1, waiting for transfers between devices: 3.15 us -> 5.63 us  [shards(): lax.all_to_all(jnp.broadcast_to(share, (chan_count, chans, wide)), 'chan'...]
  transfers between devices with their start and end apart: 19 -> 19, of which waited for: 12 -> 12; matrix products, arithmetic and copies ran while one was open for 0% -> 0% of each run, Pallas kernels for 5% -> 6%
where the time goes in v3:
time: 118 us; the launch traced here: 117 us
  starting transfers between devices  46.2 us (39%)
  waiting for transfers between devices  33 us (28%)
  Pallas kernels  19.9 us (17%)
  between operations  13.6 us (12%)
  local copies, waits for them, and re-layouts  4.39 us (4%)
    ppermute x16, starting transfers between devices, crossed(): lax.ppermute(array, 'tm', [(k, k ^ mask) for k in range(time_count)])  25.7 us
    ppermute x16, waiting for transfers between devices, crossed(): lax.ppermute(array, 'tm', [(k, k ^ mask) for k in range(time_count)])  20.2 us
    pallas_call x1, Pallas kernels, shards(): pl.pallas_call(functools.partial(filter_kernel, rows=rows, spread=spread)...  12.9 us
    all_to_all x1, starting transfers between devices, shards(): lax.all_to_all(jnp.broadcast_to(share, (chan_count, chans, wide)), 'chan'...  10.7 us
    all_to_all x1, starting transfers between devices, shards(): lax.all_to_all(packed.reshape(devices, 1, rows * LANES), everyone, split_...  9.78 us
    all_to_all x1, waiting for transfers between devices, shards(): lax.all_to_all(packed.reshape(devices, 1, rows * LANES), everyone, split_...  7.2 us
    all_to_all x1, waiting for transfers between devices, shards(): lax.all_to_all(jnp.broadcast_to(share, (chan_count, chans, wide)), 'chan'...  5.63 us
    pallas_call x1, Pallas kernels, shards(): pl.pallas_call(functools.partial(pack_kernel, rows=rows), in_specs=[far,...  4.81 us
  transfers between devices with their start and end apart: 19, of which 12 were waited for; matrix products, arithmetic and copies ran while one was open for 0% of the time, Pallas kernels for 6%

profile of v3, /device:TPU:33, one launch (start us, length us, event | category | flops | bytes accessed | tf_op | source)
XLA Modules:
  0.0 117.2 jit_solution(7138443200745363185)
XLA Ops:
  6.5 0.0 copy-start
  6.5 0.9 copy-done
  7.5 0.7 broadcast_in_dim.8
  8.2 10.7 %all-to-all-start = ((bf16[16,32,256]{2,1,0:T(8,128)(2,1)}), bf16[16,32,256]{2,1,0:T(8,128)(2,1)S(1)}, u32[]{:S(2)}, u32[]{:S(2)}) async-start(bf16[16,32,256]{2,1,0:T(8,128)(2,1)} %broadcast_in_dim.8), calls=%async_computation | async-start | bytes 524288 | tf_op jit(solution)/shard_map/all_to_all | solution.py:260
  18.9 0.0 all-gather.2.cloned.1.call-start
  18.9 0.0 copy-start.1
  18.9 4.8 %pack.1 = s32[4352,128]{1,0:T(8,128)} custom-call(f32[2,8,32,2048]{3,2,1,0:T(8,128)} %bitcast.15, s32[32,2048]{1,0:T(8,128)} %bitcast.17), custom_call_target="tpu_custom_call" | custom-call | tf_op jit(solution)/shard_map/pack/pallas_call | solution.py:268
  23.8 0.0 copy-start.3
  23.8 5.6 %all-to-all-done = bf16[16,32,256]{2,1,0:T(8,128)(2,1)S(1)} async-done(((bf16[16,32,256]{2,1,0:T(8,128)(2,1)}), bf16[16,32,256]{2,1,0:T(8,128)(2,1)S(1)}, u32[]{:S(2)}, u32[]{:S(2)}) %all-to-all-start) | async-done | bytes 262176 | tf_op jit(solution)/shard_map/all_to_all | solution.py:260
  29.4 0.0 copy-start.6
  29.4 0.7 copy-done.6
  30.1 0.0 all-gather.2.cloned.1.call-update
  30.1 9.8 %all-to-all-start.1 = ((s32[256,1,2176]{2,1,0:T(1,128)}), s32[256,1,2176]{2,1,0:T(1,128)S(1)}, u32[]{:S(2)}, u32[]{:S(2)}) async-start(s32[256,1,2176]{2,1,0:T(1,128)} %bitcast.13), calls=%async_computation.1 | async-start | bytes 4456448 | tf_op jit(solution)/shard_map/all_to_all | solution.py:287
  39.9 0.1 pad_add_fusion.place_ref
  40.0 0.0 copy-done.1
  40.0 0.6 shares.1
  40.7 0.4 collective-permute-start
  41.1 1.0 collective-permute-done.refs_1_
  42.1 1.3 %collective-permute-start.1 = (bf16[2,4,16,128]{3,2,1,0:T(8,128)(2,1)S(1)}, bf16[2,4,16,128]{3,2,1,0:T(8,128)(2,1)S(1)}, u32[]{:S(2)}, u32[]{:S(2)}) collective-permute-start(bf16[2,4,16,128]{3,2,1,0:T(8,128)(2,1)S(1)} %get-tuple-element.34), channel_id=1, source_target_pairs={{0,32},{16,48},{32,0},{48,16},{64,96},{80,112},{96,64},{112,80},{1... | collective-permute-start | bytes 98312 | tf_op jit(solution)/shard_map/ppermute | solution.py:293
  43.4 2.4 %collective-permute-start.2 = (bf16[2,4,16,128]{3,2,1,0:T(8,128)(2,1)S(1)}, bf16[2,4,16,128]{3,2,1,0:T(8,128)(2,1)S(1)}, u32[]{:S(2)}, u32[]{:S(2)}) collective-permute-start(bf16[2,4,16,128]{3,2,1,0:T(8,128)(2,1)S(1)} %get-tuple-element.35), channel_id=1, source_target_pairs={{0,64},{16,80},{32,96},{48,112},{64,0},{80,16},{96,32},{112,48},{1... | collective-permute-start | bytes 98312 | tf_op jit(solution)/shard_map/ppermute | solution.py:293
  45.8 0.2 collective-permute-start.3
  46.1 1.2 %collective-permute-start.4 = (bf16[2,4,16,128]{3,2,1,0:T(8,128)(2,1)S(1)}, bf16[2,4,16,128]{3,2,1,0:T(8,128)(2,1)S(1)}, u32[]{:S(2)}, u32[]{:S(2)}) collective-permute-start(bf16[2,4,16,128]{3,2,1,0:T(8,128)(2,1)S(1)} %get-tuple-element.37), channel_id=1, source_target_pairs={{0,128},{16,144},{32,160},{48,176},{64,192},{80,208},{96,224},{112... | collective-permute-start | bytes 98312 | tf_op jit(solution)/shard_map/ppermute | solution.py:293
  47.3 0.0 collective-permute-start.5
  47.3 1.5 %collective-permute-done.1.refs_1_ = bf16[2,4,16,128]{3,2,1,0:T(8,128)(2,1)S(1)} collective-permute-done((bf16[2,4,16,128]{3,2,1,0:T(8,128)(2,1)S(1)}, bf16[2,4,16,128]{3,2,1,0:T(8,128)(2,1)S(1)}, u32[]{:S(2)}, u32[]{:S(2)}) %collective-permute-start.1) | collective-permute-done | bytes 32800 | tf_op jit(solution)/shard_map/ppermute | solution.py:293
  48.8 3.5 %collective-permute-start.6 = (bf16[2,4,16,128]{3,2,1,0:T(8,128)(2,1)S(1)}, bf16[2,4,16,128]{3,2,1,0:T(8,128)(2,1)S(1)}, u32[]{:S(2)}, u32[]{:S(2)}) collective-permute-start(bf16[2,4,16,128]{3,2,1,0:T(8,128)(2,1)S(1)} %get-tuple-element.39), channel_id=1, source_target_pairs={{0,192},{16,208},{32,224},{48,240},{64,128},{80,144},{96,160},{112... | collective-permute-start | bytes 98312 | tf_op jit(solution)/shard_map/ppermute | solution.py:293
  52.3 2.1 %collective-permute-done.2.refs_2_ = bf16[2,4,16,128]{3,2,1,0:T(8,128)(2,1)S(1)} collective-permute-done((bf16[2,4,16,128]{3,2,1,0:T(8,128)(2,1)S(1)}, bf16[2,4,16,128]{3,2,1,0:T(8,128)(2,1)S(1)}, u32[]{:S(2)}, u32[]{:S(2)}) %collective-permute-start.2) | collective-permute-done | bytes 32800 | tf_op jit(solution)/shard_map/ppermute | solution.py:293
  54.4 1.1 collective-permute-start.7
  55.4 0.0 collective-permute-done.3.refs_3_
  55.5 0.0 collective-permute-done.4.refs_4_
  55.5 0.0 collective-permute-done.5.refs_5_
  55.5 4.1 %collective-permute-done.6.refs_6_ = bf16[2,4,16,128]{3,2,1,0:T(8,128)(2,1)S(1)} collective-permute-done((bf16[2,4,16,128]{3,2,1,0:T(8,128)(2,1)S(1)}, bf16[2,4,16,128]{3,2,1,0:T(8,128)(2,1)S(1)}, u32[]{:S(2)}, u32[]{:S(2)}) %collective-permute-start.6) | collective-permute-done | bytes 32800 | tf_op jit(solution)/shard_map/ppermute | solution.py:293
  59.6 0.3 collective-permute-done.7.refs_7_
  59.9 0.0 copy-done.3
  59.9 1.5 %select.7 = (bf16[8,8,16,128]{3,2,1,0:T(8,128)(2,1)S(1)}, bf16[8,8,16,128]{3,2,1,0:T(8,128)(2,1)S(1)}) custom-call(s32[2048]{0:T(1024)S(1)} %copy-done.3, s32[2]{0:T(128)S(1)} %pad_add_fusion.place_ref, bf16[2,4,16,128]{3,2,1,0:T(8,128)(2,1)S(1)} %get-tuple-element.33.refs_0_, bf16[2,4,16,128]{3,2,1,0:T(8,128)(2,1)S(1)} %collective-permute-done.1.refs_1_, ...), custom_call_target="tpu_custom_call" | custom-call | tf_op jit(solution)/shard_map/select/pallas_call | solution.py:321
  61.4 3.0 %collective-permute-start.8 = (bf16[8,8,16,128]{3,2,1,0:T(8,128)(2,1)S(1)}, bf16[8,8,16,128]{3,2,1,0:T(8,128)(2,1)S(1)}, u32[]{:S(2)}, u32[]{:S(2)}) collective-permute-start(bf16[8,8,16,128]{3,2,1,0:T(8,128)(2,1)S(1)} %get-tuple-element.42), channel_id=1, source_target_pairs={{0,16},{16,0},{32,48},{48,32},{64,80},{80,64},{96,112},{112,96},{1... | collective-permute-start | bytes 786440 | tf_op jit(solution)/shard_map/ppermute | solution.py:293
  64.4 1.2 collective-permute-done.8.refs_1_
  65.6 0.0 copy-start.2
  65.6 0.6 copy-done.2
  66.2 1.2 %collective-permute-start.9 = (bf16[2,8,16,128]{3,2,1,0:T(8,128)(2,1)S(1)}, bf16[2,8,16,128]{3,2,1,0:T(8,128)(2,1)S(1)}, u32[]{:S(2)}, u32[]{:S(2)}) collective-permute-start(bf16[2,8,16,128]{3,2,1,0:T(8,128)(2,1)S(1)} %get-tuple-element.44), channel_id=1, source_target_pairs={{0,32},{16,48},{32,0},{48,16},{64,96},{80,112},{96,64},{112,80},{1... | collective-permute-start | bytes 196616 | tf_op jit(solution)/shard_map/ppermute | solution.py:293
  67.4 1.0 collective-permute-start.10
  68.4 1.6 %collective-permute-start.11 = (bf16[2,8,16,128]{3,2,1,0:T(8,128)(2,1)S(1)}, bf16[2,8,16,128]{3,2,1,0:T(8,128)(2,1)S(1)}, u32[]{:S(2)}, u32[]{:S(2)}) collective-permute-start(bf16[2,8,16,128]{3,2,1,0:T(8,128)(2,1)S(1)} %get-tuple-element.46), channel_id=1, source_target_pairs={{0,96},{16,112},{32,64},{48,80},{64,32},{80,48},{96,0},{112,16},{1... | collective-permute-start | bytes 196616 | tf_op jit(solution)/shard_map/ppermute | solution.py:293
  70.1 1.6 %collective-permute-start.12 = (bf16[2,8,16,128]{3,2,1,0:T(8,128)(2,1)S(1)}, bf16[2,8,16,128]{3,2,1,0:T(8,128)(2,1)S(1)}, u32[]{:S(2)}, u32[]{:S(2)}) collective-permute-start(bf16[2,8,16,128]{3,2,1,0:T(8,128)(2,1)S(1)} %get-tuple-element.47), channel_id=1, source_target_pairs={{0,128},{16,144},{32,160},{48,176},{64,192},{80,208},{96,224},{112... | collective-permute-start | bytes 196616 | tf_op jit(solution)/shard_map/ppermute | solution.py:293
  71.7 0.0 collective-permute-start.13
  71.7 2.5 %collective-permute-done.9.refs_1_ = bf16[2,8,16,128]{3,2,1,0:T(8,128)(2,1)S(1)} collective-permute-done((bf16[2,8,16,128]{3,2,1,0:T(8,128)(2,1)S(1)}, bf16[2,8,16,128]{3,2,1,0:T(8,128)(2,1)S(1)}, u32[]{:S(2)}, u32[]{:S(2)}) %collective-permute-start.9) | collective-permute-done | bytes 65568 | tf_op jit(solution)/shard_map/ppermute | solution.py:293
  74.2 2.3 %collective-permute-start.14 = (bf16[2,8,16,128]{3,2,1,0:T(8,128)(2,1)S(1)}, bf16[2,8,16,128]{3,2,1,0:T(8,128)(2,1)S(1)}, u32[]{:S(2)}, u32[]{:S(2)}) collective-permute-start(bf16[2,8,16,128]{3,2,1,0:T(8,128)(2,1)S(1)} %get-tuple-element.49), channel_id=1, source_target_pairs={{0,192},{16,208},{32,224},{48,240},{64,128},{80,144},{96,160},{112... | collective-permute-start | bytes 196616 | tf_op jit(solution)/shard_map/ppermute | solution.py:293
  76.5 1.3 %collective-permute-done.10.refs_2_ = bf16[2,8,16,128]{3,2,1,0:T(8,128)(2,1)S(1)} collective-permute-done((bf16[2,8,16,128]{3,2,1,0:T(8,128)(2,1)S(1)}, bf16[2,8,16,128]{3,2,1,0:T(8,128)(2,1)S(1)}, u32[]{:S(2)}, u32[]{:S(2)}) %collective-permute-start.10) | collective-permute-done | bytes 65568 | tf_op jit(solution)/shard_map/ppermute | solution.py:293
  77.7 4.7 %collective-permute-start.15 = (bf16[2,8,16,128]{3,2,1,0:T(8,128)(2,1)S(1)}, bf16[2,8,16,128]{3,2,1,0:T(8,128)(2,1)S(1)}, u32[]{:S(2)}, u32[]{:S(2)}) collective-permute-start(bf16[2,8,16,128]{3,2,1,0:T(8,128)(2,1)S(1)} %get-tuple-element.50), channel_id=1, source_target_pairs={{0,224},{16,240},{32,192},{48,208},{64,160},{80,176},{96,128},{112... | collective-permute-start | bytes 196616 | tf_op jit(solution)/shard_map/ppermute | solution.py:293
  82.4 0.0 collective-permute-done.11.refs_3_
  82.4 0.0 collective-permute-done.12.refs_4_
  82.5 0.0 copy-start.10
  82.5 2.8 %collective-permute-done.13.refs_5_ = bf16[2,8,16,128]{3,2,1,0:T(8,128)(2,1)S(1)} collective-permute-done((bf16[2,8,16,128]{3,2,1,0:T(8,128)(2,1)S(1)}, bf16[2,8,16,128]{3,2,1,0:T(8,128)(2,1)S(1)}, u32[]{:S(2)}, u32[]{:S(2)}) %collective-permute-start.13) | collective-permute-done | bytes 65568 | tf_op jit(solution)/shard_map/ppermute | solution.py:293
  85.3 3.5 %collective-permute-done.14.refs_6_ = bf16[2,8,16,128]{3,2,1,0:T(8,128)(2,1)S(1)} collective-permute-done((bf16[2,8,16,128]{3,2,1,0:T(8,128)(2,1)S(1)}, bf16[2,8,16,128]{3,2,1,0:T(8,128)(2,1)S(1)}, u32[]{:S(2)}, u32[]{:S(2)}) %collective-permute-start.14) | collective-permute-done | bytes 65568 | tf_op jit(solution)/shard_map/ppermute | solution.py:293
  88.8 0.0 collective-permute-done.15.refs_7_
  88.8 7.2 %all-to-all-done.1 = s32[256,1,2176]{2,1,0:T(1,128)S(1)} async-done(((s32[256,1,2176]{2,1,0:T(1,128)}), s32[256,1,2176]{2,1,0:T(1,128)S(1)}, u32[]{:S(2)}, u32[]{:S(2)}) %all-to-all-start.1) | async-done | bytes 2228256 | tf_op jit(solution)/shard_map/all_to_all | solution.py:287
  96.0 0.0 copy-done.4
  96.0 0.0 copy-done.7
  96.0 0.0 copy-done.8
  96.0 0.0 copy-done.9
  96.0 0.0 copy-done.10
  96.0 0.0 copy-done.11
  96.0 0.0 copy-done.12
  96.0 0.0 copy-done.13
  96.0 1.3 %copy-done.5 = s32[256,1,2176]{2,1,0:T(1,128)} copy-done((s32[256,1,2176]{2,1,0:T(1,128)}, s32[256,1,2176]{2,1,0:T(1,128)S(1)}, u32[]{:S(2)}) %copy-start.5) | copy-done | bytes 2228248
  97.4 12.9 %filter.1 = f32[2,8,128,512]{3,2,1,0:T(8,128)} custom-call(s32[2048]{0:T(1024)} %groups_ref.3, s32[2]{0:T(128)} %copy-done.4, s32[16,272,128]{2,1,0:T(8,128)} %bitcast.12, bf16[8,2,512,256]{3,2,1,0:T(8,128)(2,1)} %bitcast.14, bf16[2,8,16,128]{3,2,1,0:T(8,128)(2,1)} %copy-done.2, bf16[2,8,16,128]{3,2,1,0:T(8,128)(2,1)} %copy-done.7, ...), custom_call_target="tpu_custom_call" | custom-call | tf_op jit(solution)/shard_map/filter/pallas_call | solution.py:338
  (12 shorter events, 0.1 us)
Async XLA Ops:
  6.5 1.0 copy-start
  8.2 21.2 %all-to-all-start = ((bf16[16,32,256]{2,1,0:T(8,128)(2,1)}), bf16[16,32,256]{2,1,0:T(8,128)(2,1)S(1)}, u32[]{:S(2)}, u32[]{:S(2)}) async-start(bf16[16,32,256]{2,1,0:T(8,128)(2,1)} %broadcast_in_dim.8), calls=%async_computation | async-start | bytes 524288 | tf_op jit(solution)/shard_map/all_to_all | solution.py:260
  18.9 77.1 %all-gather.2.cloned.1.call-start = ((), (), s32[]{:S(2)}) async-start(), calls=%async_computation.2 | async-start | bytes 4456448 | tf_op jit(solution)/shard_map/all_gather | solution.py:285
  18.9 21.1 %copy-start.1 = (bf16[2,4,128,128]{3,2,1,0:T(8,128)(2,1)S(1)}, bf16[2,4,128,128]{3,2,1,0:T(8,128)(2,1)}, u32[]{:S(2)}) copy-start(bf16[2,4,128,128]{3,2,1,0:T(8,128)(2,1)} %param.8) | copy-start | bytes 786436
  23.8 36.1 %copy-start.3 = (s32[2048]{0:T(1024)S(1)}, s32[2048]{0:T(1024)}, u32[]{:S(2)}) copy-start(s32[2048]{0:T(1024)} %groups_ref.3) | copy-start | bytes 24580
  29.4 0.7 copy-start.6
  30.1 65.8 %all-to-all-start.1 = ((s32[256,1,2176]{2,1,0:T(1,128)}), s32[256,1,2176]{2,1,0:T(1,128)S(1)}, u32[]{:S(2)}, u32[]{:S(2)}) async-start(s32[256,1,2176]{2,1,0:T(1,128)} %bitcast.13), calls=%async_computation.1 | async-start | bytes 4456448 | tf_op jit(solution)/shard_map/all_to_all | solution.py:287
  40.0 56.0 %copy-start.4 = (s32[2]{0:T(128)}, s32[2]{0:T(128)S(1)}, u32[]{:S(2)}) copy-start(s32[2]{0:T(128)S(1)} %pad_add_fusion.place_ref) | copy-start | bytes 28
  40.7 1.4 %collective-permute-start = (bf16[8,4,16,128]{3,2,1,0:T(8,128)(2,1)S(1)}, bf16[8,4,16,128]{3,2,1,0:T(8,128)(2,1)S(1)}, u32[]{:S(2)}, u32[]{:S(2)}) collective-permute-start(bf16[8,4,16,128]{3,2,1,0:T(8,128)(2,1)S(1)} %get-tuple-element.32), channel_id=1, source_target_pairs={{0,16},{16,0},{32,48},{48,32},{64,80},{80,64},{96,112},{112,96},{1... | collective-permute-start | bytes 393224 | tf_op jit(solution)/shard_map/ppermute | solution.py:293
  42.1 6.7 %collective-permute-start.1 = (bf16[2,4,16,128]{3,2,1,0:T(8,128)(2,1)S(1)}, bf16[2,4,16,128]{3,2,1,0:T(8,128)(2,1)S(1)}, u32[]{:S(2)}, u32[]{:S(2)}) collective-permute-start(bf16[2,4,16,128]{3,2,1,0:T(8,128)(2,1)S(1)} %get-tuple-element.34), channel_id=1, source_target_pairs={{0,32},{16,48},{32,0},{48,16},{64,96},{80,112},{96,64},{112,80},{1... | collective-permute-start | bytes 98312 | tf_op jit(solution)/shard_map/ppermute | solution.py:293
  43.4 11.0 %collective-permute-start.2 = (bf16[2,4,16,128]{3,2,1,0:T(8,128)(2,1)S(1)}, bf16[2,4,16,128]{3,2,1,0:T(8,128)(2,1)S(1)}, u32[]{:S(2)}, u32[]{:S(2)}) collective-permute-start(bf16[2,4,16,128]{3,2,1,0:T(8,128)(2,1)S(1)} %get-tuple-element.35), channel_id=1, source_target_pairs={{0,64},{16,80},{32,96},{48,112},{64,0},{80,16},{96,32},{112,48},{1... | collective-permute-start | bytes 98312 | tf_op jit(solution)/shard_map/ppermute | solution.py:293
  45.8 9.6 %collective-permute-start.3 = (bf16[2,4,16,128]{3,2,1,0:T(8,128)(2,1)S(1)}, bf16[2,4,16,128]{3,2,1,0:T(8,128)(2,1)S(1)}, u32[]{:S(2)}, u32[]{:S(2)}) collective-permute-start(bf16[2,4,16,128]{3,2,1,0:T(8,128)(2,1)S(1)} %get-tuple-element.36), channel_id=1, source_target_pairs={{0,96},{16,112},{32,64},{48,80},{64,32},{80,48},{96,0},{112,16},{1... | collective-permute-start | bytes 98312 | tf_op jit(solution)/shard_map/ppermute | solution.py:293
  46.1 9.4 %collective-permute-start.4 = (bf16[2,4,16,128]{3,2,1,0:T(8,128)(2,1)S(1)}, bf16[2,4,16,128]{3,2,1,0:T(8,128)(2,1)S(1)}, u32[]{:S(2)}, u32[]{:S(2)}) collective-permute-start(bf16[2,4,16,128]{3,2,1,0:T(8,128)(2,1)S(1)} %get-tuple-element.37), channel_id=1, source_target_pairs={{0,128},{16,144},{32,160},{48,176},{64,192},{80,208},{96,224},{112... | collective-permute-start | bytes 98312 | tf_op jit(solution)/shard_map/ppermute | solution.py:293
  47.3 8.1 %collective-permute-start.5 = (bf16[2,4,16,128]{3,2,1,0:T(8,128)(2,1)S(1)}, bf16[2,4,16,128]{3,2,1,0:T(8,128)(2,1)S(1)}, u32[]{:S(2)}, u32[]{:S(2)}) collective-permute-start(bf16[2,4,16,128]{3,2,1,0:T(8,128)(2,1)S(1)} %get-tuple-element.38), channel_id=1, source_target_pairs={{0,160},{16,176},{32,128},{48,144},{64,224},{80,240},{96,192},{112... | collective-permute-start | bytes 98312 | tf_op jit(solution)/shard_map/ppermute | solution.py:293
  48.8 10.8 %collective-permute-start.6 = (bf16[2,4,16,128]{3,2,1,0:T(8,128)(2,1)S(1)}, bf16[2,4,16,128]{3,2,1,0:T(8,128)(2,1)S(1)}, u32[]{:S(2)}, u32[]{:S(2)}) collective-permute-start(bf16[2,4,16,128]{3,2,1,0:T(8,128)(2,1)S(1)} %get-tuple-element.39), channel_id=1, source_target_pairs={{0,192},{16,208},{32,224},{48,240},{64,128},{80,144},{96,160},{112... | collective-permute-start | bytes 98312 | tf_op jit(solution)/shard_map/ppermute | solution.py:293
  54.4 5.5 %collective-permute-start.7 = (bf16[2,4,16,128]{3,2,1,0:T(8,128)(2,1)S(1)}, bf16[2,4,16,128]{3,2,1,0:T(8,128)(2,1)S(1)}, u32[]{:S(2)}, u32[]{:S(2)}) collective-permute-start(bf16[2,4,16,128]{3,2,1,0:T(8,128)(2,1)S(1)} %get-tuple-element.40), channel_id=1, source_target_pairs={{0,224},{16,240},{32,192},{48,208},{64,160},{80,176},{96,128},{112... | collective-permute-start | bytes 98312 | tf_op jit(solution)/shard_map/ppermute | solution.py:293
  61.4 4.2 %collective-permute-start.8 = (bf16[8,8,16,128]{3,2,1,0:T(8,128)(2,1)S(1)}, bf16[8,8,16,128]{3,2,1,0:T(8,128)(2,1)S(1)}, u32[]{:S(2)}, u32[]{:S(2)}) collective-permute-start(bf16[8,8,16,128]{3,2,1,0:T(8,128)(2,1)S(1)} %get-tuple-element.42), channel_id=1, source_target_pairs={{0,16},{16,0},{32,48},{48,32},{64,80},{80,64},{96,112},{112,96},{1... | collective-permute-start | bytes 786440 | tf_op jit(solution)/shard_map/ppermute | solution.py:293
  65.6 0.6 copy-start.2
  66.2 8.0 %collective-permute-start.9 = (bf16[2,8,16,128]{3,2,1,0:T(8,128)(2,1)S(1)}, bf16[2,8,16,128]{3,2,1,0:T(8,128)(2,1)S(1)}, u32[]{:S(2)}, u32[]{:S(2)}) collective-permute-start(bf16[2,8,16,128]{3,2,1,0:T(8,128)(2,1)S(1)} %get-tuple-element.44), channel_id=1, source_target_pairs={{0,32},{16,48},{32,0},{48,16},{64,96},{80,112},{96,64},{112,80},{1... | collective-permute-start | bytes 196616 | tf_op jit(solution)/shard_map/ppermute | solution.py:293
  67.4 10.3 %collective-permute-start.10 = (bf16[2,8,16,128]{3,2,1,0:T(8,128)(2,1)S(1)}, bf16[2,8,16,128]{3,2,1,0:T(8,128)(2,1)S(1)}, u32[]{:S(2)}, u32[]{:S(2)}) collective-permute-start(bf16[2,8,16,128]{3,2,1,0:T(8,128)(2,1)S(1)} %get-tuple-element.45), channel_id=1, source_target_pairs={{0,64},{16,80},{32,96},{48,112},{64,0},{80,16},{96,32},{112,48},{1... | collective-permute-start | bytes 196616 | tf_op jit(solution)/shard_map/ppermute | solution.py:293
  68.4 14.0 %collective-permute-start.11 = (bf16[2,8,16,128]{3,2,1,0:T(8,128)(2,1)S(1)}, bf16[2,8,16,128]{3,2,1,0:T(8,128)(2,1)S(1)}, u32[]{:S(2)}, u32[]{:S(2)}) collective-permute-start(bf16[2,8,16,128]{3,2,1,0:T(8,128)(2,1)S(1)} %get-tuple-element.46), channel_id=1, source_target_pairs={{0,96},{16,112},{32,64},{48,80},{64,32},{80,48},{96,0},{112,16},{1... | collective-permute-start | bytes 196616 | tf_op jit(solution)/shard_map/ppermute | solution.py:293
  70.1 12.4 %collective-permute-start.12 = (bf16[2,8,16,128]{3,2,1,0:T(8,128)(2,1)S(1)}, bf16[2,8,16,128]{3,2,1,0:T(8,128)(2,1)S(1)}, u32[]{:S(2)}, u32[]{:S(2)}) collective-permute-start(bf16[2,8,16,128]{3,2,1,0:T(8,128)(2,1)S(1)} %get-tuple-element.47), channel_id=1, source_target_pairs={{0,128},{16,144},{32,160},{48,176},{64,192},{80,208},{96,224},{112... | collective-permute-start | bytes 196616 | tf_op jit(solution)/shard_map/ppermute | solution.py:293
  71.7 13.6 %collective-permute-start.13 = (bf16[2,8,16,128]{3,2,1,0:T(8,128)(2,1)S(1)}, bf16[2,8,16,128]{3,2,1,0:T(8,128)(2,1)S(1)}, u32[]{:S(2)}, u32[]{:S(2)}) collective-permute-start(bf16[2,8,16,128]{3,2,1,0:T(8,128)(2,1)S(1)} %get-tuple-element.48), channel_id=1, source_target_pairs={{0,160},{16,176},{32,128},{48,144},{64,224},{80,240},{96,192},{112... | collective-permute-start | bytes 196616 | tf_op jit(solution)/shard_map/ppermute | solution.py:293
  74.2 21.8 %copy-start.7 = (bf16[2,8,16,128]{3,2,1,0:T(8,128)(2,1)}, bf16[2,8,16,128]{3,2,1,0:T(8,128)(2,1)S(1)}, u32[]{:S(2)}) copy-start(bf16[2,8,16,128]{3,2,1,0:T(8,128)(2,1)S(1)} %collective-permute-done.9.refs_1_) | copy-start | bytes 196612
  74.2 14.6 %collective-permute-start.14 = (bf16[2,8,16,128]{3,2,1,0:T(8,128)(2,1)S(1)}, bf16[2,8,16,128]{3,2,1,0:T(8,128)(2,1)S(1)}, u32[]{:S(2)}, u32[]{:S(2)}) collective-permute-start(bf16[2,8,16,128]{3,2,1,0:T(8,128)(2,1)S(1)} %get-tuple-element.49), channel_id=1, source_target_pairs={{0,192},{16,208},{32,224},{48,240},{64,128},{80,144},{96,160},{112... | collective-permute-start | bytes 196616 | tf_op jit(solution)/shard_map/ppermute | solution.py:293
  77.7 18.3 %copy-start.8 = (bf16[2,8,16,128]{3,2,1,0:T(8,128)(2,1)}, bf16[2,8,16,128]{3,2,1,0:T(8,128)(2,1)S(1)}, u32[]{:S(2)}) copy-start(bf16[2,8,16,128]{3,2,1,0:T(8,128)(2,1)S(1)} %collective-permute-done.10.refs_2_) | copy-start | bytes 196612
  77.7 11.1 %collective-permute-start.15 = (bf16[2,8,16,128]{3,2,1,0:T(8,128)(2,1)S(1)}, bf16[2,8,16,128]{3,2,1,0:T(8,128)(2,1)S(1)}, u32[]{:S(2)}, u32[]{:S(2)}) collective-permute-start(bf16[2,8,16,128]{3,2,1,0:T(8,128)(2,1)S(1)} %get-tuple-element.50), channel_id=1, source_target_pairs={{0,224},{16,240},{32,192},{48,208},{64,160},{80,176},{96,128},{112... | collective-permute-start | bytes 196616 | tf_op jit(solution)/shard_map/ppermute | solution.py:293
  82.4 13.6 %copy-start.9 = (bf16[2,8,16,128]{3,2,1,0:T(8,128)(2,1)}, bf16[2,8,16,128]{3,2,1,0:T(8,128)(2,1)S(1)}, u32[]{:S(2)}) copy-start(bf16[2,8,16,128]{3,2,1,0:T(8,128)(2,1)S(1)} %collective-permute-done.11.refs_3_) | copy-start | bytes 196612
  82.5 13.6 %copy-start.10 = (bf16[2,8,16,128]{3,2,1,0:T(8,128)(2,1)}, bf16[2,8,16,128]{3,2,1,0:T(8,128)(2,1)S(1)}, u32[]{:S(2)}) copy-start(bf16[2,8,16,128]{3,2,1,0:T(8,128)(2,1)S(1)} %collective-permute-done.12.refs_4_) | copy-start | bytes 196612
  85.3 10.7 %copy-start.11 = (bf16[2,8,16,128]{3,2,1,0:T(8,128)(2,1)}, bf16[2,8,16,128]{3,2,1,0:T(8,128)(2,1)S(1)}, u32[]{:S(2)}) copy-start(bf16[2,8,16,128]{3,2,1,0:T(8,128)(2,1)S(1)} %collective-permute-done.13.refs_5_) | copy-start | bytes 196612
  88.8 7.3 %copy-start.12 = (bf16[2,8,16,128]{3,2,1,0:T(8,128)(2,1)}, bf16[2,8,16,128]{3,2,1,0:T(8,128)(2,1)S(1)}, u32[]{:S(2)}) copy-start(bf16[2,8,16,128]{3,2,1,0:T(8,128)(2,1)S(1)} %collective-permute-done.14.refs_6_) | copy-start | bytes 196612
  88.8 7.3 %copy-start.13 = (bf16[2,8,16,128]{3,2,1,0:T(8,128)(2,1)}, bf16[2,8,16,128]{3,2,1,0:T(8,128)(2,1)S(1)}, u32[]{:S(2)}) copy-start(bf16[2,8,16,128]{3,2,1,0:T(8,128)(2,1)S(1)} %collective-permute-done.15.refs_7_) | copy-start | bytes 196612
  96.0 1.4 %copy-start.5 = (s32[256,1,2176]{2,1,0:T(1,128)}, s32[256,1,2176]{2,1,0:T(1,128)S(1)}, u32[]{:S(2)}) copy-start(s32[256,1,2176]{2,1,0:T(1,128)S(1)} %all-to-all-done.1) | copy-start | bytes 6684676
Sparse Core Ops, SparseCore 0:
  30.3 65.2 all-gather.1

commit v4 on v3

--- a/solution.py
+++ b/solution.py
@@ -105,7 +105,8 @@
     quads = chan_count // 4
 
     def fetch_words(block):
-        return pltpu.make_async_copy(words_ref.at[block], words.at[block], word_sems.at[block])
+        there = words.at[block, pl.ds(0, words_ref.shape[1])]
+        return pltpu.make_async_copy(words_ref.at[block], there, word_sems.at[block])
 
     def fetch_slabs(chip):
         return pltpu.make_async_copy(fringe_refs[chip], slabs.at[chip], slab_sems.at[chip])
@@ -175,7 +176,7 @@
             fetch_slabs(chip).wait()
 
     unpack()
-    count = samples.shape[2] // SUB
+    count = results.shape[2]
 
     def over_time(baseline):
         parts = []
@@ -343,9 +344,9 @@
             in_specs=[pl.BlockSpec(memory_space=pltpu.HBM)] * 2 + [pl.BlockSpec(memory_space=pl.ANY)] * chips,
             out_specs=pl.BlockSpec(memory_space=pl.ANY),
             scratch_shapes=[
-                pltpu.VMEM((time_count, chan_count * rows, LANES), jnp.int32),
+                pltpu.VMEM((time_count, chan_count * rows + LANES // SUB, LANES), jnp.int32),
                 pltpu.VMEM((LANES, LANES), jnp.float32),
-                pltpu.VMEM((2, all_chans // LANES, all_times * SUB, LANES), jnp.float32),
+                pltpu.VMEM((2, all_chans // LANES, all_times * SUB + SUB, LANES), jnp.float32),
                 pltpu.VMEM((chips, CORES, own, slab, all_times), jnp.bfloat16),
                 pltpu.VMEM((time_count, slab, all_times), jnp.bfloat16),
                 pltpu.VMEM((own, pieces, all_chans, wide), jnp.bfloat16),

time: 118 us -> 118 us (level)
  no operation moved by 1% of the time
where the time goes in v4:
time: 118 us; the launch traced here: 117 us
  starting transfers between devices  46.2 us (39%)
  waiting for transfers between devices  33 us (28%)
  Pallas kernels  19.9 us (17%)
  between operations  13.6 us (12%)
  local copies, waits for them, and re-layouts  4.39 us (4%)
    ppermute x16, starting transfers between devices, crossed(): lax.ppermute(array, 'tm', [(k, k ^ mask) for k in range(time_count)])  25.7 us
    ppermute x16, waiting for transfers between devices, crossed(): lax.ppermute(array, 'tm', [(k, k ^ mask) for k in range(time_count)])  20.2 us
    pallas_call x1, Pallas kernels, shards(): pl.pallas_call(functools.partial(filter_kernel, rows=rows, spread=spread)...  12.9 us
    all_to_all x1, starting transfers between devices, shards(): lax.all_to_all(jnp.broadcast_to(share, (chan_count, chans, wide)), 'chan'...  10.7 us
    all_to_all x1, starting transfers between devices, shards(): lax.all_to_all(packed.reshape(devices, 1, rows * LANES), everyone, split_...  9.78 us
    all_to_all x1, waiting for transfers between devices, shards(): lax.all_to_all(packed.reshape(devices, 1, rows * LANES), everyone, split_...  7.2 us
    all_to_all x1, waiting for transfers between devices, shards(): lax.all_to_all(jnp.broadcast_to(share, (chan_count, chans, wide)), 'chan'...  5.63 us
    pallas_call x1, Pallas kernels, shards(): pl.pallas_call(functools.partial(pack_kernel, rows=rows), in_specs=[far,...  4.81 us
  transfers between devices with their start and end apart: 19, of which 12 were waited for; matrix products, arithmetic and copies ran while one was open for 0% of the time, Pallas kernels for 6%

profile of v4, /device:TPU:33, one launch (start us, length us, event | category | flops | bytes accessed | tf_op | source)
XLA Modules:
  0.0 117.2 jit_solution(15790436962344521815)
XLA Ops:
  6.5 0.0 copy-start
  6.5 0.9 copy-done
  7.5 0.7 broadcast_in_dim.8
  8.2 10.7 %all-to-all-start = ((bf16[16,32,256]{2,1,0:T(8,128)(2,1)}), bf16[16,32,256]{2,1,0:T(8,128)(2,1)S(1)}, u32[]{:S(2)}, u32[]{:S(2)}) async-start(bf16[16,32,256]{2,1,0:T(8,128)(2,1)} %broadcast_in_dim.8), calls=%async_computation | async-start | bytes 524288 | tf_op jit(solution)/shard_map/all_to_all | solution.py:261
  18.9 0.0 all-gather.2.cloned.1.call-start
  18.9 0.0 copy-start.1
  18.9 4.8 %pack.1 = s32[4352,128]{1,0:T(8,128)} custom-call(f32[2,8,32,2048]{3,2,1,0:T(8,128)} %bitcast.15, s32[32,2048]{1,0:T(8,128)} %bitcast.17), custom_call_target="tpu_custom_call" | custom-call | tf_op jit(solution)/shard_map/pack/pallas_call | solution.py:269
  23.8 0.0 copy-start.3
  23.8 5.6 %all-to-all-done = bf16[16,32,256]{2,1,0:T(8,128)(2,1)S(1)} async-done(((bf16[16,32,256]{2,1,0:T(8,128)(2,1)}), bf16[16,32,256]{2,1,0:T(8,128)(2,1)S(1)}, u32[]{:S(2)}, u32[]{:S(2)}) %all-to-all-start) | async-done | bytes 262176 | tf_op jit(solution)/shard_map/all_to_all | solution.py:261
  29.4 0.0 copy-start.6
  29.4 0.7 copy-done.6
  30.1 0.0 all-gather.2.cloned.1.call-update
  30.1 9.8 %all-to-all-start.1 = ((s32[256,1,2176]{2,1,0:T(1,128)}), s32[256,1,2176]{2,1,0:T(1,128)S(1)}, u32[]{:S(2)}, u32[]{:S(2)}) async-start(s32[256,1,2176]{2,1,0:T(1,128)} %bitcast.13), calls=%async_computation.1 | async-start | bytes 4456448 | tf_op jit(solution)/shard_map/all_to_all | solution.py:288
  39.9 0.1 pad_add_fusion.place_ref
  40.0 0.0 copy-done.1
  40.0 0.6 shares.1
  40.7 0.4 collective-permute-start
  41.1 1.0 collective-permute-done.refs_1_
  42.1 1.3 %collective-permute-start.1 = (bf16[2,4,16,128]{3,2,1,0:T(8,128)(2,1)S(1)}, bf16[2,4,16,128]{3,2,1,0:T(8,128)(2,1)S(1)}, u32[]{:S(2)}, u32[]{:S(2)}) collective-permute-start(bf16[2,4,16,128]{3,2,1,0:T(8,128)(2,1)S(1)} %get-tuple-element.34), channel_id=1, source_target_pairs={{0,32},{16,48},{32,0},{48,16},{64,96},{80,112},{96,64},{112,80},{1... | collective-permute-start | bytes 98312 | tf_op jit(solution)/shard_map/ppermute | solution.py:294
  43.4 2.4 %collective-permute-start.2 = (bf16[2,4,16,128]{3,2,1,0:T(8,128)(2,1)S(1)}, bf16[2,4,16,128]{3,2,1,0:T(8,128)(2,1)S(1)}, u32[]{:S(2)}, u32[]{:S(2)}) collective-permute-start(bf16[2,4,16,128]{3,2,1,0:T(8,128)(2,1)S(1)} %get-tuple-element.35), channel_id=1, source_target_pairs={{0,64},{16,80},{32,96},{48,112},{64,0},{80,16},{96,32},{112,48},{1... | collective-permute-start | bytes 98312 | tf_op jit(solution)/shard_map/ppermute | solution.py:294
  45.8 0.2 collective-permute-start.3
  46.1 1.2 %collective-permute-start.4 = (bf16[2,4,16,128]{3,2,1,0:T(8,128)(2,1)S(1)}, bf16[2,4,16,128]{3,2,1,0:T(8,128)(2,1)S(1)}, u32[]{:S(2)}, u32[]{:S(2)}) collective-permute-start(bf16[2,4,16,128]{3,2,1,0:T(8,128)(2,1)S(1)} %get-tuple-element.37), channel_id=1, source_target_pairs={{0,128},{16,144},{32,160},{48,176},{64,192},{80,208},{96,224},{112... | collective-permute-start | bytes 98312 | tf_op jit(solution)/shard_map/ppermute | solution.py:294
  47.3 0.0 collective-permute-start.5
  47.3 1.5 %collective-permute-done.1.refs_1_ = bf16[2,4,16,128]{3,2,1,0:T(8,128)(2,1)S(1)} collective-permute-done((bf16[2,4,16,128]{3,2,1,0:T(8,128)(2,1)S(1)}, bf16[2,4,16,128]{3,2,1,0:T(8,128)(2,1)S(1)}, u32[]{:S(2)}, u32[]{:S(2)}) %collective-permute-start.1) | collective-permute-done | bytes 32800 | tf_op jit(solution)/shard_map/ppermute | solution.py:294
  48.8 3.5 %collective-permute-start.6 = (bf16[2,4,16,128]{3,2,1,0:T(8,128)(2,1)S(1)}, bf16[2,4,16,128]{3,2,1,0:T(8,128)(2,1)S(1)}, u32[]{:S(2)}, u32[]{:S(2)}) collective-permute-start(bf16[2,4,16,128]{3,2,1,0:T(8,128)(2,1)S(1)} %get-tuple-element.39), channel_id=1, source_target_pairs={{0,192},{16,208},{32,224},{48,240},{64,128},{80,144},{96,160},{112... | collective-permute-start | bytes 98312 | tf_op jit(solution)/shard_map/ppermute | solution.py:294
  52.3 2.1 %collective-permute-done.2.refs_2_ = bf16[2,4,16,128]{3,2,1,0:T(8,128)(2,1)S(1)} collective-permute-done((bf16[2,4,16,128]{3,2,1,0:T(8,128)(2,1)S(1)}, bf16[2,4,16,128]{3,2,1,0:T(8,128)(2,1)S(1)}, u32[]{:S(2)}, u32[]{:S(2)}) %collective-permute-start.2) | collective-permute-done | bytes 32800 | tf_op jit(solution)/shard_map/ppermute | solution.py:294
  54.4 1.1 collective-permute-start.7
  55.4 0.0 collective-permute-done.3.refs_3_
  55.5 0.0 collective-permute-done.4.refs_4_
  55.5 0.0 collective-permute-done.5.refs_5_
  55.5 4.1 %collective-permute-done.6.refs_6_ = bf16[2,4,16,128]{3,2,1,0:T(8,128)(2,1)S(1)} collective-permute-done((bf16[2,4,16,128]{3,2,1,0:T(8,128)(2,1)S(1)}, bf16[2,4,16,128]{3,2,1,0:T(8,128)(2,1)S(1)}, u32[]{:S(2)}, u32[]{:S(2)}) %collective-permute-start.6) | collective-permute-done | bytes 32800 | tf_op jit(solution)/shard_map/ppermute | solution.py:294
  59.6 0.3 collective-permute-done.7.refs_7_
  59.9 0.0 copy-done.3
  59.9 1.5 %select.7 = (bf16[8,8,16,128]{3,2,1,0:T(8,128)(2,1)S(1)}, bf16[8,8,16,128]{3,2,1,0:T(8,128)(2,1)S(1)}) custom-call(s32[2048]{0:T(1024)S(1)} %copy-done.3, s32[2]{0:T(128)S(1)} %pad_add_fusion.place_ref, bf16[2,4,16,128]{3,2,1,0:T(8,128)(2,1)S(1)} %get-tuple-element.33.refs_0_, bf16[2,4,16,128]{3,2,1,0:T(8,128)(2,1)S(1)} %collective-permute-done.1.refs_1_, ...), custom_call_target="tpu_custom_call" | custom-call | tf_op jit(solution)/shard_map/select/pallas_call | solution.py:322
  61.4 3.0 %collective-permute-start.8 = (bf16[8,8,16,128]{3,2,1,0:T(8,128)(2,1)S(1)}, bf16[8,8,16,128]{3,2,1,0:T(8,128)(2,1)S(1)}, u32[]{:S(2)}, u32[]{:S(2)}) collective-permute-start(bf16[8,8,16,128]{3,2,1,0:T(8,128)(2,1)S(1)} %get-tuple-element.42), channel_id=1, source_target_pairs={{0,16},{16,0},{32,48},{48,32},{64,80},{80,64},{96,112},{112,96},{1... | collective-permute-start | bytes 786440 | tf_op jit(solution)/shard_map/ppermute | solution.py:294
  64.4 1.2 collective-permute-done.8.refs_1_
  65.6 0.0 copy-start.2
  65.6 0.6 copy-done.2
  66.2 1.2 %collective-permute-start.9 = (bf16[2,8,16,128]{3,2,1,0:T(8,128)(2,1)S(1)}, bf16[2,8,16,128]{3,2,1,0:T(8,128)(2,1)S(1)}, u32[]{:S(2)}, u32[]{:S(2)}) collective-permute-start(bf16[2,8,16,128]{3,2,1,0:T(8,128)(2,1)S(1)} %get-tuple-element.44), channel_id=1, source_target_pairs={{0,32},{16,48},{32,0},{48,16},{64,96},{80,112},{96,64},{112,80},{1... | collective-permute-start | bytes 196616 | tf_op jit(solution)/shard_map/ppermute | solution.py:294
  67.4 1.0 collective-permute-start.10
  68.4 1.6 %collective-permute-start.11 = (bf16[2,8,16,128]{3,2,1,0:T(8,128)(2,1)S(1)}, bf16[2,8,16,128]{3,2,1,0:T(8,128)(2,1)S(1)}, u32[]{:S(2)}, u32[]{:S(2)}) collective-permute-start(bf16[2,8,16,128]{3,2,1,0:T(8,128)(2,1)S(1)} %get-tuple-element.46), channel_id=1, source_target_pairs={{0,96},{16,112},{32,64},{48,80},{64,32},{80,48},{96,0},{112,16},{1... | collective-permute-start | bytes 196616 | tf_op jit(solution)/shard_map/ppermute | solution.py:294
  70.1 1.6 %collective-permute-start.12 = (bf16[2,8,16,128]{3,2,1,0:T(8,128)(2,1)S(1)}, bf16[2,8,16,128]{3,2,1,0:T(8,128)(2,1)S(1)}, u32[]{:S(2)}, u32[]{:S(2)}) collective-permute-start(bf16[2,8,16,128]{3,2,1,0:T(8,128)(2,1)S(1)} %get-tuple-element.47), channel_id=1, source_target_pairs={{0,128},{16,144},{32,160},{48,176},{64,192},{80,208},{96,224},{112... | collective-permute-start | bytes 196616 | tf_op jit(solution)/shard_map/ppermute | solution.py:294
  71.7 0.0 collective-permute-start.13
  71.7 2.5 %collective-permute-done.9.refs_1_ = bf16[2,8,16,128]{3,2,1,0:T(8,128)(2,1)S(1)} collective-permute-done((bf16[2,8,16,128]{3,2,1,0:T(8,128)(2,1)S(1)}, bf16[2,8,16,128]{3,2,1,0:T(8,128)(2,1)S(1)}, u32[]{:S(2)}, u32[]{:S(2)}) %collective-permute-start.9) | collective-permute-done | bytes 65568 | tf_op jit(solution)/shard_map/ppermute | solution.py:294
  74.2 2.3 %collective-permute-start.14 = (bf16[2,8,16,128]{3,2,1,0:T(8,128)(2,1)S(1)}, bf16[2,8,16,128]{3,2,1,0:T(8,128)(2,1)S(1)}, u32[]{:S(2)}, u32[]{:S(2)}) collective-permute-start(bf16[2,8,16,128]{3,2,1,0:T(8,128)(2,1)S(1)} %get-tuple-element.49), channel_id=1, source_target_pairs={{0,192},{16,208},{32,224},{48,240},{64,128},{80,144},{96,160},{112... | collective-permute-start | bytes 196616 | tf_op jit(solution)/shard_map/ppermute | solution.py:294
  76.5 1.3 %collective-permute-done.10.refs_2_ = bf16[2,8,16,128]{3,2,1,0:T(8,128)(2,1)S(1)} collective-permute-done((bf16[2,8,16,128]{3,2,1,0:T(8,128)(2,1)S(1)}, bf16[2,8,16,128]{3,2,1,0:T(8,128)(2,1)S(1)}, u32[]{:S(2)}, u32[]{:S(2)}) %collective-permute-start.10) | collective-permute-done | bytes 65568 | tf_op jit(solution)/shard_map/ppermute | solution.py:294
  77.7 4.7 %collective-permute-start.15 = (bf16[2,8,16,128]{3,2,1,0:T(8,128)(2,1)S(1)}, bf16[2,8,16,128]{3,2,1,0:T(8,128)(2,1)S(1)}, u32[]{:S(2)}, u32[]{:S(2)}) collective-permute-start(bf16[2,8,16,128]{3,2,1,0:T(8,128)(2,1)S(1)} %get-tuple-element.50), channel_id=1, source_target_pairs={{0,224},{16,240},{32,192},{48,208},{64,160},{80,176},{96,128},{112... | collective-permute-start | bytes 196616 | tf_op jit(solution)/shard_map/ppermute | solution.py:294
  82.4 0.0 collective-permute-done.11.refs_3_
  82.4 0.0 collective-permute-done.12.refs_4_
  82.5 0.0 copy-start.10
  82.5 2.8 %collective-permute-done.13.refs_5_ = bf16[2,8,16,128]{3,2,1,0:T(8,128)(2,1)S(1)} collective-permute-done((bf16[2,8,16,128]{3,2,1,0:T(8,128)(2,1)S(1)}, bf16[2,8,16,128]{3,2,1,0:T(8,128)(2,1)S(1)}, u32[]{:S(2)}, u32[]{:S(2)}) %collective-permute-start.13) | collective-permute-done | bytes 65568 | tf_op jit(solution)/shard_map/ppermute | solution.py:294
  85.3 3.5 %collective-permute-done.14.refs_6_ = bf16[2,8,16,128]{3,2,1,0:T(8,128)(2,1)S(1)} collective-permute-done((bf16[2,8,16,128]{3,2,1,0:T(8,128)(2,1)S(1)}, bf16[2,8,16,128]{3,2,1,0:T(8,128)(2,1)S(1)}, u32[]{:S(2)}, u32[]{:S(2)}) %collective-permute-start.14) | collective-permute-done | bytes 65568 | tf_op jit(solution)/shard_map/ppermute | solution.py:294
  88.8 0.0 collective-permute-done.15.refs_7_
  88.8 7.2 %all-to-all-done.1 = s32[256,1,2176]{2,1,0:T(1,128)S(1)} async-done(((s32[256,1,2176]{2,1,0:T(1,128)}), s32[256,1,2176]{2,1,0:T(1,128)S(1)}, u32[]{:S(2)}, u32[]{:S(2)}) %all-to-all-start.1) | async-done | bytes 2228256 | tf_op jit(solution)/shard_map/all_to_all | solution.py:288
  96.0 0.0 copy-done.4
  96.0 0.0 copy-done.7
  96.0 0.0 copy-done.8
  96.0 0.0 copy-done.9
  96.0 0.0 copy-done.10
  96.0 0.0 copy-done.11
  96.0 0.0 copy-done.12
  96.0 0.0 copy-done.13
  96.0 1.3 %copy-done.5 = s32[256,1,2176]{2,1,0:T(1,128)} copy-done((s32[256,1,2176]{2,1,0:T(1,128)}, s32[256,1,2176]{2,1,0:T(1,128)S(1)}, u32[]{:S(2)}) %copy-start.5) | copy-done | bytes 2228248
  97.4 12.9 %filter.1 = f32[2,8,128,512]{3,2,1,0:T(8,128)} custom-call(s32[2048]{0:T(1024)} %groups_ref.3, s32[2]{0:T(128)} %copy-done.4, s32[16,272,128]{2,1,0:T(8,128)} %bitcast.12, bf16[8,2,512,256]{3,2,1,0:T(8,128)(2,1)} %bitcast.14, bf16[2,8,16,128]{3,2,1,0:T(8,128)(2,1)} %copy-done.2, bf16[2,8,16,128]{3,2,1,0:T(8,128)(2,1)} %copy-done.7, ...), custom_call_target="tpu_custom_call" | custom-call | tf_op jit(solution)/shard_map/filter/pallas_call | solution.py:339
  (12 shorter events, 0.1 us)
Async XLA Ops:
  6.5 1.0 copy-start
  8.2 21.2 %all-to-all-start = ((bf16[16,32,256]{2,1,0:T(8,128)(2,1)}), bf16[16,32,256]{2,1,0:T(8,128)(2,1)S(1)}, u32[]{:S(2)}, u32[]{:S(2)}) async-start(bf16[16,32,256]{2,1,0:T(8,128)(2,1)} %broadcast_in_dim.8), calls=%async_computation | async-start | bytes 524288 | tf_op jit(solution)/shard_map/all_to_all | solution.py:261
  18.9 77.1 %all-gather.2.cloned.1.call-start = ((), (), s32[]{:S(2)}) async-start(), calls=%async_computation.2 | async-start | bytes 4456448 | tf_op jit(solution)/shard_map/all_gather | solution.py:286
  18.9 21.1 %copy-start.1 = (bf16[2,4,128,128]{3,2,1,0:T(8,128)(2,1)S(1)}, bf16[2,4,128,128]{3,2,1,0:T(8,128)(2,1)}, u32[]{:S(2)}) copy-start(bf16[2,4,128,128]{3,2,1,0:T(8,128)(2,1)} %param.8) | copy-start | bytes 786436
  23.8 36.1 %copy-start.3 = (s32[2048]{0:T(1024)S(1)}, s32[2048]{0:T(1024)}, u32[]{:S(2)}) copy-start(s32[2048]{0:T(1024)} %groups_ref.3) | copy-start | bytes 24580
  29.4 0.7 copy-start.6
  30.1 65.8 %all-to-all-start.1 = ((s32[256,1,2176]{2,1,0:T(1,128)}), s32[256,1,2176]{2,1,0:T(1,128)S(1)}, u32[]{:S(2)}, u32[]{:S(2)}) async-start(s32[256,1,2176]{2,1,0:T(1,128)} %bitcast.13), calls=%async_computation.1 | async-start | bytes 4456448 | tf_op jit(solution)/shard_map/all_to_all | solution.py:288
  40.0 56.0 %copy-start.4 = (s32[2]{0:T(128)}, s32[2]{0:T(128)S(1)}, u32[]{:S(2)}) copy-start(s32[2]{0:T(128)S(1)} %pad_add_fusion.place_ref) | copy-start | bytes 28
  40.7 1.4 %collective-permute-start = (bf16[8,4,16,128]{3,2,1,0:T(8,128)(2,1)S(1)}, bf16[8,4,16,128]{3,2,1,0:T(8,128)(2,1)S(1)}, u32[]{:S(2)}, u32[]{:S(2)}) collective-permute-start(bf16[8,4,16,128]{3,2,1,0:T(8,128)(2,1)S(1)} %get-tuple-element.32), channel_id=1, source_target_pairs={{0,16},{16,0},{32,48},{48,32},{64,80},{80,64},{96,112},{112,96},{1... | collective-permute-start | bytes 393224 | tf_op jit(solution)/shard_map/ppermute | solution.py:294
  42.1 6.7 %collective-permute-start.1 = (bf16[2,4,16,128]{3,2,1,0:T(8,128)(2,1)S(1)}, bf16[2,4,16,128]{3,2,1,0:T(8,128)(2,1)S(1)}, u32[]{:S(2)}, u32[]{:S(2)}) collective-permute-start(bf16[2,4,16,128]{3,2,1,0:T(8,128)(2,1)S(1)} %get-tuple-element.34), channel_id=1, source_target_pairs={{0,32},{16,48},{32,0},{48,16},{64,96},{80,112},{96,64},{112,80},{1... | collective-permute-start | bytes 98312 | tf_op jit(solution)/shard_map/ppermute | solution.py:294
  43.4 11.0 %collective-permute-start.2 = (bf16[2,4,16,128]{3,2,1,0:T(8,128)(2,1)S(1)}, bf16[2,4,16,128]{3,2,1,0:T(8,128)(2,1)S(1)}, u32[]{:S(2)}, u32[]{:S(2)}) collective-permute-start(bf16[2,4,16,128]{3,2,1,0:T(8,128)(2,1)S(1)} %get-tuple-element.35), channel_id=1, source_target_pairs={{0,64},{16,80},{32,96},{48,112},{64,0},{80,16},{96,32},{112,48},{1... | collective-permute-start | bytes 98312 | tf_op jit(solution)/shard_map/ppermute | solution.py:294
  45.8 9.6 %collective-permute-start.3 = (bf16[2,4,16,128]{3,2,1,0:T(8,128)(2,1)S(1)}, bf16[2,4,16,128]{3,2,1,0:T(8,128)(2,1)S(1)}, u32[]{:S(2)}, u32[]{:S(2)}) collective-permute-start(bf16[2,4,16,128]{3,2,1,0:T(8,128)(2,1)S(1)} %get-tuple-element.36), channel_id=1, source_target_pairs={{0,96},{16,112},{32,64},{48,80},{64,32},{80,48},{96,0},{112,16},{1... | collective-permute-start | bytes 98312 | tf_op jit(solution)/shard_map/ppermute | solution.py:294
  46.1 9.4 %collective-permute-start.4 = (bf16[2,4,16,128]{3,2,1,0:T(8,128)(2,1)S(1)}, bf16[2,4,16,128]{3,2,1,0:T(8,128)(2,1)S(1)}, u32[]{:S(2)}, u32[]{:S(2)}) collective-permute-start(bf16[2,4,16,128]{3,2,1,0:T(8,128)(2,1)S(1)} %get-tuple-element.37), channel_id=1, source_target_pairs={{0,128},{16,144},{32,160},{48,176},{64,192},{80,208},{96,224},{112... | collective-permute-start | bytes 98312 | tf_op jit(solution)/shard_map/ppermute | solution.py:294
  47.3 8.1 %collective-permute-start.5 = (bf16[2,4,16,128]{3,2,1,0:T(8,128)(2,1)S(1)}, bf16[2,4,16,128]{3,2,1,0:T(8,128)(2,1)S(1)}, u32[]{:S(2)}, u32[]{:S(2)}) collective-permute-start(bf16[2,4,16,128]{3,2,1,0:T(8,128)(2,1)S(1)} %get-tuple-element.38), channel_id=1, source_target_pairs={{0,160},{16,176},{32,128},{48,144},{64,224},{80,240},{96,192},{112... | collective-permute-start | bytes 98312 | tf_op jit(solution)/shard_map/ppermute | solution.py:294
  48.8 10.8 %collective-permute-start.6 = (bf16[2,4,16,128]{3,2,1,0:T(8,128)(2,1)S(1)}, bf16[2,4,16,128]{3,2,1,0:T(8,128)(2,1)S(1)}, u32[]{:S(2)}, u32[]{:S(2)}) collective-permute-start(bf16[2,4,16,128]{3,2,1,0:T(8,128)(2,1)S(1)} %get-tuple-element.39), channel_id=1, source_target_pairs={{0,192},{16,208},{32,224},{48,240},{64,128},{80,144},{96,160},{112... | collective-permute-start | bytes 98312 | tf_op jit(solution)/shard_map/ppermute | solution.py:294
  54.4 5.5 %collective-permute-start.7 = (bf16[2,4,16,128]{3,2,1,0:T(8,128)(2,1)S(1)}, bf16[2,4,16,128]{3,2,1,0:T(8,128)(2,1)S(1)}, u32[]{:S(2)}, u32[]{:S(2)}) collective-permute-start(bf16[2,4,16,128]{3,2,1,0:T(8,128)(2,1)S(1)} %get-tuple-element.40), channel_id=1, source_target_pairs={{0,224},{16,240},{32,192},{48,208},{64,160},{80,176},{96,128},{112... | collective-permute-start | bytes 98312 | tf_op jit(solution)/shard_map/ppermute | solution.py:294
  61.4 4.2 %collective-permute-start.8 = (bf16[8,8,16,128]{3,2,1,0:T(8,128)(2,1)S(1)}, bf16[8,8,16,128]{3,2,1,0:T(8,128)(2,1)S(1)}, u32[]{:S(2)}, u32[]{:S(2)}) collective-permute-start(bf16[8,8,16,128]{3,2,1,0:T(8,128)(2,1)S(1)} %get-tuple-element.42), channel_id=1, source_target_pairs={{0,16},{16,0},{32,48},{48,32},{64,80},{80,64},{96,112},{112,96},{1... | collective-permute-start | bytes 786440 | tf_op jit(solution)/shard_map/ppermute | solution.py:294
  65.6 0.6 copy-start.2
  66.2 8.0 %collective-permute-start.9 = (bf16[2,8,16,128]{3,2,1,0:T(8,128)(2,1)S(1)}, bf16[2,8,16,128]{3,2,1,0:T(8,128)(2,1)S(1)}, u32[]{:S(2)}, u32[]{:S(2)}) collective-permute-start(bf16[2,8,16,128]{3,2,1,0:T(8,128)(2,1)S(1)} %get-tuple-element.44), channel_id=1, source_target_pairs={{0,32},{16,48},{32,0},{48,16},{64,96},{80,112},{96,64},{112,80},{1... | collective-permute-start | bytes 196616 | tf_op jit(solution)/shard_map/ppermute | solution.py:294
  67.4 10.3 %collective-permute-start.10 = (bf16[2,8,16,128]{3,2,1,0:T(8,128)(2,1)S(1)}, bf16[2,8,16,128]{3,2,1,0:T(8,128)(2,1)S(1)}, u32[]{:S(2)}, u32[]{:S(2)}) collective-permute-start(bf16[2,8,16,128]{3,2,1,0:T(8,128)(2,1)S(1)} %get-tuple-element.45), channel_id=1, source_target_pairs={{0,64},{16,80},{32,96},{48,112},{64,0},{80,16},{96,32},{112,48},{1... | collective-permute-start | bytes 196616 | tf_op jit(solution)/shard_map/ppermute | solution.py:294
  68.4 14.0 %collective-permute-start.11 = (bf16[2,8,16,128]{3,2,1,0:T(8,128)(2,1)S(1)}, bf16[2,8,16,128]{3,2,1,0:T(8,128)(2,1)S(1)}, u32[]{:S(2)}, u32[]{:S(2)}) collective-permute-start(bf16[2,8,16,128]{3,2,1,0:T(8,128)(2,1)S(1)} %get-tuple-element.46), channel_id=1, source_target_pairs={{0,96},{16,112},{32,64},{48,80},{64,32},{80,48},{96,0},{112,16},{1... | collective-permute-start | bytes 196616 | tf_op jit(solution)/shard_map/ppermute | solution.py:294
  70.1 12.4 %collective-permute-start.12 = (bf16[2,8,16,128]{3,2,1,0:T(8,128)(2,1)S(1)}, bf16[2,8,16,128]{3,2,1,0:T(8,128)(2,1)S(1)}, u32[]{:S(2)}, u32[]{:S(2)}) collective-permute-start(bf16[2,8,16,128]{3,2,1,0:T(8,128)(2,1)S(1)} %get-tuple-element.47), channel_id=1, source_target_pairs={{0,128},{16,144},{32,160},{48,176},{64,192},{80,208},{96,224},{112... | collective-permute-start | bytes 196616 | tf_op jit(solution)/shard_map/ppermute | solution.py:294
  71.7 13.6 %collective-permute-start.13 = (bf16[2,8,16,128]{3,2,1,0:T(8,128)(2,1)S(1)}, bf16[2,8,16,128]{3,2,1,0:T(8,128)(2,1)S(1)}, u32[]{:S(2)}, u32[]{:S(2)}) collective-permute-start(bf16[2,8,16,128]{3,2,1,0:T(8,128)(2,1)S(1)} %get-tuple-element.48), channel_id=1, source_target_pairs={{0,160},{16,176},{32,128},{48,144},{64,224},{80,240},{96,192},{112... | collective-permute-start | bytes 196616 | tf_op jit(solution)/shard_map/ppermute | solution.py:294
  74.2 21.8 %copy-start.7 = (bf16[2,8,16,128]{3,2,1,0:T(8,128)(2,1)}, bf16[2,8,16,128]{3,2,1,0:T(8,128)(2,1)S(1)}, u32[]{:S(2)}) copy-start(bf16[2,8,16,128]{3,2,1,0:T(8,128)(2,1)S(1)} %collective-permute-done.9.refs_1_) | copy-start | bytes 196612
  74.2 14.6 %collective-permute-start.14 = (bf16[2,8,16,128]{3,2,1,0:T(8,128)(2,1)S(1)}, bf16[2,8,16,128]{3,2,1,0:T(8,128)(2,1)S(1)}, u32[]{:S(2)}, u32[]{:S(2)}) collective-permute-start(bf16[2,8,16,128]{3,2,1,0:T(8,128)(2,1)S(1)} %get-tuple-element.49), channel_id=1, source_target_pairs={{0,192},{16,208},{32,224},{48,240},{64,128},{80,144},{96,160},{112... | collective-permute-start | bytes 196616 | tf_op jit(solution)/shard_map/ppermute | solution.py:294
  77.7 18.3 %copy-start.8 = (bf16[2,8,16,128]{3,2,1,0:T(8,128)(2,1)}, bf16[2,8,16,128]{3,2,1,0:T(8,128)(2,1)S(1)}, u32[]{:S(2)}) copy-start(bf16[2,8,16,128]{3,2,1,0:T(8,128)(2,1)S(1)} %collective-permute-done.10.refs_2_) | copy-start | bytes 196612
  77.7 11.1 %collective-permute-start.15 = (bf16[2,8,16,128]{3,2,1,0:T(8,128)(2,1)S(1)}, bf16[2,8,16,128]{3,2,1,0:T(8,128)(2,1)S(1)}, u32[]{:S(2)}, u32[]{:S(2)}) collective-permute-start(bf16[2,8,16,128]{3,2,1,0:T(8,128)(2,1)S(1)} %get-tuple-element.50), channel_id=1, source_target_pairs={{0,224},{16,240},{32,192},{48,208},{64,160},{80,176},{96,128},{112... | collective-permute-start | bytes 196616 | tf_op jit(solution)/shard_map/ppermute | solution.py:294
  82.4 13.6 %copy-start.9 = (bf16[2,8,16,128]{3,2,1,0:T(8,128)(2,1)}, bf16[2,8,16,128]{3,2,1,0:T(8,128)(2,1)S(1)}, u32[]{:S(2)}) copy-start(bf16[2,8,16,128]{3,2,1,0:T(8,128)(2,1)S(1)} %collective-permute-done.11.refs_3_) | copy-start | bytes 196612
  82.5 13.6 %copy-start.10 = (bf16[2,8,16,128]{3,2,1,0:T(8,128)(2,1)}, bf16[2,8,16,128]{3,2,1,0:T(8,128)(2,1)S(1)}, u32[]{:S(2)}) copy-start(bf16[2,8,16,128]{3,2,1,0:T(8,128)(2,1)S(1)} %collective-permute-done.12.refs_4_) | copy-start | bytes 196612
  85.3 10.7 %copy-start.11 = (bf16[2,8,16,128]{3,2,1,0:T(8,128)(2,1)}, bf16[2,8,16,128]{3,2,1,0:T(8,128)(2,1)S(1)}, u32[]{:S(2)}) copy-start(bf16[2,8,16,128]{3,2,1,0:T(8,128)(2,1)S(1)} %collective-permute-done.13.refs_5_) | copy-start | bytes 196612
  88.8 7.3 %copy-start.12 = (bf16[2,8,16,128]{3,2,1,0:T(8,128)(2,1)}, bf16[2,8,16,128]{3,2,1,0:T(8,128)(2,1)S(1)}, u32[]{:S(2)}) copy-start(bf16[2,8,16,128]{3,2,1,0:T(8,128)(2,1)S(1)} %collective-permute-done.14.refs_6_) | copy-start | bytes 196612
  88.8 7.3 %copy-start.13 = (bf16[2,8,16,128]{3,2,1,0:T(8,128)(2,1)}, bf16[2,8,16,128]{3,2,1,0:T(8,128)(2,1)S(1)}, u32[]{:S(2)}) copy-start(bf16[2,8,16,128]{3,2,1,0:T(8,128)(2,1)S(1)} %collective-permute-done.15.refs_7_) | copy-start | bytes 196612
  96.0 1.4 %copy-start.5 = (s32[256,1,2176]{2,1,0:T(1,128)}, s32[256,1,2176]{2,1,0:T(1,128)S(1)}, u32[]{:S(2)}) copy-start(s32[256,1,2176]{2,1,0:T(1,128)S(1)} %all-to-all-done.1) | copy-start | bytes 6684676
Sparse Core Ops, SparseCore 0:
  30.3 65.2 all-gather.1

commit v5 on v4

--- a/solution.py
+++ b/solution.py
@@ -13,6 +13,7 @@
 MIDDLE = 32768.0
 VMEM = 32 * 1024 * 1024
 LARGE_VMEM = 60 * 1024 * 1024
+PACK_VMEM = 64 * 1024 * 1024 - 128 * 1024
 CORES = 2
 
 
@@ -279,7 +280,7 @@
             pltpu.SemaphoreType.DMA((steps,)),
         ],
         out_shape=jax.ShapeDtypeStruct((devices * rows, LANES), jnp.int32),
-        compiler_params=pltpu.CompilerParams(vmem_limit_bytes=LARGE_VMEM),
+        compiler_params=pltpu.CompilerParams(vmem_limit_bytes=PACK_VMEM),
         name="pack",
     )(jnp.transpose(visibility, (0, 2, 3, 1)), flags.T)
     share, fringe, packed = lax.optimization_barrier((share, fringe, packed))

time: 118 us -> 117 us (level)
    unnamed x28 -> x24, local copies, waits for them, and re-layouts: 3.66 us -> 2 us
where the time goes in v5:
time: 117 us; the launch traced here: 116 us
  starting transfers between devices  46.2 us (39%)
  waiting for transfers between devices  33.2 us (28%)
  Pallas kernels  19.9 us (17%)
  between operations  13.6 us (12%)
  local copies, waits for them, and re-layouts  3.45 us (3%)
    ppermute x16, starting transfers between devices, crossed(): lax.ppermute(array, 'tm', [(k, k ^ mask) for k in range(time_count)])  25.7 us
    ppermute x16, waiting for transfers between devices, crossed(): lax.ppermute(array, 'tm', [(k, k ^ mask) for k in range(time_count)])  20.2 us
    pallas_call x1, Pallas kernels, shards(): pl.pallas_call(functools.partial(filter_kernel, rows=rows, spread=spread)...  12.9 us
    all_to_all x1, starting transfers between devices, shards(): lax.all_to_all(jnp.broadcast_to(share, (chan_count, chans, wide)), 'chan'...  10.7 us
    all_to_all x1, starting transfers between devices, shards(): lax.all_to_all(packed.reshape(devices, 1, rows * LANES), everyone, split_...  9.78 us
    all_to_all x1, waiting for transfers between devices, shards(): lax.all_to_all(packed.reshape(devices, 1, rows * LANES), everyone, split_...  7.2 us
    all_to_all x1, waiting for transfers between devices, shards(): lax.all_to_all(jnp.broadcast_to(share, (chan_count, chans, wide)), 'chan'...  5.78 us
    pallas_call x1, Pallas kernels, shards(): pl.pallas_call(functools.partial(pack_kernel, rows=rows), in_specs=[far,...  4.77 us
  transfers between devices with their start and end apart: 19, of which 12 were waited for; matrix products, arithmetic and copies ran while one was open for 0% of the time, Pallas kernels for 6%

profile of v5, /device:TPU:33, one launch (start us, length us, event | category | flops | bytes accessed | tf_op | source)
XLA Modules:
  0.0 116.3 jit_solution(8461336755909894835)
XLA Ops:
  6.5 0.7 dynamic-slice_bitcast_fusion
  7.3 0.7 broadcast_in_dim.8
  8.0 10.7 %all-to-all-start = ((bf16[16,32,256]{2,1,0:T(8,128)(2,1)}), bf16[16,32,256]{2,1,0:T(8,128)(2,1)}, u32[]{:S(2)}, u32[]{:S(2)}) async-start(bf16[16,32,256]{2,1,0:T(8,128)(2,1)} %broadcast_in_dim.8), calls=%async_computation | async-start | bytes 524288 | tf_op jit(solution)/shard_map/all_to_all | solution.py:262
  18.6 0.0 all-gather.2.cloned.1.call-start
  18.7 4.8 %pack.1 = s32[4352,128]{1,0:T(8,128)} custom-call(f32[2,8,32,2048]{3,2,1,0:T(8,128)} %bitcast.15, s32[32,2048]{1,0:T(8,128)} %bitcast.16), custom_call_target="tpu_custom_call" | custom-call | tf_op jit(solution)/shard_map/pack/pallas_call | solution.py:270
  23.5 0.0 copy-start
  23.5 0.0 copy-start.2
  23.5 5.8 %all-to-all-done = bf16[16,32,256]{2,1,0:T(8,128)(2,1)} async-done(((bf16[16,32,256]{2,1,0:T(8,128)(2,1)}), bf16[16,32,256]{2,1,0:T(8,128)(2,1)}, u32[]{:S(2)}, u32[]{:S(2)}) %all-to-all-start) | async-done | bytes 262176 | tf_op jit(solution)/shard_map/all_to_all | solution.py:262
  29.3 0.0 all-gather.2.cloned.1.call-update
  29.3 9.8 %all-to-all-start.1 = ((s32[256,1,2176]{2,1,0:T(1,128)}), s32[256,1,2176]{2,1,0:T(1,128)S(1)}, u32[]{:S(2)}, u32[]{:S(2)}) async-start(s32[256,1,2176]{2,1,0:T(1,128)} %bitcast.13), calls=%async_computation.1 | async-start | bytes 4456448 | tf_op jit(solution)/shard_map/all_to_all | solution.py:289
  39.1 0.1 pad_add_fusion.place_ref
  39.2 0.0 copy-start.3
  39.2 0.0 copy-done
  39.2 0.6 shares.1
  39.8 0.4 collective-permute-start
  40.3 1.0 collective-permute-done.refs_1_
  41.3 1.3 %collective-permute-start.1 = (bf16[2,4,16,128]{3,2,1,0:T(8,128)(2,1)S(1)}, bf16[2,4,16,128]{3,2,1,0:T(8,128)(2,1)S(1)}, u32[]{:S(2)}, u32[]{:S(2)}) collective-permute-start(bf16[2,4,16,128]{3,2,1,0:T(8,128)(2,1)S(1)} %get-tuple-element.34), channel_id=1, source_target_pairs={{0,32},{16,48},{32,0},{48,16},{64,96},{80,112},{96,64},{112,80},{1... | collective-permute-start | bytes 98312 | tf_op jit(solution)/shard_map/ppermute | solution.py:295
  42.6 2.4 %collective-permute-start.2 = (bf16[2,4,16,128]{3,2,1,0:T(8,128)(2,1)S(1)}, bf16[2,4,16,128]{3,2,1,0:T(8,128)(2,1)S(1)}, u32[]{:S(2)}, u32[]{:S(2)}) collective-permute-start(bf16[2,4,16,128]{3,2,1,0:T(8,128)(2,1)S(1)} %get-tuple-element.35), channel_id=1, source_target_pairs={{0,64},{16,80},{32,96},{48,112},{64,0},{80,16},{96,32},{112,48},{1... | collective-permute-start | bytes 98312 | tf_op jit(solution)/shard_map/ppermute | solution.py:295
  45.0 0.2 collective-permute-start.3
  45.2 1.2 %collective-permute-start.4 = (bf16[2,4,16,128]{3,2,1,0:T(8,128)(2,1)S(1)}, bf16[2,4,16,128]{3,2,1,0:T(8,128)(2,1)S(1)}, u32[]{:S(2)}, u32[]{:S(2)}) collective-permute-start(bf16[2,4,16,128]{3,2,1,0:T(8,128)(2,1)S(1)} %get-tuple-element.37), channel_id=1, source_target_pairs={{0,128},{16,144},{32,160},{48,176},{64,192},{80,208},{96,224},{112... | collective-permute-start | bytes 98312 | tf_op jit(solution)/shard_map/ppermute | solution.py:295
  46.5 0.0 collective-permute-start.5
  46.5 1.5 %collective-permute-done.1.refs_1_ = bf16[2,4,16,128]{3,2,1,0:T(8,128)(2,1)S(1)} collective-permute-done((bf16[2,4,16,128]{3,2,1,0:T(8,128)(2,1)S(1)}, bf16[2,4,16,128]{3,2,1,0:T(8,128)(2,1)S(1)}, u32[]{:S(2)}, u32[]{:S(2)}) %collective-permute-start.1) | collective-permute-done | bytes 32800 | tf_op jit(solution)/shard_map/ppermute | solution.py:295
  47.9 3.5 %collective-permute-start.6 = (bf16[2,4,16,128]{3,2,1,0:T(8,128)(2,1)S(1)}, bf16[2,4,16,128]{3,2,1,0:T(8,128)(2,1)S(1)}, u32[]{:S(2)}, u32[]{:S(2)}) collective-permute-start(bf16[2,4,16,128]{3,2,1,0:T(8,128)(2,1)S(1)} %get-tuple-element.39), channel_id=1, source_target_pairs={{0,192},{16,208},{32,224},{48,240},{64,128},{80,144},{96,160},{112... | collective-permute-start | bytes 98312 | tf_op jit(solution)/shard_map/ppermute | solution.py:295
  51.4 2.1 %collective-permute-done.2.refs_2_ = bf16[2,4,16,128]{3,2,1,0:T(8,128)(2,1)S(1)} collective-permute-done((bf16[2,4,16,128]{3,2,1,0:T(8,128)(2,1)S(1)}, bf16[2,4,16,128]{3,2,1,0:T(8,128)(2,1)S(1)}, u32[]{:S(2)}, u32[]{:S(2)}) %collective-permute-start.2) | collective-permute-done | bytes 32800 | tf_op jit(solution)/shard_map/ppermute | solution.py:295
  53.5 1.1 collective-permute-start.7
  54.6 0.0 collective-permute-done.3.refs_3_
  54.6 0.0 collective-permute-done.4.refs_4_
  54.6 0.0 collective-permute-done.5.refs_5_
  54.6 4.1 %collective-permute-done.6.refs_6_ = bf16[2,4,16,128]{3,2,1,0:T(8,128)(2,1)S(1)} collective-permute-done((bf16[2,4,16,128]{3,2,1,0:T(8,128)(2,1)S(1)}, bf16[2,4,16,128]{3,2,1,0:T(8,128)(2,1)S(1)}, u32[]{:S(2)}, u32[]{:S(2)}) %collective-permute-start.6) | collective-permute-done | bytes 32800 | tf_op jit(solution)/shard_map/ppermute | solution.py:295
  58.7 0.3 collective-permute-done.7.refs_7_
  59.0 0.0 copy-done.2
  59.0 1.5 %select.7 = (bf16[8,8,16,128]{3,2,1,0:T(8,128)(2,1)S(1)}, bf16[8,8,16,128]{3,2,1,0:T(8,128)(2,1)S(1)}) custom-call(s32[2048]{0:T(1024)S(1)} %copy-done.2, s32[2]{0:T(128)S(1)} %pad_add_fusion.place_ref, bf16[2,4,16,128]{3,2,1,0:T(8,128)(2,1)S(1)} %get-tuple-element.33.refs_0_, bf16[2,4,16,128]{3,2,1,0:T(8,128)(2,1)S(1)} %collective-permute-done.1.refs_1_, ...), custom_call_target="tpu_custom_call" | custom-call | tf_op jit(solution)/shard_map/select/pallas_call | solution.py:323
  60.5 3.0 %collective-permute-start.8 = (bf16[8,8,16,128]{3,2,1,0:T(8,128)(2,1)S(1)}, bf16[8,8,16,128]{3,2,1,0:T(8,128)(2,1)S(1)}, u32[]{:S(2)}, u32[]{:S(2)}) collective-permute-start(bf16[8,8,16,128]{3,2,1,0:T(8,128)(2,1)S(1)} %get-tuple-element.42), channel_id=1, source_target_pairs={{0,16},{16,0},{32,48},{48,32},{64,80},{80,64},{96,112},{112,96},{1... | collective-permute-start | bytes 786440 | tf_op jit(solution)/shard_map/ppermute | solution.py:295
  63.5 1.2 collective-permute-done.8.refs_1_
  64.7 0.0 copy-start.1
  64.7 0.6 copy-done.1
  65.4 1.2 %collective-permute-start.9 = (bf16[2,8,16,128]{3,2,1,0:T(8,128)(2,1)S(1)}, bf16[2,8,16,128]{3,2,1,0:T(8,128)(2,1)S(1)}, u32[]{:S(2)}, u32[]{:S(2)}) collective-permute-start(bf16[2,8,16,128]{3,2,1,0:T(8,128)(2,1)S(1)} %get-tuple-element.44), channel_id=1, source_target_pairs={{0,32},{16,48},{32,0},{48,16},{64,96},{80,112},{96,64},{112,80},{1... | collective-permute-start | bytes 196616 | tf_op jit(solution)/shard_map/ppermute | solution.py:295
  66.6 1.0 collective-permute-start.10
  67.6 1.6 %collective-permute-start.11 = (bf16[2,8,16,128]{3,2,1,0:T(8,128)(2,1)S(1)}, bf16[2,8,16,128]{3,2,1,0:T(8,128)(2,1)S(1)}, u32[]{:S(2)}, u32[]{:S(2)}) collective-permute-start(bf16[2,8,16,128]{3,2,1,0:T(8,128)(2,1)S(1)} %get-tuple-element.46), channel_id=1, source_target_pairs={{0,96},{16,112},{32,64},{48,80},{64,32},{80,48},{96,0},{112,16},{1... | collective-permute-start | bytes 196616 | tf_op jit(solution)/shard_map/ppermute | solution.py:295
  69.2 1.6 %collective-permute-start.12 = (bf16[2,8,16,128]{3,2,1,0:T(8,128)(2,1)S(1)}, bf16[2,8,16,128]{3,2,1,0:T(8,128)(2,1)S(1)}, u32[]{:S(2)}, u32[]{:S(2)}) collective-permute-start(bf16[2,8,16,128]{3,2,1,0:T(8,128)(2,1)S(1)} %get-tuple-element.47), channel_id=1, source_target_pairs={{0,128},{16,144},{32,160},{48,176},{64,192},{80,208},{96,224},{112... | collective-permute-start | bytes 196616 | tf_op jit(solution)/shard_map/ppermute | solution.py:295
  70.8 0.0 collective-permute-start.13
  70.8 2.5 %collective-permute-done.9.refs_1_ = bf16[2,8,16,128]{3,2,1,0:T(8,128)(2,1)S(1)} collective-permute-done((bf16[2,8,16,128]{3,2,1,0:T(8,128)(2,1)S(1)}, bf16[2,8,16,128]{3,2,1,0:T(8,128)(2,1)S(1)}, u32[]{:S(2)}, u32[]{:S(2)}) %collective-permute-start.9) | collective-permute-done | bytes 65568 | tf_op jit(solution)/shard_map/ppermute | solution.py:295
  73.3 0.0 copy-start.5
  73.3 2.3 %collective-permute-start.14 = (bf16[2,8,16,128]{3,2,1,0:T(8,128)(2,1)S(1)}, bf16[2,8,16,128]{3,2,1,0:T(8,128)(2,1)S(1)}, u32[]{:S(2)}, u32[]{:S(2)}) collective-permute-start(bf16[2,8,16,128]{3,2,1,0:T(8,128)(2,1)S(1)} %get-tuple-element.49), channel_id=1, source_target_pairs={{0,192},{16,208},{32,224},{48,240},{64,128},{80,144},{96,160},{112... | collective-permute-start | bytes 196616 | tf_op jit(solution)/shard_map/ppermute | solution.py:295
  75.6 1.3 %collective-permute-done.10.refs_2_ = bf16[2,8,16,128]{3,2,1,0:T(8,128)(2,1)S(1)} collective-permute-done((bf16[2,8,16,128]{3,2,1,0:T(8,128)(2,1)S(1)}, bf16[2,8,16,128]{3,2,1,0:T(8,128)(2,1)S(1)}, u32[]{:S(2)}, u32[]{:S(2)}) %collective-permute-start.10) | collective-permute-done | bytes 65568 | tf_op jit(solution)/shard_map/ppermute | solution.py:295
  76.9 0.0 copy-start.6
  76.9 4.7 %collective-permute-start.15 = (bf16[2,8,16,128]{3,2,1,0:T(8,128)(2,1)S(1)}, bf16[2,8,16,128]{3,2,1,0:T(8,128)(2,1)S(1)}, u32[]{:S(2)}, u32[]{:S(2)}) collective-permute-start(bf16[2,8,16,128]{3,2,1,0:T(8,128)(2,1)S(1)} %get-tuple-element.50), channel_id=1, source_target_pairs={{0,224},{16,240},{32,192},{48,208},{64,160},{80,176},{96,128},{112... | collective-permute-start | bytes 196616 | tf_op jit(solution)/shard_map/ppermute | solution.py:295
  81.6 0.0 collective-permute-done.11.refs_3_
  81.6 0.0 collective-permute-done.12.refs_4_
  81.6 0.0 copy-start.8
  81.6 2.8 %collective-permute-done.13.refs_5_ = bf16[2,8,16,128]{3,2,1,0:T(8,128)(2,1)S(1)} collective-permute-done((bf16[2,8,16,128]{3,2,1,0:T(8,128)(2,1)S(1)}, bf16[2,8,16,128]{3,2,1,0:T(8,128)(2,1)S(1)}, u32[]{:S(2)}, u32[]{:S(2)}) %collective-permute-start.13) | collective-permute-done | bytes 65568 | tf_op jit(solution)/shard_map/ppermute | solution.py:295
  84.5 3.5 %collective-permute-done.14.refs_6_ = bf16[2,8,16,128]{3,2,1,0:T(8,128)(2,1)S(1)} collective-permute-done((bf16[2,8,16,128]{3,2,1,0:T(8,128)(2,1)S(1)}, bf16[2,8,16,128]{3,2,1,0:T(8,128)(2,1)S(1)}, u32[]{:S(2)}, u32[]{:S(2)}) %collective-permute-start.14) | collective-permute-done | bytes 65568 | tf_op jit(solution)/shard_map/ppermute | solution.py:295
  87.9 0.0 collective-permute-done.15.refs_7_
  87.9 7.2 %all-to-all-done.1 = s32[256,1,2176]{2,1,0:T(1,128)S(1)} async-done(((s32[256,1,2176]{2,1,0:T(1,128)}), s32[256,1,2176]{2,1,0:T(1,128)S(1)}, u32[]{:S(2)}, u32[]{:S(2)}) %all-to-all-start.1) | async-done | bytes 2228256 | tf_op jit(solution)/shard_map/all_to_all | solution.py:289
  95.1 0.0 copy-done.3
  95.1 0.0 copy-done.5
  95.1 0.0 copy-done.6
  95.1 0.0 copy-done.7
  95.2 0.0 copy-done.8
  95.2 0.0 copy-done.9
  95.2 0.0 copy-done.10
  95.2 0.0 copy-done.11
  95.2 1.3 %copy-done.4 = s32[256,1,2176]{2,1,0:T(1,128)} copy-done((s32[256,1,2176]{2,1,0:T(1,128)}, s32[256,1,2176]{2,1,0:T(1,128)S(1)}, u32[]{:S(2)}) %copy-start.4) | copy-done | bytes 2228248
  96.5 12.9 %filter.1 = f32[2,8,128,512]{3,2,1,0:T(8,128)} custom-call(s32[2048]{0:T(1024)} %groups_ref.3, s32[2]{0:T(128)} %copy-done.3, s32[16,272,128]{2,1,0:T(8,128)} %bitcast.12, bf16[8,2,512,256]{3,2,1,0:T(8,128)(2,1)} %bitcast.14, bf16[2,8,16,128]{3,2,1,0:T(8,128)(2,1)} %copy-done.1, bf16[2,8,16,128]{3,2,1,0:T(8,128)(2,1)} %copy-done.5, ...), custom_call_target="tpu_custom_call" | custom-call | tf_op jit(solution)/shard_map/filter/pallas_call | solution.py:340
  (8 shorter events, 0.1 us)
Async XLA Ops:
  8.0 21.3 %all-to-all-start = ((bf16[16,32,256]{2,1,0:T(8,128)(2,1)}), bf16[16,32,256]{2,1,0:T(8,128)(2,1)}, u32[]{:S(2)}, u32[]{:S(2)}) async-start(bf16[16,32,256]{2,1,0:T(8,128)(2,1)} %broadcast_in_dim.8), calls=%async_computation | async-start | bytes 524288 | tf_op jit(solution)/shard_map/all_to_all | solution.py:262
  18.6 76.5 %all-gather.2.cloned.1.call-start = ((), (), s32[]{:S(2)}) async-start(), calls=%async_computation.2 | async-start | bytes 4456448 | tf_op jit(solution)/shard_map/all_gather | solution.py:287
  23.5 15.7 %copy-start = (bf16[2,4,128,128]{3,2,1,0:T(8,128)(2,1)S(1)}, bf16[2,4,128,128]{3,2,1,0:T(8,128)(2,1)}, u32[]{:S(2)}) copy-start(bf16[2,4,128,128]{3,2,1,0:T(8,128)(2,1)} %param.8) | copy-start | bytes 786436
  23.5 35.5 %copy-start.2 = (s32[2048]{0:T(1024)S(1)}, s32[2048]{0:T(1024)}, u32[]{:S(2)}) copy-start(s32[2048]{0:T(1024)} %groups_ref.3) | copy-start | bytes 24580
  29.3 65.8 %all-to-all-start.1 = ((s32[256,1,2176]{2,1,0:T(1,128)}), s32[256,1,2176]{2,1,0:T(1,128)S(1)}, u32[]{:S(2)}, u32[]{:S(2)}) async-start(s32[256,1,2176]{2,1,0:T(1,128)} %bitcast.13), calls=%async_computation.1 | async-start | bytes 4456448 | tf_op jit(solution)/shard_map/all_to_all | solution.py:289
  39.2 56.0 %copy-start.3 = (s32[2]{0:T(128)}, s32[2]{0:T(128)S(1)}, u32[]{:S(2)}) copy-start(s32[2]{0:T(128)S(1)} %pad_add_fusion.place_ref) | copy-start | bytes 28
  39.8 1.4 %collective-permute-start = (bf16[8,4,16,128]{3,2,1,0:T(8,128)(2,1)S(1)}, bf16[8,4,16,128]{3,2,1,0:T(8,128)(2,1)S(1)}, u32[]{:S(2)}, u32[]{:S(2)}) collective-permute-start(bf16[8,4,16,128]{3,2,1,0:T(8,128)(2,1)S(1)} %get-tuple-element.32), channel_id=1, source_target_pairs={{0,16},{16,0},{32,48},{48,32},{64,80},{80,64},{96,112},{112,96},{1... | collective-permute-start | bytes 393224 | tf_op jit(solution)/shard_map/ppermute | solution.py:295
  41.3 6.7 %collective-permute-start.1 = (bf16[2,4,16,128]{3,2,1,0:T(8,128)(2,1)S(1)}, bf16[2,4,16,128]{3,2,1,0:T(8,128)(2,1)S(1)}, u32[]{:S(2)}, u32[]{:S(2)}) collective-permute-start(bf16[2,4,16,128]{3,2,1,0:T(8,128)(2,1)S(1)} %get-tuple-element.34), channel_id=1, source_target_pairs={{0,32},{16,48},{32,0},{48,16},{64,96},{80,112},{96,64},{112,80},{1... | collective-permute-start | bytes 98312 | tf_op jit(solution)/shard_map/ppermute | solution.py:295
  42.6 11.0 %collective-permute-start.2 = (bf16[2,4,16,128]{3,2,1,0:T(8,128)(2,1)S(1)}, bf16[2,4,16,128]{3,2,1,0:T(8,128)(2,1)S(1)}, u32[]{:S(2)}, u32[]{:S(2)}) collective-permute-start(bf16[2,4,16,128]{3,2,1,0:T(8,128)(2,1)S(1)} %get-tuple-element.35), channel_id=1, source_target_pairs={{0,64},{16,80},{32,96},{48,112},{64,0},{80,16},{96,32},{112,48},{1... | collective-permute-start | bytes 98312 | tf_op jit(solution)/shard_map/ppermute | solution.py:295
  45.0 9.6 %collective-permute-start.3 = (bf16[2,4,16,128]{3,2,1,0:T(8,128)(2,1)S(1)}, bf16[2,4,16,128]{3,2,1,0:T(8,128)(2,1)S(1)}, u32[]{:S(2)}, u32[]{:S(2)}) collective-permute-start(bf16[2,4,16,128]{3,2,1,0:T(8,128)(2,1)S(1)} %get-tuple-element.36), channel_id=1, source_target_pairs={{0,96},{16,112},{32,64},{48,80},{64,32},{80,48},{96,0},{112,16},{1... | collective-permute-start | bytes 98312 | tf_op jit(solution)/shard_map/ppermute | solution.py:295
  45.2 9.4 %collective-permute-start.4 = (bf16[2,4,16,128]{3,2,1,0:T(8,128)(2,1)S(1)}, bf16[2,4,16,128]{3,2,1,0:T(8,128)(2,1)S(1)}, u32[]{:S(2)}, u32[]{:S(2)}) collective-permute-start(bf16[2,4,16,128]{3,2,1,0:T(8,128)(2,1)S(1)} %get-tuple-element.37), channel_id=1, source_target_pairs={{0,128},{16,144},{32,160},{48,176},{64,192},{80,208},{96,224},{112... | collective-permute-start | bytes 98312 | tf_op jit(solution)/shard_map/ppermute | solution.py:295
  46.5 8.1 %collective-permute-start.5 = (bf16[2,4,16,128]{3,2,1,0:T(8,128)(2,1)S(1)}, bf16[2,4,16,128]{3,2,1,0:T(8,128)(2,1)S(1)}, u32[]{:S(2)}, u32[]{:S(2)}) collective-permute-start(bf16[2,4,16,128]{3,2,1,0:T(8,128)(2,1)S(1)} %get-tuple-element.38), channel_id=1, source_target_pairs={{0,160},{16,176},{32,128},{48,144},{64,224},{80,240},{96,192},{112... | collective-permute-start | bytes 98312 | tf_op jit(solution)/shard_map/ppermute | solution.py:295
  47.9 10.8 %collective-permute-start.6 = (bf16[2,4,16,128]{3,2,1,0:T(8,128)(2,1)S(1)}, bf16[2,4,16,128]{3,2,1,0:T(8,128)(2,1)S(1)}, u32[]{:S(2)}, u32[]{:S(2)}) collective-permute-start(bf16[2,4,16,128]{3,2,1,0:T(8,128)(2,1)S(1)} %get-tuple-element.39), channel_id=1, source_target_pairs={{0,192},{16,208},{32,224},{48,240},{64,128},{80,144},{96,160},{112... | collective-permute-start | bytes 98312 | tf_op jit(solution)/shard_map/ppermute | solution.py:295
  53.5 5.5 %collective-permute-start.7 = (bf16[2,4,16,128]{3,2,1,0:T(8,128)(2,1)S(1)}, bf16[2,4,16,128]{3,2,1,0:T(8,128)(2,1)S(1)}, u32[]{:S(2)}, u32[]{:S(2)}) collective-permute-start(bf16[2,4,16,128]{3,2,1,0:T(8,128)(2,1)S(1)} %get-tuple-element.40), channel_id=1, source_target_pairs={{0,224},{16,240},{32,192},{48,208},{64,160},{80,176},{96,128},{112... | collective-permute-start | bytes 98312 | tf_op jit(solution)/shard_map/ppermute | solution.py:295
  60.5 4.2 %collective-permute-start.8 = (bf16[8,8,16,128]{3,2,1,0:T(8,128)(2,1)S(1)}, bf16[8,8,16,128]{3,2,1,0:T(8,128)(2,1)S(1)}, u32[]{:S(2)}, u32[]{:S(2)}) collective-permute-start(bf16[8,8,16,128]{3,2,1,0:T(8,128)(2,1)S(1)} %get-tuple-element.42), channel_id=1, source_target_pairs={{0,16},{16,0},{32,48},{48,32},{64,80},{80,64},{96,112},{112,96},{1... | collective-permute-start | bytes 786440 | tf_op jit(solution)/shard_map/ppermute | solution.py:295
  64.7 0.6 copy-start.1
  65.4 8.0 %collective-permute-start.9 = (bf16[2,8,16,128]{3,2,1,0:T(8,128)(2,1)S(1)}, bf16[2,8,16,128]{3,2,1,0:T(8,128)(2,1)S(1)}, u32[]{:S(2)}, u32[]{:S(2)}) collective-permute-start(bf16[2,8,16,128]{3,2,1,0:T(8,128)(2,1)S(1)} %get-tuple-element.44), channel_id=1, source_target_pairs={{0,32},{16,48},{32,0},{48,16},{64,96},{80,112},{96,64},{112,80},{1... | collective-permute-start | bytes 196616 | tf_op jit(solution)/shard_map/ppermute | solution.py:295
  66.6 10.3 %collective-permute-start.10 = (bf16[2,8,16,128]{3,2,1,0:T(8,128)(2,1)S(1)}, bf16[2,8,16,128]{3,2,1,0:T(8,128)(2,1)S(1)}, u32[]{:S(2)}, u32[]{:S(2)}) collective-permute-start(bf16[2,8,16,128]{3,2,1,0:T(8,128)(2,1)S(1)} %get-tuple-element.45), channel_id=1, source_target_pairs={{0,64},{16,80},{32,96},{48,112},{64,0},{80,16},{96,32},{112,48},{1... | collective-permute-start | bytes 196616 | tf_op jit(solution)/shard_map/ppermute | solution.py:295
  67.6 14.0 %collective-permute-start.11 = (bf16[2,8,16,128]{3,2,1,0:T(8,128)(2,1)S(1)}, bf16[2,8,16,128]{3,2,1,0:T(8,128)(2,1)S(1)}, u32[]{:S(2)}, u32[]{:S(2)}) collective-permute-start(bf16[2,8,16,128]{3,2,1,0:T(8,128)(2,1)S(1)} %get-tuple-element.46), channel_id=1, source_target_pairs={{0,96},{16,112},{32,64},{48,80},{64,32},{80,48},{96,0},{112,16},{1... | collective-permute-start | bytes 196616 | tf_op jit(solution)/shard_map/ppermute | solution.py:295
  69.2 12.4 %collective-permute-start.12 = (bf16[2,8,16,128]{3,2,1,0:T(8,128)(2,1)S(1)}, bf16[2,8,16,128]{3,2,1,0:T(8,128)(2,1)S(1)}, u32[]{:S(2)}, u32[]{:S(2)}) collective-permute-start(bf16[2,8,16,128]{3,2,1,0:T(8,128)(2,1)S(1)} %get-tuple-element.47), channel_id=1, source_target_pairs={{0,128},{16,144},{32,160},{48,176},{64,192},{80,208},{96,224},{112... | collective-permute-start | bytes 196616 | tf_op jit(solution)/shard_map/ppermute | solution.py:295
  70.8 13.6 %collective-permute-start.13 = (bf16[2,8,16,128]{3,2,1,0:T(8,128)(2,1)S(1)}, bf16[2,8,16,128]{3,2,1,0:T(8,128)(2,1)S(1)}, u32[]{:S(2)}, u32[]{:S(2)}) collective-permute-start(bf16[2,8,16,128]{3,2,1,0:T(8,128)(2,1)S(1)} %get-tuple-element.48), channel_id=1, source_target_pairs={{0,160},{16,176},{32,128},{48,144},{64,224},{80,240},{96,192},{112... | collective-permute-start | bytes 196616 | tf_op jit(solution)/shard_map/ppermute | solution.py:295
  73.3 21.8 %copy-start.5 = (bf16[2,8,16,128]{3,2,1,0:T(8,128)(2,1)}, bf16[2,8,16,128]{3,2,1,0:T(8,128)(2,1)S(1)}, u32[]{:S(2)}) copy-start(bf16[2,8,16,128]{3,2,1,0:T(8,128)(2,1)S(1)} %collective-permute-done.9.refs_1_) | copy-start | bytes 196612
  73.3 14.6 %collective-permute-start.14 = (bf16[2,8,16,128]{3,2,1,0:T(8,128)(2,1)S(1)}, bf16[2,8,16,128]{3,2,1,0:T(8,128)(2,1)S(1)}, u32[]{:S(2)}, u32[]{:S(2)}) collective-permute-start(bf16[2,8,16,128]{3,2,1,0:T(8,128)(2,1)S(1)} %get-tuple-element.49), channel_id=1, source_target_pairs={{0,192},{16,208},{32,224},{48,240},{64,128},{80,144},{96,160},{112... | collective-permute-start | bytes 196616 | tf_op jit(solution)/shard_map/ppermute | solution.py:295
  76.9 18.3 %copy-start.6 = (bf16[2,8,16,128]{3,2,1,0:T(8,128)(2,1)}, bf16[2,8,16,128]{3,2,1,0:T(8,128)(2,1)S(1)}, u32[]{:S(2)}) copy-start(bf16[2,8,16,128]{3,2,1,0:T(8,128)(2,1)S(1)} %collective-permute-done.10.refs_2_) | copy-start | bytes 196612
  76.9 11.1 %collective-permute-start.15 = (bf16[2,8,16,128]{3,2,1,0:T(8,128)(2,1)S(1)}, bf16[2,8,16,128]{3,2,1,0:T(8,128)(2,1)S(1)}, u32[]{:S(2)}, u32[]{:S(2)}) collective-permute-start(bf16[2,8,16,128]{3,2,1,0:T(8,128)(2,1)S(1)} %get-tuple-element.50), channel_id=1, source_target_pairs={{0,224},{16,240},{32,192},{48,208},{64,160},{80,176},{96,128},{112... | collective-permute-start | bytes 196616 | tf_op jit(solution)/shard_map/ppermute | solution.py:295
  81.6 13.6 %copy-start.7 = (bf16[2,8,16,128]{3,2,1,0:T(8,128)(2,1)}, bf16[2,8,16,128]{3,2,1,0:T(8,128)(2,1)S(1)}, u32[]{:S(2)}) copy-start(bf16[2,8,16,128]{3,2,1,0:T(8,128)(2,1)S(1)} %collective-permute-done.11.refs_3_) | copy-start | bytes 196612
  81.6 13.6 %copy-start.8 = (bf16[2,8,16,128]{3,2,1,0:T(8,128)(2,1)}, bf16[2,8,16,128]{3,2,1,0:T(8,128)(2,1)S(1)}, u32[]{:S(2)}) copy-start(bf16[2,8,16,128]{3,2,1,0:T(8,128)(2,1)S(1)} %collective-permute-done.12.refs_4_) | copy-start | bytes 196612
  84.5 10.7 %copy-start.9 = (bf16[2,8,16,128]{3,2,1,0:T(8,128)(2,1)}, bf16[2,8,16,128]{3,2,1,0:T(8,128)(2,1)S(1)}, u32[]{:S(2)}) copy-start(bf16[2,8,16,128]{3,2,1,0:T(8,128)(2,1)S(1)} %collective-permute-done.13.refs_5_) | copy-start | bytes 196612
  87.9 7.3 %copy-start.10 = (bf16[2,8,16,128]{3,2,1,0:T(8,128)(2,1)}, bf16[2,8,16,128]{3,2,1,0:T(8,128)(2,1)S(1)}, u32[]{:S(2)}) copy-start(bf16[2,8,16,128]{3,2,1,0:T(8,128)(2,1)S(1)} %collective-permute-done.14.refs_6_) | copy-start | bytes 196612
  87.9 7.3 %copy-start.11 = (bf16[2,8,16,128]{3,2,1,0:T(8,128)(2,1)}, bf16[2,8,16,128]{3,2,1,0:T(8,128)(2,1)S(1)}, u32[]{:S(2)}) copy-start(bf16[2,8,16,128]{3,2,1,0:T(8,128)(2,1)S(1)} %collective-permute-done.15.refs_7_) | copy-start | bytes 196612
  95.1 1.4 %copy-start.4 = (s32[256,1,2176]{2,1,0:T(1,128)}, s32[256,1,2176]{2,1,0:T(1,128)S(1)}, u32[]{:S(2)}) copy-start(s32[256,1,2176]{2,1,0:T(1,128)S(1)} %all-to-all-done.1) | copy-start | bytes 6684676
Sparse Core Ops, SparseCore 0:
  29.4 65.2 all-gather.1
